TPU v7x, 512 devices: a whole 4x8x8 slice. The times are simulated.
512 devices in a mesh: row: 16 (over y, core), col: 32 (over z, x).
Axes of the slice: x: 4, y: 8, z: 8, core: 2. Of those that a mesh axis runs over, the one named last changes fastest.
Arguments:
- features: bfloat16 [65536, 256], P(('col', 'row')), may hold values from -6 to 6
- col_norm: float32 [65536], P(('col', 'row')), may hold values from 0.03 to 0.3
- weight: bfloat16 [256, 256], replicated, may hold values from -0.375 to 0.375
- bias: float32 [256], replicated, may hold values from -4 to 4
- tile_coords: int32 [16, 32, 24, 2], P('row', 'col'), may hold values from 0 to 31, as said below
- tile_count: int32 [16, 32], P('row', 'col'), may hold values from 6 to 24
- tile_values: bfloat16 [16, 32, 24, 128, 128], P('row', 'col'), may hold values from 0 to 1
- row_norm: float32 [65536], P(('row', 'col')), may hold values from 0.03 to 0.3
- cotangent: bfloat16 [65536, 256], P(('row', 'col')), may hold values from -6 to 6
Outputs:
- output: bfloat16 [65536, 256], P(('row', 'col'))
- grad_features: bfloat16 [65536, 256], P(('col', 'row'))
- grad_weight: float32 [256, 256], replicated
- grad_bias: float32 [256], replicated
Inputs may be any that keep to these rules, and one draw needn't show every extreme that they name: `tile_coords`: column 0 is a tile row below 32, column 1 a tile column below 16; the 24 pairs of one grid block are distinct. Slots from tile_count onward hold no tiles.
All inputs are finite; a program needn't handle non-finite values.
Results may differ from a plain program's by a relative error of at most 0.025.
Values may be sent and summed in bfloat16 or wider, within the bound.
No kernel may reach another device: no remote copies, remote signals or barrier semaphores. Data moves between devices by JAX's collectives and lax.ppermute only.
A program may use at most 64 MiB of HBM per device.

v0:
```python
import jax
import jax.numpy as jnp
from jax import lax
from jax.sharding import PartitionSpec as P


def body(
    features, col_norm, weight, bias, tile_coords, tile_count, tile_values, row_norm, cotangent
):
    rows_here = features.shape[0]
    hidden = weight.shape[0]
    tile_size = tile_values.shape[-1]
    slot_count = tile_values.shape[2]
    row_devices = lax.axis_size("row")
    col_devices = lax.axis_size("col")
    tile_rows = rows_here * col_devices // tile_size
    tile_cols = rows_here * row_devices // tile_size
    coords = tile_coords[0, 0]
    tile_block = tile_values[0, 0]
    live = (jnp.arange(slot_count) < tile_count[0, 0]).astype(jnp.float32)
    scale = float(rows_here * row_devices * col_devices) ** (-0.5)
    mixed = jnp.dot(features, weight, preferred_element_type=jnp.float32)
    shares = (col_norm[:, None] * mixed).astype(jnp.bfloat16)
    panel = lax.all_gather(shares, "row", axis=0, tiled=True)
    picked = panel.reshape(tile_cols, tile_size, hidden)[coords[:, 1]]
    product = jnp.einsum("kab,kbh->kah", tile_block, picked, preferred_element_type=jnp.float32)
    product = product * live[:, None, None]
    partial_value = (
        jnp.zeros((tile_rows, tile_size, hidden), jnp.float32).at[coords[:, 0]].add(product)
    )
    partial_value = partial_value.reshape(tile_rows * tile_size, hidden)
    summed = lax.psum_scatter(
        partial_value.astype(jnp.bfloat16), "col", scatter_dimension=0, tiled=True
    ).astype(jnp.float32)
    pre = row_norm[:, None] * summed + bias[None, :]
    sigma = jax.nn.sigmoid(pre)
    output = (pre * sigma).astype(jnp.bfloat16)
    grad_pre = cotangent.astype(jnp.float32) * (sigma * (1.0 + pre * (1.0 - sigma)))
    grad_here = (grad_pre * row_norm[:, None]).astype(jnp.bfloat16)
    grad_block = lax.all_gather(grad_here, "col", axis=0, tiled=True)
    bias_part = jnp.sum(grad_pre, axis=0) * scale
    back_picked = grad_block.reshape(tile_rows, tile_size, hidden)[coords[:, 0]]
    back_product = jnp.einsum(
        "kba,kbh->kah", tile_block, back_picked, preferred_element_type=jnp.float32
    )
    back_product = back_product * live[:, None, None]
    back_partial = (
        jnp.zeros((tile_cols, tile_size, hidden), jnp.float32).at[coords[:, 1]].add(back_product)
    )
    back_partial = back_partial.reshape(tile_cols * tile_size, hidden)
    column_total = lax.psum_scatter(
        back_partial.astype(jnp.bfloat16), "row", scatter_dimension=0, tiled=True
    ).astype(jnp.float32)
    grad_mixed = (col_norm[:, None] * column_total).astype(jnp.bfloat16)
    grad_features = lax.dot_general(
        grad_mixed, weight, (((1,), (1,)), ((), ())), preferred_element_type=jnp.float32
    ).astype(jnp.bfloat16)
    weight_part = (
        lax.dot_general(
            features, grad_mixed, (((0,), (0,)), ((), ())), preferred_element_type=jnp.float32
        )
        * scale
    )
    grad_weight, grad_bias = lax.psum((weight_part, bias_part), ("row", "col"))
    return (output, grad_features, grad_weight, grad_bias)


def solution(mesh):
    in_specs = (
        P(("col", "row"), None),
        P(("col", "row")),
        P(),
        P(),
        P("row", "col", None, None),
        P("row", "col"),
        P("row", "col", None, None, None),
        P(("row", "col")),
        P(("row", "col"), None),
    )
    out_specs = (P(("row", "col"), None), P(("col", "row"), None), P(), P())
    return jax.shard_map(body, mesh=mesh, in_specs=in_specs, out_specs=out_specs, check_vma=False)
```

profile of v0, /device:TPU:1, one launch (start us, length us, event | category | flops | bytes accessed | tf_op | source)
XLA Modules:
  0.0 773.6 jit_solution(15311268736848351698)
XLA Ops:
  7.2 1.8 fusion.1
  9.7 0.8 fusion.5
  10.5 46.9 %all-gather.3.cloned.1.call-done = bf16[2048,256]{1,0:T(8,128)(2,1)} async-done(((bf16[128,256]{1,0:T(8,128)(2,1)}), bf16[2048,256]{1,0:T(8,128)(2,1)}) %all-gather.3.cloned.1.call-update) | async-done | bytes 1048592 | tf_op jit(solution)/shard_map/all_gather | solution.py:24
  57.4 1.9 gather_fusion
  59.3 2.4 multiply_bitcast_fusion.1
  61.7 3.6 copy.17
  65.3 2.4 broadcast_in_dim.4
  67.7 9.2 %scatter_fusion = f32[32,128,256]{2,1,0:T(8,128)} fusion(f32[32,128,256]{2,1,0:T(8,128)} %broadcast_in_dim.4, s32[24]{0:T(128)S(1)} %get-tuple-element.16, f32[24,128,256]{2,1,0:T(8,128)} %copy.17), kind=kCustom, calls=%fused_computation.2 | custom fusion | flops 786432 | bytes 9437280 | tf_op jit(solution)/shard_map/scatter-add | solution.py:29
  76.9 3.8 convert_element_type.45
  80.8 216.1 %reduce-scatter.3.cloned.1.call-done = bf16[128,256]{1,0:T(8,128)(2,1)} async-done(((bf16[4096,256]{1,0:T(8,128)(2,1)}), bf16[128,256]{1,0:T(8,128)(2,1)}) %reduce-scatter.3.cloned.1.call-update) | async-done | bytes 65552 | tf_op jit(solution)/shard_map/reduce_scatter | solution.py:32
  296.9 1.6 fusion.6
  298.5 0.7 multiply_convert_fusion.1
  299.3 84.8 %all-gather.5.cloned.1.call-done = bf16[4096,256]{1,0:T(8,128)(2,1)} async-done(((bf16[128,256]{1,0:T(8,128)(2,1)}), bf16[4096,256]{1,0:T(8,128)(2,1)}) %all-gather.5.cloned.1.call-update) | async-done | bytes 2097168 | tf_op jit(solution)/shard_map/all_gather | solution.py:40
  384.2 2.2 gather_fusion.1
  386.4 2.4 multiply_bitcast_fusion
  388.8 3.5 copy.19
  392.3 0.2 broadcast_in_dim.5
  392.5 6.1 scatter_fusion.1
  398.7 1.1 convert_element_type.51
  399.9 99.5 %psum.15 = f32[256]{0:T(256)} all-reduce(f32[256]{0:T(256)S(1)} %broadcast_multiply_fusion), channel_id=1, replica_groups=mesh['row'=16,'col'=32] {'row','col'}, use_global_device_ids=true, to_apply=%region_6.0 | all-reduce | flops 256 | bytes 2048 | tf_op jit(solution)/shard_map/psum | solution.py:64
  499.4 1.8 fusion
  501.3 1.7 convolution_convert_fusion
  503.0 262.4 %all-reduce.2.cloned.1.call-done = f32[256,256]{0,1:T(8,128)} async-done(((f32[256,256]{0,1:T(8,128)}), f32[256,256]{0,1:T(8,128)}) %all-reduce.2.cloned.1.call-update) | async-done | bytes 262160 | tf_op jit(solution)/shard_map/psum | solution.py:64
  765.3 1.8 copy.20
  (29 shorter events, 0.3 us)
Async XLA Ops:
  7.2 52.2 %copy-start = (bf16[1,1,24,128,128]{4,3,2,1,0:T(8,128)(2,1)S(1)}, bf16[1,1,24,128,128]{4,3,2,1,0:T(8,128)(2,1)}, u32[]{:S(2)}) copy-start(bf16[1,1,24,128,128]{4,3,2,1,0:T(8,128)(2,1)} %param.15) | copy-start | bytes 2359300
  7.2 50.3 %all-gather.3.cloned.1.call-start = ((), (), s32[]{:S(2)}) async-start(), calls=%async_computation.2 | async-start | bytes 1114112 | tf_op jit(solution)/shard_map/all_gather | solution.py:24
  9.0 287.9 %reduce-scatter.3.cloned.1.call-start = ((), (), s32[]{:S(2)}) async-start(), calls=%async_computation.3 | async-start | bytes 2162688 | tf_op jit(solution)/shard_map/reduce_scatter | solution.py:32
  80.7 216.2 %copy-start.3 = (bf16[128,256]{1,0:T(8,128)(2,1)S(1)}, bf16[128,256]{1,0:T(8,128)(2,1)}, u32[]{:S(2)}) copy-start(bf16[128,256]{1,0:T(8,128)(2,1)} %param.17) | copy-start | bytes 196612
  80.7 216.2 %copy-start.5 = (f32[128]{0:T(128)S(1)}, f32[128]{0:T(128)}, u32[]{:S(2)}) copy-start(f32[128]{0:T(128)} %param.16) | copy-start | bytes 1540
  80.7 216.2 %copy-start.6 = (f32[256]{0:T(256)S(1)}, f32[256]{0:T(256)}, u32[]{:S(2)}) copy-start(f32[256]{0:T(256)} %param.12) | copy-start | bytes 3076
  80.7 303.4 %all-gather.5.cloned.1.call-start = ((), (), s32[]{:S(2)}) async-start(), calls=%async_computation.4 | async-start | bytes 2162688 | tf_op jit(solution)/shard_map/all_gather | solution.py:40
  299.3 200.1 %reduce-scatter.5.cloned.1.call-start = ((), (), s32[]{:S(2)}) async-start(), calls=%async_computation.5 | async-start | bytes 1114112 | tf_op jit(solution)/shard_map/reduce_scatter | solution.py:51
  398.7 100.8 %copy-start.2 = (bf16[128,256]{1,0:T(8,128)(2,1)S(1)}, bf16[128,256]{1,0:T(8,128)(2,1)}, u32[]{:S(2)}) copy-start(bf16[128,256]{1,0:T(8,128)(2,1)} %param.9) | copy-start | bytes 196612
  398.7 100.7 %copy-start.4 = (f32[128]{0:T(128)S(1)}, f32[128]{0:T(128)}, u32[]{:S(2)}) copy-start(f32[128]{0:T(128)} %param.10) | copy-start | bytes 1540
  398.7 102.6 %copy-start.1 = (bf16[256,256]{1,0:T(8,128)(2,1)S(1)}, bf16[256,256]{1,0:T(8,128)(2,1)}, u32[]{:S(2)}) copy-start(bf16[256,256]{1,0:T(8,128)(2,1)} %param.11) | copy-start | bytes 393220
  399.8 365.5 %all-reduce.2.cloned.1.call-start = ((), (), s32[]{:S(2)}) async-start(), calls=%async_computation.6 | async-start | bytes 524288 | tf_op jit(solution)/shard_map/psum | solution.py:64
Sparse Core Ops, SparseCore 0:
  10.7 46.6 all-gather.2
  80.9 216.0 reduce-scatter.2
  301.1 82.9 all-gather.4
  399.9 58.8 reduce-scatter.4
  501.4 263.8 all-reduce.1
where the time goes:
time: 774 us
  waiting for transfers between devices  610 us (79%)
  blocking collectives  99.5 us (13%)
  other arithmetic  23.3 us (3%)
  local copies, waits for them, and re-layouts  15.7 us (2%)
  between operations  14.5 us (2%)
  matrix products  10 us (1%)
    psum x1, waiting for transfers between devices, body(): grad_weight, grad_bias = lax.psum((weight_part, bias_part), ('row', 'col'))  262 us
    reduce_scatter x1, waiting for transfers between devices, body(): lax.psum_scatter(partial_value.astype(jnp.bfloat16), 'col', scatter_dimen...  216 us
    psum x1, blocking collectives, body(): grad_weight, grad_bias = lax.psum((weight_part, bias_part), ('row', 'col'))  99.5 us
    all_gather x1, waiting for transfers between devices, body(): grad_block = lax.all_gather(grad_here, 'col', axis=0, tiled=True)  84.8 us
    all_gather x1, waiting for transfers between devices, body(): panel = lax.all_gather(shares, 'row', axis=0, tiled=True)  46.9 us
  transfers between devices with their start and end apart: 5, of which 4 were waited for; matrix products, arithmetic and copies ran while one was open for 0% of the time, Pallas kernels for 0%

commit v1 on v0

v1 whole, which is shorter than its diff:
```python
import jax
import jax.numpy as jnp
from jax import lax
from jax.experimental import pallas as pl
from jax.experimental.pallas import tpu as pltpu
from jax.sharding import Mesh, PartitionSpec as P

COL = ("z", "x")
ROW = ("y", "core")
VMEM = pl.BlockSpec(memory_space=pltpu.VMEM)
SMEM = pl.BlockSpec(memory_space=pltpu.SMEM)
F32 = jnp.float32
BF16 = jnp.bfloat16


def forward_kernel(info, tiles, own, other, out, total):
    slots = tiles.shape[0]
    core = info[2 * slots + 1]
    total[...] = jnp.zeros_like(total)

    def step(k, _):
        r = info[k]
        c = info[slots + k]
        half = c // 2
        mine = (c % 2) == core
        picked = jnp.where(mine, own[half], other[half])
        total[r] += jnp.dot(tiles[k], picked, preferred_element_type=F32)
        return 0

    lax.fori_loop(0, info[2 * slots], step, 0)
    out[...] = total[...].astype(out.dtype)


def backward_kernel(info, tiles, g0, g1, g2, g3, keep, send, total):
    slots = tiles.shape[0]
    core = info[2 * slots + 1]
    here = info[2 * slots + 2]
    n_half = keep.shape[0]
    total[...] = jnp.zeros_like(total)

    def step(k, _):
        r = info[k]
        c = info[slots + k]
        z = r // 4
        d = (r % 4 - here + 4) % 4
        picked = jnp.where(
            d < 2,
            jnp.where(d == 0, g0[z], g1[z]),
            jnp.where(d == 2, g2[z], g3[z]),
        )
        place = jnp.where((c % 2) == core, 0, n_half) + c // 2
        total[place] += lax.dot_general(
            tiles[k], picked, (((0,), (0,)), ((), ())), preferred_element_type=F32
        )
        return 0

    lax.fori_loop(0, info[2 * slots], step, 0)
    keep[...] = total[:n_half]
    send[...] = total[n_half:].astype(send.dtype)


def repeat(a, n):
    return jnp.broadcast_to(a[None], (n,) + a.shape)


def body(
    features, col_norm, weight, bias, tile_coords, tile_count, tile_values, row_norm, cotangent
):
    n, hidden = features.shape
    n_y, n_core = lax.axis_size("y"), lax.axis_size("core")
    n_z, n_x = lax.axis_size("z"), lax.axis_size("x")
    tile_rows, tile_cols = n_z * n_x, n_y * n_core
    scale = float(n * tile_rows * tile_cols) ** (-0.5)
    tiles = tile_values[0, 0]
    coords = tile_coords[0, 0]
    swap = [(0, 1), (1, 0)]
    info = jnp.concatenate(
        [
            coords[:, 0],
            coords[:, 1],
            tile_count[0],
            lax.axis_index("core").reshape(1),
            lax.axis_index("x").reshape(1),
        ]
    )

    share = (col_norm[:, None] * features.astype(F32)).astype(BF16)
    own = lax.all_to_all(repeat(share, n_y), "y", 0, 0, tiled=True)
    other = lax.ppermute(own, "core", swap)

    part = hidden // 2
    sums = []
    for h in range(2):
        block = pl.pallas_call(
            forward_kernel,
            out_shape=jax.ShapeDtypeStruct((tile_rows, n, part), BF16),
            in_specs=[SMEM, VMEM, VMEM, VMEM],
            out_specs=VMEM,
            scratch_shapes=[pltpu.VMEM((tile_rows, n, part), F32)],
            compiler_params=pltpu.CompilerParams(vmem_limit_bytes=40 * 2**20),
            name="forward_tiles",
        )(info, tiles, own[:, :, h * part : (h + 1) * part], other[:, :, h * part : (h + 1) * part])
        terms = lax.all_to_all(block, COL, 0, 0, tiled=True)
        sums.append(jnp.sum(terms.astype(F32), axis=0))
    mixed = jnp.concatenate(sums, axis=1)

    high = mixed.astype(BF16)
    low = (mixed - high.astype(F32)).astype(BF16)
    rowsum = jnp.dot(high, weight, preferred_element_type=F32) + jnp.dot(
        low, weight, preferred_element_type=F32
    )
    pre = row_norm[:, None] * rowsum + bias[None, :]
    sigma = jax.nn.sigmoid(pre)
    output = (pre * sigma).astype(BF16)
    grad_pre = cotangent.astype(F32) * (sigma * (1.0 + pre * (1.0 - sigma)))
    grad_here = (grad_pre * row_norm[:, None]).astype(BF16)

    g0 = lax.all_to_all(repeat(grad_here, n_z), "z", 0, 0, tiled=True)
    g = [g0]
    for d in range(1, n_x):
        g.append(lax.ppermute(g0, "x", [((i + d) % n_x, i) for i in range(n_x)]))

    weight_part = lax.dot_general(
        high, grad_here, (((0,), (0,)), ((), ())), preferred_element_type=F32
    )
    bias_part = jnp.sum(grad_pre, axis=0)
    both = jnp.concatenate(
        [weight_part, jnp.broadcast_to(bias_part[:, None], (hidden, 128))], axis=1
    )
    both = (both * scale).reshape(tile_rows, hidden // tile_rows, hidden + 128)
    both = jnp.sum(lax.all_to_all(both, COL, 0, 0, tiled=True), axis=0)
    both = jnp.sum(lax.all_to_all(repeat(both, tile_cols), ROW, 0, 0, tiled=True), axis=0)
    both = lax.all_to_all(repeat(both, tile_rows), COL, 0, 0, tiled=True)
    both = both.reshape(hidden, hidden + 128)
    grad_weight = both[:, :hidden]
    grad_bias = both[:, hidden]

    keep, send = pl.pallas_call(
        backward_kernel,
        out_shape=(
            jax.ShapeDtypeStruct((n_y, n, hidden), F32),
            jax.ShapeDtypeStruct((n_y, n, hidden), BF16),
        ),
        in_specs=[SMEM, VMEM, VMEM, VMEM, VMEM, VMEM],
        out_specs=(VMEM, VMEM),
        scratch_shapes=[pltpu.VMEM((tile_cols, n, hidden), F32)],
        compiler_params=pltpu.CompilerParams(vmem_limit_bytes=40 * 2**20),
        name="backward_tiles",
    )(info, tiles, *g)
    pair = (keep + lax.ppermute(send, "core", swap).astype(F32)).astype(BF16)
    column_total = jnp.sum(lax.all_to_all(pair, "y", 0, 0, tiled=True).astype(F32), axis=0)
    grad_mixed = (col_norm[:, None] * column_total).astype(BF16)
    grad_features = lax.dot_general(
        grad_mixed, weight, (((1,), (1,)), ((), ())), preferred_element_type=F32
    ).astype(BF16)
    return (output, grad_features, grad_weight, grad_bias)


def solution(mesh):
    devices = mesh.devices
    sub = Mesh(devices.reshape(8, 2, 8, 4), ("y", "core", "z", "x"))
    by_col = ("z", "x", "y", "core")
    by_row = ("y", "core", "z", "x")
    in_specs = (
        P(by_col, None),
        P(by_col),
        P(),
        P(),
        P(ROW, COL, None, None),
        P(ROW, COL),
        P(ROW, COL, None, None, None),
        P(by_row),
        P(by_row, None),
    )
    out_specs = (P(by_row, None), P(by_col, None), P(), P())
    return jax.shard_map(body, mesh=sub, in_specs=in_specs, out_specs=out_specs, check_vma=False)
```

time: 774 us -> 223 us (0.29)
  waiting for transfers between devices: 610 us -> 109 us
  blocking collectives: 99.5 us -> 22.2 us
  starting transfers between devices: 0.21 us -> 68.2 us
  other arithmetic: 23.3 us -> 4.11 us
  between operations: 14.5 us -> 1.57 us
  local copies, waits for them, and re-layouts: 15.7 us -> 6.33 us
  Pallas kernels: 0 us -> 8 us
  matrix products: 10 us -> 2.06 us
    psum x1 -> x0, waiting for transfers between devices: 262 us -> none  [body(): grad_weight, grad_bias = lax.psum((weight_part, bias_part), ('row', 'col'))]
    reduce_scatter x2 -> x0, waiting for transfers between devices: 216 us -> none  [the longest x1 216 us: body(): lax.psum_scatter(partial_value.astype(jnp.bfloat16), 'col', scatter_dimen...]
    all_gather x2 -> x0, waiting for transfers between devices: 132 us -> none  [the longest x1 84.8 us: body(): grad_block = lax.all_gather(grad_here, 'col', axis=0, tiled=True)]
    psum x1 -> x0, blocking collectives: 99.5 us -> none  [body(): grad_weight, grad_bias = lax.psum((weight_part, bias_part), ('row', 'col'))]
    all_to_all x0 -> x7, waiting for transfers between devices: none -> 94.6 us  [the longest x2 50.8 us: body(): terms = lax.all_to_all(block, COL, 0, 0, tiled=True)]
    all_to_all x0 -> x7, starting transfers between devices: none -> 50.5 us  [the longest x2 19.7 us: body(): terms = lax.all_to_all(block, COL, 0, 0, tiled=True)]
    all_to_all x0 -> x1, blocking collectives: none -> 22.2 us  [body(): own = lax.all_to_all(repeat(share, n_y), 'y', 0, 0, tiled=True)]
    ppermute x0 -> x5, starting transfers between devices: none -> 17.7 us  [the longest x3 9.32 us: body(): g.append(lax.ppermute(g0, 'x', [((i + d) % n_x, i) for i in range(n_x)]))]
  transfers between devices with their start and end apart: 5 -> 12, of which waited for: 4 -> 9; matrix products, arithmetic and copies ran while one was open for 0% -> 3% of each run, Pallas kernels for 0% -> 2%
where the time goes in v1:
time: 223 us; the launch traced here: 221 us
  waiting for transfers between devices  109 us (49%)
  starting transfers between devices  68.2 us (31%)
  blocking collectives  22.2 us (10%)
  Pallas kernels  8 us (4%)
  local copies, waits for them, and re-layouts  6.33 us (3%)
  other arithmetic  4.11 us (2%)
    all_to_all x2, waiting for transfers between devices, body(): terms = lax.all_to_all(block, COL, 0, 0, tiled=True)  50.8 us
    all_to_all x1, blocking collectives, body(): own = lax.all_to_all(repeat(share, n_y), 'y', 0, 0, tiled=True)  22.2 us
    all_to_all x2, starting transfers between devices, body(): terms = lax.all_to_all(block, COL, 0, 0, tiled=True)  19.7 us
    all_to_all x1, waiting for transfers between devices, body(): lax.all_to_all(pair, 'y', 0, 0, tiled=True).astype(F32)  14.5 us
    all_to_all x1, waiting for transfers between devices, body(): both = lax.all_to_all(repeat(both, tile_rows), COL, 0, 0, tiled=True)  13.5 us
    ppermute x3, waiting for transfers between devices, body(): g.append(lax.ppermute(g0, 'x', [((i + d) % n_x, i) for i in range(n_x)]))  13.3 us
    all_to_all x1, waiting for transfers between devices, body(): g0 = lax.all_to_all(repeat(grad_here, n_z), 'z', 0, 0, tiled=True)  13.2 us
    ppermute x3, starting transfers between devices, body(): g.append(lax.ppermute(g0, 'x', [((i + d) % n_x, i) for i in range(n_x)]))  9.32 us
  transfers between devices with their start and end apart: 12, of which 9 were waited for; matrix products, arithmetic and copies ran while one was open for 3% of the time, Pallas kernels for 2%

profile of v1, /device:TPU:1, one launch (start us, length us, event | category | flops | bytes accessed | tf_op | source)
XLA Modules:
  0.0 221.0 jit_solution(12027439257098268142)
XLA Ops:
  1.7 22.2 %all_to_all.40 = bf16[8,128,256]{2,1,0:T(8,128)(2,1)S(1)} all-to-all(bf16[8,128,256]{2,1,0:T(8,128)(2,1)S(1)} %broadcast_in_dim.12), channel_id=1, replica_groups=mesh['y'=8,'core'=2,'z'=8,'x'=4] {'y'}, dimensions={0} | all-to-all | bytes 1048576 | tf_op jit(solution)/shard_map/all_to_all | solution.py:88
  23.9 5.6 %collective-permute-start = (bf16[8,128,256]{2,1,0:T(8,128)(2,1)S(1)}, bf16[8,128,256]{2,1,0:T(8,128)(2,1)S(1)}, u32[]{:S(2)}, u32[]{:S(2)}) collective-permute-start(bf16[8,128,256]{2,1,0:T(8,128)(2,1)S(1)} %all_to_all.40), channel_id=1, source_target_pairs={{0,32},{32,0},{1,33},{33,1},{2,34},{34,2},{3,35},{35,3},{4,36},{36... | collective-permute-start | bytes 1572872 | tf_op jit(solution)/shard_map/ppermute | solution.py:89
  31.4 2.6 %forward_tiles.3 = bf16[32,128,128]{2,1,0:T(8,128)(2,1)} custom-call(s32[51]{0:T(128)S(1)} %concatenate.12.info, bf16[24,128,128]{2,1,0:T(8,128)(2,1)S(1)} %bitcast.17, bf16[8,128,128]{2,1,0:T(8,128)(2,1)S(1)} %get-tuple-element.13.own, bf16[8,128,128]{2,1,0:T(8,128)(2,1)S(1)} %get-tuple-element.11.other), custom_call_target="tpu_custom_call" | custom-call | tf_op jit(solution)/shard_map/forward_tiles/pallas_call | solution.py:94
  34.0 14.7 %all-to-all-start.2 = ((bf16[32,128,128]{2,1,0:T(8,128)(2,1)}), bf16[32,128,128]{2,1,0:T(8,128)(2,1)S(1)}, u32[]{:S(2)}, u32[]{:S(2)}) async-start(bf16[32,128,128]{2,1,0:T(8,128)(2,1)} %forward_tiles.3), calls=%async_computation.2 | async-start | bytes 2097152 | tf_op jit(solution)/shard_map/all_to_all | solution.py:103
  48.8 2.6 %forward_tiles.2 = bf16[32,128,128]{2,1,0:T(8,128)(2,1)} custom-call(s32[51]{0:T(128)S(1)} %concatenate.12.info, bf16[24,128,128]{2,1,0:T(8,128)(2,1)S(1)} %bitcast.18, bf16[8,128,128]{2,1,0:T(8,128)(2,1)S(1)} %get-tuple-element.12.own, bf16[8,128,128]{2,1,0:T(8,128)(2,1)S(1)} %get-tuple-element.10.other), custom_call_target="tpu_custom_call" | custom-call | tf_op jit(solution)/shard_map/forward_tiles/pallas_call | solution.py:94
  51.4 25.4 %all-to-all-done.2 = bf16[32,128,128]{2,1,0:T(8,128)(2,1)S(1)} async-done(((bf16[32,128,128]{2,1,0:T(8,128)(2,1)}), bf16[32,128,128]{2,1,0:T(8,128)(2,1)S(1)}, u32[]{:S(2)}, u32[]{:S(2)}) %all-to-all-start.2) | async-done | bytes 1048608 | tf_op jit(solution)/shard_map/all_to_all | solution.py:103
  76.8 5.0 %all-to-all-start.1 = ((bf16[32,128,128]{2,1,0:T(8,128)(2,1)}), bf16[32,128,128]{2,1,0:T(8,128)(2,1)S(1)}, u32[]{:S(2)}, u32[]{:S(2)}) async-start(bf16[32,128,128]{2,1,0:T(8,128)(2,1)} %forward_tiles.2), calls=%async_computation.1 | async-start | bytes 2097152 | tf_op jit(solution)/shard_map/all_to_all | solution.py:103
  82.0 25.4 %all-to-all-done.1 = bf16[32,128,128]{2,1,0:T(8,128)(2,1)S(1)} async-done(((bf16[32,128,128]{2,1,0:T(8,128)(2,1)}), bf16[32,128,128]{2,1,0:T(8,128)(2,1)S(1)}, u32[]{:S(2)}, u32[]{:S(2)}) %all-to-all-start.1) | async-done | bytes 1048608 | tf_op jit(solution)/shard_map/all_to_all | solution.py:103
  109.6 4.5 %all-to-all-start.3 = ((bf16[8,128,256]{2,1,0:T(8,128)(2,1)}), bf16[8,128,256]{2,1,0:T(8,128)(2,1)S(1)}, u32[]{:S(2)}, u32[]{:S(2)}) async-start(bf16[8,128,256]{2,1,0:T(8,128)(2,1)} %broadcast_in_dim.13), calls=%async_computation.3 | async-start | bytes 1048576 | tf_op jit(solution)/shard_map/all_to_all | solution.py:118
  115.2 13.2 %all-to-all-done.3.g0 = bf16[8,128,256]{2,1,0:T(8,128)(2,1)S(1)} async-done(((bf16[8,128,256]{2,1,0:T(8,128)(2,1)}), bf16[8,128,256]{2,1,0:T(8,128)(2,1)S(1)}, u32[]{:S(2)}, u32[]{:S(2)}) %all-to-all-start.3) | async-done | bytes 524320 | tf_op jit(solution)/shard_map/all_to_all | solution.py:118
  128.4 5.6 %all-to-all-start.5 = ((f32[32,8,384]{2,1,0:T(8,128)}), f32[32,8,384]{2,1,0:T(8,128)S(1)}, u32[]{:S(2)}, u32[]{:S(2)}) async-start(f32[32,8,384]{2,1,0:T(8,128)} %maximum_multiply_fusion), calls=%async_computation.5 | async-start | bytes 786432 | tf_op jit(solution)/shard_map/all_to_all | solution.py:131
  134.0 4.3 %collective-permute-start.1 = (bf16[8,128,256]{2,1,0:T(8,128)(2,1)S(1)}, bf16[8,128,256]{2,1,0:T(8,128)(2,1)S(1)}, u32[]{:S(2)}, u32[]{:S(2)}) collective-permute-start(bf16[8,128,256]{2,1,0:T(8,128)(2,1)S(1)} %all-to-all-done.3.g0), channel_id=1, source_target_pairs={{1,0},{2,1},{3,2},{0,3},{5,4},{6,5},{7,6},{4,7},{9,8},{10,9},{11,1... | collective-permute-start | bytes 1572872 | tf_op jit(solution)/shard_map/ppermute | solution.py:121
  138.4 2.5 %collective-permute-start.2 = (bf16[8,128,256]{2,1,0:T(8,128)(2,1)S(1)}, bf16[8,128,256]{2,1,0:T(8,128)(2,1)S(1)}, u32[]{:S(2)}, u32[]{:S(2)}) collective-permute-start(bf16[8,128,256]{2,1,0:T(8,128)(2,1)S(1)} %all-to-all-done.3.g0), channel_id=1, source_target_pairs={{2,0},{3,1},{0,2},{1,3},{6,4},{7,5},{4,6},{5,7},{10,8},{11,9},{8,1... | collective-permute-start | bytes 1572872 | tf_op jit(solution)/shard_map/ppermute | solution.py:121
  140.9 2.5 %collective-permute-start.3 = (bf16[8,128,256]{2,1,0:T(8,128)(2,1)S(1)}, bf16[8,128,256]{2,1,0:T(8,128)(2,1)S(1)}, u32[]{:S(2)}, u32[]{:S(2)}) collective-permute-start(bf16[8,128,256]{2,1,0:T(8,128)(2,1)S(1)} %all-to-all-done.3.g0), channel_id=1, source_target_pairs={{3,0},{0,1},{1,2},{2,3},{7,4},{4,5},{5,6},{6,7},{11,8},{8,9},{9,10... | collective-permute-start | bytes 1572872 | tf_op jit(solution)/shard_map/ppermute | solution.py:121
  143.4 2.6 %all-to-all-done.5 = f32[32,8,384]{2,1,0:T(8,128)S(1)} async-done(((f32[32,8,384]{2,1,0:T(8,128)}), f32[32,8,384]{2,1,0:T(8,128)S(1)}, u32[]{:S(2)}, u32[]{:S(2)}) %all-to-all-start.5) | async-done | bytes 393248 | tf_op jit(solution)/shard_map/all_to_all | solution.py:131
  146.7 8.4 %all-to-all-start.6 = ((f32[16,8,384]{2,1,0:T(8,128)}), f32[16,8,384]{2,1,0:T(8,128)}, u32[]{:S(2)}, u32[]{:S(2)}) async-start(f32[16,8,384]{2,1,0:T(8,128)} %broadcast_in_dim.16), calls=%async_computation.6 | async-start | bytes 393216 | tf_op jit(solution)/shard_map/all_to_all | solution.py:132
  155.5 12.9 %collective-permute-done.3.g3 = bf16[8,128,256]{2,1,0:T(8,128)(2,1)S(1)} collective-permute-done((bf16[8,128,256]{2,1,0:T(8,128)(2,1)S(1)}, bf16[8,128,256]{2,1,0:T(8,128)(2,1)S(1)}, u32[]{:S(2)}, u32[]{:S(2)}) %collective-permute-start.3) | collective-permute-done | bytes 524320 | tf_op jit(solution)/shard_map/ppermute | solution.py:121
  169.2 1.0 copy-done.3
  170.3 2.7 %backward_tiles.1 = (f32[8,128,256]{2,1,0:T(8,128)S(1)}, bf16[8,128,256]{2,1,0:T(8,128)(2,1)}) custom-call(s32[51]{0:T(128)S(1)} %concatenate.12.info, bf16[24,128,128]{2,1,0:T(8,128)(2,1)S(1)} %bitcast.19, bf16[8,128,256]{2,1,0:T(8,128)(2,1)S(1)} %all-to-all-done.3.g0, bf16[8,128,256]{2,1,0:T(8,128)(2,1)S(1)} %collective-permute-done.1.g1, ...), custom_call_target="tpu_custom_call" | custom-call | tf_op jit(solution)/shard_map/backward_tiles/pallas_call | solution.py:138
  173.0 2.7 %collective-permute-start.4 = (bf16[8,128,256]{2,1,0:T(8,128)(2,1)}, bf16[8,128,256]{2,1,0:T(8,128)(2,1)S(1)}, u32[]{:S(2)}, u32[]{:S(2)}) collective-permute-start(bf16[8,128,256]{2,1,0:T(8,128)(2,1)} %get-tuple-element.7), channel_id=1, source_target_pairs={{0,32},{32,0},{1,33},{33,1},{2,34},{34,2},{3,35},{35,3},{4,36},{36... | collective-permute-start | bytes 1572872 | tf_op jit(solution)/shard_map/ppermute | solution.py:150
  177.5 8.8 %all-to-all-start.7 = ((f32[32,8,384]{2,1,0:T(8,128)}), f32[32,8,384]{2,1,0:T(8,128)S(1)}, u32[]{:S(2)}, u32[]{:S(2)}) async-start(f32[32,8,384]{2,1,0:T(8,128)} %broadcast_in_dim.17), calls=%async_computation.7 | async-start | bytes 786432 | tf_op jit(solution)/shard_map/all_to_all | solution.py:133
  187.2 13.5 %all-to-all-done.7 = f32[32,8,384]{2,1,0:T(8,128)S(1)} async-done(((f32[32,8,384]{2,1,0:T(8,128)}), f32[32,8,384]{2,1,0:T(8,128)S(1)}, u32[]{:S(2)}, u32[]{:S(2)}) %all-to-all-start.7) | async-done | bytes 393248 | tf_op jit(solution)/shard_map/all_to_all | solution.py:133
  200.7 3.5 %all-to-all-start.4 = ((bf16[8,128,256]{2,1,0:T(8,128)(2,1)}), bf16[8,128,256]{2,1,0:T(8,128)(2,1)S(1)}, u32[]{:S(2)}, u32[]{:S(2)}) async-start(bf16[8,128,256]{2,1,0:T(8,128)(2,1)} %add_convert_fusion), calls=%async_computation.4 | async-start | bytes 1048576 | tf_op jit(solution)/shard_map/all_to_all | solution.py:151
  205.6 14.5 %all-to-all-done.4 = bf16[8,128,256]{2,1,0:T(8,128)(2,1)S(1)} async-done(((bf16[8,128,256]{2,1,0:T(8,128)(2,1)}), bf16[8,128,256]{2,1,0:T(8,128)(2,1)S(1)}, u32[]{:S(2)}, u32[]{:S(2)}) %all-to-all-start.4) | async-done | bytes 524320 | tf_op jit(solution)/shard_map/all_to_all | solution.py:151
  (51 shorter events, 12.5 us)
Async XLA Ops:
  0.6 106.9 %copy-start = (bf16[256,256]{1,0:T(8,128)(2,1)S(1)}, bf16[256,256]{1,0:T(8,128)(2,1)}, u32[]{:S(2)}) copy-start(bf16[256,256]{1,0:T(8,128)(2,1)} %param.11) | copy-start | bytes 393220
  0.6 29.5 %copy-start.7 = (s32[1,1,24,2]{2,3,1,0:T(2,128)S(1)}, s32[1,1,24,2]{2,3,1,0:T(2,128)}, u32[]{:S(2)}) copy-start(s32[1,1,24,2]{2,3,1,0:T(2,128)} %param.13) | copy-start | bytes 580
  23.9 7.1 %collective-permute-start = (bf16[8,128,256]{2,1,0:T(8,128)(2,1)S(1)}, bf16[8,128,256]{2,1,0:T(8,128)(2,1)S(1)}, u32[]{:S(2)}, u32[]{:S(2)}) collective-permute-start(bf16[8,128,256]{2,1,0:T(8,128)(2,1)S(1)} %all_to_all.40), channel_id=1, source_target_pairs={{0,32},{32,0},{1,33},{33,1},{2,34},{34,2},{3,35},{35,3},{4,36},{36... | collective-permute-start | bytes 1572872 | tf_op jit(solution)/shard_map/ppermute | solution.py:89
  30.2 1.1 copy-start.1
  34.0 42.8 %all-to-all-start.2 = ((bf16[32,128,128]{2,1,0:T(8,128)(2,1)}), bf16[32,128,128]{2,1,0:T(8,128)(2,1)S(1)}, u32[]{:S(2)}, u32[]{:S(2)}) async-start(bf16[32,128,128]{2,1,0:T(8,128)(2,1)} %forward_tiles.3), calls=%async_computation.2 | async-start | bytes 2097152 | tf_op jit(solution)/shard_map/all_to_all | solution.py:103
  76.8 30.6 %all-to-all-start.1 = ((bf16[32,128,128]{2,1,0:T(8,128)(2,1)}), bf16[32,128,128]{2,1,0:T(8,128)(2,1)S(1)}, u32[]{:S(2)}, u32[]{:S(2)}) async-start(bf16[32,128,128]{2,1,0:T(8,128)(2,1)} %forward_tiles.2), calls=%async_computation.1 | async-start | bytes 2097152 | tf_op jit(solution)/shard_map/all_to_all | solution.py:103
  81.8 26.0 %copy-start.8 = (f32[128]{0:T(128)S(1)}, f32[128]{0:T(128)}, u32[]{:S(2)}) copy-start(f32[128]{0:T(128)} %param.16) | copy-start | bytes 1540
  81.8 26.0 %copy-start.9 = (bf16[128,256]{1,0:T(8,128)(2,1)S(1)}, bf16[128,256]{1,0:T(8,128)(2,1)}, u32[]{:S(2)}) copy-start(bf16[128,256]{1,0:T(8,128)(2,1)} %param.17) | copy-start | bytes 196612
  81.8 26.0 %copy-start.10 = (f32[256]{0:T(256)S(1)}, f32[256]{0:T(256)}, u32[]{:S(2)}) copy-start(f32[256]{0:T(256)} %param.12) | copy-start | bytes 3076
  82.0 26.7 %copy-start.4 = (f32[128,128]{1,0:T(8,128)}, f32[128,128]{1,0:T(8,128)S(1)}, u32[]{:S(2)}) copy-start(f32[128,128]{1,0:T(8,128)S(1)} %convert_reduce_fusion) | copy-start | bytes 196612
  108.6 5.5 %copy-start.5 = (f32[128,128]{1,0:T(8,128)S(1)}, f32[128,128]{1,0:T(8,128)}, u32[]{:S(2)}) copy-start(f32[128,128]{1,0:T(8,128)} %copy-done.4) | copy-start | bytes 196612
  109.6 18.9 %all-to-all-start.3 = ((bf16[8,128,256]{2,1,0:T(8,128)(2,1)}), bf16[8,128,256]{2,1,0:T(8,128)(2,1)S(1)}, u32[]{:S(2)}, u32[]{:S(2)}) async-start(bf16[8,128,256]{2,1,0:T(8,128)(2,1)} %broadcast_in_dim.13), calls=%async_computation.3 | async-start | bytes 1048576 | tf_op jit(solution)/shard_map/all_to_all | solution.py:118
  128.4 17.5 %all-to-all-start.5 = ((f32[32,8,384]{2,1,0:T(8,128)}), f32[32,8,384]{2,1,0:T(8,128)S(1)}, u32[]{:S(2)}, u32[]{:S(2)}) async-start(f32[32,8,384]{2,1,0:T(8,128)} %maximum_multiply_fusion), calls=%async_computation.5 | async-start | bytes 786432 | tf_op jit(solution)/shard_map/all_to_all | solution.py:131
  134.0 21.1 %collective-permute-start.1 = (bf16[8,128,256]{2,1,0:T(8,128)(2,1)S(1)}, bf16[8,128,256]{2,1,0:T(8,128)(2,1)S(1)}, u32[]{:S(2)}, u32[]{:S(2)}) collective-permute-start(bf16[8,128,256]{2,1,0:T(8,128)(2,1)S(1)} %all-to-all-done.3.g0), channel_id=1, source_target_pairs={{1,0},{2,1},{3,2},{0,3},{5,4},{6,5},{7,6},{4,7},{9,8},{10,9},{11,1... | collective-permute-start | bytes 1572872 | tf_op jit(solution)/shard_map/ppermute | solution.py:121
  138.4 17.2 %collective-permute-start.2 = (bf16[8,128,256]{2,1,0:T(8,128)(2,1)S(1)}, bf16[8,128,256]{2,1,0:T(8,128)(2,1)S(1)}, u32[]{:S(2)}, u32[]{:S(2)}) collective-permute-start(bf16[8,128,256]{2,1,0:T(8,128)(2,1)S(1)} %all-to-all-done.3.g0), channel_id=1, source_target_pairs={{2,0},{3,1},{0,2},{1,3},{6,4},{7,5},{4,6},{5,7},{10,8},{11,9},{8,1... | collective-permute-start | bytes 1572872 | tf_op jit(solution)/shard_map/ppermute | solution.py:121
  140.9 27.6 %collective-permute-start.3 = (bf16[8,128,256]{2,1,0:T(8,128)(2,1)S(1)}, bf16[8,128,256]{2,1,0:T(8,128)(2,1)S(1)}, u32[]{:S(2)}, u32[]{:S(2)}) collective-permute-start(bf16[8,128,256]{2,1,0:T(8,128)(2,1)S(1)} %all-to-all-done.3.g0), channel_id=1, source_target_pairs={{3,0},{0,1},{1,2},{2,3},{7,4},{4,5},{5,6},{6,7},{11,8},{8,9},{9,10... | collective-permute-start | bytes 1572872 | tf_op jit(solution)/shard_map/ppermute | solution.py:121
  146.7 29.0 %all-to-all-start.6 = ((f32[16,8,384]{2,1,0:T(8,128)}), f32[16,8,384]{2,1,0:T(8,128)}, u32[]{:S(2)}, u32[]{:S(2)}) async-start(f32[16,8,384]{2,1,0:T(8,128)} %broadcast_in_dim.16), calls=%async_computation.6 | async-start | bytes 393216 | tf_op jit(solution)/shard_map/all_to_all | solution.py:132
  168.4 0.8 copy-start.2
  169.2 1.0 copy-start.3
  173.0 13.3 %collective-permute-start.4 = (bf16[8,128,256]{2,1,0:T(8,128)(2,1)}, bf16[8,128,256]{2,1,0:T(8,128)(2,1)S(1)}, u32[]{:S(2)}, u32[]{:S(2)}) collective-permute-start(bf16[8,128,256]{2,1,0:T(8,128)(2,1)} %get-tuple-element.7), channel_id=1, source_target_pairs={{0,32},{32,0},{1,33},{33,1},{2,34},{34,2},{3,35},{35,3},{4,36},{36... | collective-permute-start | bytes 1572872 | tf_op jit(solution)/shard_map/ppermute | solution.py:150
  177.5 23.3 %all-to-all-start.7 = ((f32[32,8,384]{2,1,0:T(8,128)}), f32[32,8,384]{2,1,0:T(8,128)S(1)}, u32[]{:S(2)}, u32[]{:S(2)}) async-start(f32[32,8,384]{2,1,0:T(8,128)} %broadcast_in_dim.17), calls=%async_computation.7 | async-start | bytes 786432 | tf_op jit(solution)/shard_map/all_to_all | solution.py:133
  187.2 33.0 %copy-start.6 = (f32[128]{0:T(128)S(1)}, f32[128]{0:T(128)}, u32[]{:S(2)}) copy-start(f32[128]{0:T(128)} %param.10) | copy-start | bytes 1540
  200.7 19.4 %all-to-all-start.4 = ((bf16[8,128,256]{2,1,0:T(8,128)(2,1)}), bf16[8,128,256]{2,1,0:T(8,128)(2,1)S(1)}, u32[]{:S(2)}, u32[]{:S(2)}) async-start(bf16[8,128,256]{2,1,0:T(8,128)(2,1)} %add_convert_fusion), calls=%async_computation.4 | async-start | bytes 1048576 | tf_op jit(solution)/shard_map/all_to_all | solution.py:151

commit v2 on v1

--- a/solution.py
+++ b/solution.py
@@ -13,50 +13,74 @@
 BF16 = jnp.bfloat16
 
 
-def forward_kernel(info, tiles, own, other, out, total):
+UNROLL = 4
+
+
+def forward_kernel(info, tiles, own, other, o0, o1, o2, o3, total):
     slots = tiles.shape[0]
+    count = info[2 * slots]
     core = info[2 * slots + 1]
+    here = info[2 * slots + 2]
+    n_x, n_z = 4, o0.shape[0]
     total[...] = jnp.zeros_like(total)
 
-    def step(k, _):
-        r = info[k]
-        c = info[slots + k]
-        half = c // 2
-        mine = (c % 2) == core
-        picked = jnp.where(mine, own[half], other[half])
-        total[r] += jnp.dot(tiles[k], picked, preferred_element_type=F32)
+    def step(b, _):
+        places, products = [], []
+        for u in range(UNROLL):
+            k = b * UNROLL + u
+            r = info[k]
+            c = info[slots + k]
+            half = c // 2
+            picked = jnp.where((c % 2) == core, own[half], other[half])
+            product = jnp.dot(tiles[k], picked, preferred_element_type=F32)
+            products.append(jnp.where(k < count, product, 0.0))
+            places.append((r % n_x - here + n_x) % n_x * n_z + r // n_x)
+        for place, product in zip(places, products):
+            total[place] += product
         return 0
 
-    lax.fori_loop(0, info[2 * slots], step, 0)
-    out[...] = total[...].astype(out.dtype)
+    lax.fori_loop(0, (count + UNROLL - 1) // UNROLL, step, 0)
+    for d, out in enumerate((o0, o1, o2, o3)):
+        out[...] = total[d * n_z : (d + 1) * n_z].astype(out.dtype)
 
 
 def backward_kernel(info, tiles, g0, g1, g2, g3, keep, send, total):
     slots = tiles.shape[0]
+    count = info[2 * slots]
     core = info[2 * slots + 1]
     here = info[2 * slots + 2]
     n_half = keep.shape[0]
     total[...] = jnp.zeros_like(total)
 
-    def step(k, _):
-        r = info[k]
-        c = info[slots + k]
-        z = r // 4
-        d = (r % 4 - here + 4) % 4
-        picked = jnp.where(
-            d < 2,
-            jnp.where(d == 0, g0[z], g1[z]),
-            jnp.where(d == 2, g2[z], g3[z]),
-        )
-        place = jnp.where((c % 2) == core, 0, n_half) + c // 2
-        total[place] += lax.dot_general(
-            tiles[k], picked, (((0,), (0,)), ((), ())), preferred_element_type=F32
-        )
+    def step(b, _):
+        places, products = [], []
+        for u in range(UNROLL):
+            k = b * UNROLL + u
+            r = info[k]
+            c = info[slots + k]
+            z = r // 4
+            d = (r % 4 - here + 4) % 4
+            picked = jnp.where(
+                d < 2,
+                jnp.where(d == 0, g0[z], g1[z]),
+                jnp.where(d == 2, g2[z], g3[z]),
+            )
+            product = lax.dot_general(
+                tiles[k], picked, (((0,), (0,)), ((), ())), preferred_element_type=F32
+            )
+            products.append(jnp.where(k < count, product, 0.0))
+            places.append(jnp.where((c % 2) == core, 0, n_half) + c // 2)
+        for place, product in zip(places, products):
+            total[place] += product
         return 0
 
-    lax.fori_loop(0, info[2 * slots], step, 0)
+    lax.fori_loop(0, (count + UNROLL - 1) // UNROLL, step, 0)
     keep[...] = total[:n_half]
     send[...] = total[n_half:].astype(send.dtype)
+
+
+def ring(n, d):
+    return [(i, (i + d) % n) for i in range(n)]
 
 
 def repeat(a, n):
@@ -91,16 +115,20 @@
     part = hidden // 2
     sums = []
     for h in range(2):
-        block = pl.pallas_call(
+        cut = slice(h * part, (h + 1) * part)
+        blocks = pl.pallas_call(
             forward_kernel,
-            out_shape=jax.ShapeDtypeStruct((tile_rows, n, part), BF16),
+            out_shape=(jax.ShapeDtypeStruct((n_z, n, part), BF16),) * n_x,
             in_specs=[SMEM, VMEM, VMEM, VMEM],
-            out_specs=VMEM,
+            out_specs=(VMEM,) * n_x,
             scratch_shapes=[pltpu.VMEM((tile_rows, n, part), F32)],
             compiler_params=pltpu.CompilerParams(vmem_limit_bytes=40 * 2**20),
             name="forward_tiles",
-        )(info, tiles, own[:, :, h * part : (h + 1) * part], other[:, :, h * part : (h + 1) * part])
-        terms = lax.all_to_all(block, COL, 0, 0, tiled=True)
+        )(info, tiles, own[:, :, cut], other[:, :, cut])
+        over_x = blocks[0].astype(F32)
+        for d in range(1, n_x):
+            over_x += lax.ppermute(blocks[d], "x", ring(n_x, d)).astype(F32)
+        terms = lax.all_to_all(over_x.astype(BF16), "z", 0, 0, tiled=True)
         sums.append(jnp.sum(terms.astype(F32), axis=0))
     mixed = jnp.concatenate(sums, axis=1)
 

time: 223 us -> 200 us (0.90)
  waiting for transfers between devices: 109 us -> 76.6 us
  starting transfers between devices: 68.2 us -> 77.3 us
  Pallas kernels: 8 us -> 4.44 us
    all_to_all x2, waiting for transfers between devices: 50.8 us -> 19 us  [body(): terms = lax.all_to_all(over_x.astype(BF16), 'z', 0, 0, tiled=True)]
    ppermute x0 -> x6, starting transfers between devices: none -> 19.2 us  [body(): over_x += lax.ppermute(blocks[d], 'x', ring(n_x, d)).astype(F32)]
    all_to_all x2, starting transfers between devices: 19.7 us -> 14.2 us  [body(): terms = lax.all_to_all(over_x.astype(BF16), 'z', 0, 0, tiled=True)]
    pallas_call x2, Pallas kernels: 5.28 us -> 2.36 us  [body(): pl.pallas_call(forward_kernel, out_shape=(jax.ShapeDtypeStruct((n_z, n, p...]
    all_to_all x1, starting transfers between devices: 8.78 us -> 6.04 us  [body(): both = lax.all_to_all(repeat(both, tile_rows), COL, 0, 0, tiled=True)]
  transfers between devices with their start and end apart: 12 -> 18, of which waited for: 9 -> 8; matrix products, arithmetic and copies ran while one was open for 3% -> 4% of each run, Pallas kernels for 2% -> 2%
where the time goes in v2:
time: 200 us; the launch traced here: 198 us
  starting transfers between devices  77.3 us (39%)
  waiting for transfers between devices  76.6 us (38%)
  blocking collectives  22.2 us (11%)
  local copies, waits for them, and re-layouts  8.42 us (4%)
  other arithmetic  5.57 us (3%)
  Pallas kernels  4.44 us (2%)
  matrix products  2.07 us (1%)
    all_to_all x1, blocking collectives, body(): own = lax.all_to_all(repeat(share, n_y), 'y', 0, 0, tiled=True)  22.2 us
    ppermute x6, starting transfers between devices, body(): over_x += lax.ppermute(blocks[d], 'x', ring(n_x, d)).astype(F32)  19.2 us
    all_to_all x2, waiting for transfers between devices, body(): terms = lax.all_to_all(over_x.astype(BF16), 'z', 0, 0, tiled=True)  19 us
    all_to_all x1, waiting for transfers between devices, body(): lax.all_to_all(pair, 'y', 0, 0, tiled=True).astype(F32)  14.4 us
    all_to_all x2, starting transfers between devices, body(): terms = lax.all_to_all(over_x.astype(BF16), 'z', 0, 0, tiled=True)  14.2 us
    all_to_all x1, waiting for transfers between devices, body(): both = lax.all_to_all(repeat(both, tile_rows), COL, 0, 0, tiled=True)  13.5 us
    all_to_all x1, waiting for transfers between devices, body(): g0 = lax.all_to_all(repeat(grad_here, n_z), 'z', 0, 0, tiled=True)  12.9 us
    ppermute x3, waiting for transfers between devices, body(): g.append(lax.ppermute(g0, 'x', [((i + d) % n_x, i) for i in range(n_x)]))  12.7 us
  transfers between devices with their start and end apart: 18, of which 8 were waited for; matrix products, arithmetic and copies ran while one was open for 4% of the time, Pallas kernels for 2%

profile of v2, /device:TPU:1, one launch (start us, length us, event | category | flops | bytes accessed | tf_op | source)
XLA Modules:
  0.0 198.3 jit_solution(1316743453530493586)
XLA Ops:
  1.7 22.2 %all_to_all.40 = bf16[8,128,256]{2,1,0:T(8,128)(2,1)S(1)} all-to-all(bf16[8,128,256]{2,1,0:T(8,128)(2,1)S(1)} %broadcast_in_dim.12), channel_id=1, replica_groups=mesh['y'=8,'core'=2,'z'=8,'x'=4] {'y'}, dimensions={0} | all-to-all | bytes 1048576 | tf_op jit(solution)/shard_map/all_to_all | solution.py:112
  23.9 5.6 %collective-permute-start = (bf16[8,128,256]{2,1,0:T(8,128)(2,1)S(1)}, bf16[8,128,256]{2,1,0:T(8,128)(2,1)S(1)}, u32[]{:S(2)}, u32[]{:S(2)}) collective-permute-start(bf16[8,128,256]{2,1,0:T(8,128)(2,1)S(1)} %all_to_all.40), channel_id=1, source_target_pairs={{0,32},{32,0},{1,33},{33,1},{2,34},{34,2},{3,35},{35,3},{4,36},{36... | collective-permute-start | bytes 1572872 | tf_op jit(solution)/shard_map/ppermute | solution.py:113
  33.3 4.4 %collective-permute-start.6 = (bf16[8,128,128]{2,1,0:T(8,128)(2,1)S(1)}, bf16[8,128,128]{2,1,0:T(8,128)(2,1)S(1)}, u32[]{:S(2)}, u32[]{:S(2)}) collective-permute-start(bf16[8,128,128]{2,1,0:T(8,128)(2,1)S(1)} %get-tuple-element.21), channel_id=1, source_target_pairs={{0,3},{1,0},{2,1},{3,2},{4,7},{5,4},{6,5},{7,6},{8,11},{9,8},{10,9... | collective-permute-start | bytes 786440 | tf_op jit(solution)/shard_map/ppermute | solution.py:130
  37.7 3.2 %collective-permute-start.5 = (bf16[8,128,128]{2,1,0:T(8,128)(2,1)S(1)}, bf16[8,128,128]{2,1,0:T(8,128)(2,1)S(1)}, u32[]{:S(2)}, u32[]{:S(2)}) collective-permute-start(bf16[8,128,128]{2,1,0:T(8,128)(2,1)S(1)} %get-tuple-element.20), channel_id=1, source_target_pairs={{0,2},{1,3},{2,0},{3,1},{4,6},{5,7},{6,4},{7,5},{8,10},{9,11},{10,... | collective-permute-start | bytes 786440 | tf_op jit(solution)/shard_map/ppermute | solution.py:130
  44.1 4.6 %collective-permute-start.3 = (bf16[8,128,128]{2,1,0:T(8,128)(2,1)S(1)}, bf16[8,128,128]{2,1,0:T(8,128)(2,1)S(1)}, u32[]{:S(2)}, u32[]{:S(2)}) collective-permute-start(bf16[8,128,128]{2,1,0:T(8,128)(2,1)S(1)} %get-tuple-element.17), channel_id=1, source_target_pairs={{0,3},{1,0},{2,1},{3,2},{4,7},{5,4},{6,5},{7,6},{8,11},{9,8},{10,9... | collective-permute-start | bytes 786440 | tf_op jit(solution)/shard_map/ppermute | solution.py:130
  48.7 3.1 %collective-permute-start.2 = (bf16[8,128,128]{2,1,0:T(8,128)(2,1)S(1)}, bf16[8,128,128]{2,1,0:T(8,128)(2,1)S(1)}, u32[]{:S(2)}, u32[]{:S(2)}) collective-permute-start(bf16[8,128,128]{2,1,0:T(8,128)(2,1)S(1)} %get-tuple-element.16), channel_id=1, source_target_pairs={{0,2},{1,3},{2,0},{3,1},{4,6},{5,7},{6,4},{7,5},{8,10},{9,11},{10,... | collective-permute-start | bytes 786440 | tf_op jit(solution)/shard_map/ppermute | solution.py:130
  56.0 10.8 %all-to-all-start.2 = ((bf16[8,128,128]{2,1,0:T(8,128)(2,1)}), bf16[8,128,128]{2,1,0:T(8,128)(2,1)S(1)}, u32[]{:S(2)}, u32[]{:S(2)}) async-start(bf16[8,128,128]{2,1,0:T(8,128)(2,1)} %add_convert_fusion.1), calls=%async_computation.2 | async-start | bytes 524288 | tf_op jit(solution)/shard_map/all_to_all | solution.py:131
  67.7 9.7 %all-to-all-done.2 = bf16[8,128,128]{2,1,0:T(8,128)(2,1)S(1)} async-done(((bf16[8,128,128]{2,1,0:T(8,128)(2,1)}), bf16[8,128,128]{2,1,0:T(8,128)(2,1)S(1)}, u32[]{:S(2)}, u32[]{:S(2)}) %all-to-all-start.2) | async-done | bytes 262176 | tf_op jit(solution)/shard_map/all_to_all | solution.py:131
  77.3 3.4 %all-to-all-start.1 = ((bf16[8,128,128]{2,1,0:T(8,128)(2,1)}), bf16[8,128,128]{2,1,0:T(8,128)(2,1)S(1)}, u32[]{:S(2)}, u32[]{:S(2)}) async-start(bf16[8,128,128]{2,1,0:T(8,128)(2,1)} %add_convert_fusion.2), calls=%async_computation.1 | async-start | bytes 524288 | tf_op jit(solution)/shard_map/all_to_all | solution.py:131
  80.8 9.3 %all-to-all-done.1 = bf16[8,128,128]{2,1,0:T(8,128)(2,1)S(1)} async-done(((bf16[8,128,128]{2,1,0:T(8,128)(2,1)}), bf16[8,128,128]{2,1,0:T(8,128)(2,1)S(1)}, u32[]{:S(2)}, u32[]{:S(2)}) %all-to-all-start.1) | async-done | bytes 262176 | tf_op jit(solution)/shard_map/all_to_all | solution.py:131
  92.8 3.5 %all-to-all-start.3 = ((bf16[8,128,256]{2,1,0:T(8,128)(2,1)}), bf16[8,128,256]{2,1,0:T(8,128)(2,1)S(1)}, u32[]{:S(2)}, u32[]{:S(2)}) async-start(bf16[8,128,256]{2,1,0:T(8,128)(2,1)} %broadcast_in_dim.13), calls=%async_computation.3 | async-start | bytes 1048576 | tf_op jit(solution)/shard_map/all_to_all | solution.py:146
  97.5 12.9 %all-to-all-done.3.g0 = bf16[8,128,256]{2,1,0:T(8,128)(2,1)S(1)} async-done(((bf16[8,128,256]{2,1,0:T(8,128)(2,1)}), bf16[8,128,256]{2,1,0:T(8,128)(2,1)S(1)}, u32[]{:S(2)}, u32[]{:S(2)}) %all-to-all-start.3) | async-done | bytes 524320 | tf_op jit(solution)/shard_map/all_to_all | solution.py:146
  110.4 3.9 %all-to-all-start.5 = ((f32[32,8,384]{2,1,0:T(8,128)}), f32[32,8,384]{2,1,0:T(8,128)S(1)}, u32[]{:S(2)}, u32[]{:S(2)}) async-start(f32[32,8,384]{2,1,0:T(8,128)} %maximum_multiply_fusion), calls=%async_computation.5 | async-start | bytes 786432 | tf_op jit(solution)/shard_map/all_to_all | solution.py:159
  114.3 4.2 %collective-permute-start.7 = (bf16[8,128,256]{2,1,0:T(8,128)(2,1)S(1)}, bf16[8,128,256]{2,1,0:T(8,128)(2,1)S(1)}, u32[]{:S(2)}, u32[]{:S(2)}) collective-permute-start(bf16[8,128,256]{2,1,0:T(8,128)(2,1)S(1)} %all-to-all-done.3.g0), channel_id=1, source_target_pairs={{1,0},{2,1},{3,2},{0,3},{5,4},{6,5},{7,6},{4,7},{9,8},{10,9},{11,1... | collective-permute-start | bytes 1572872 | tf_op jit(solution)/shard_map/ppermute | solution.py:149
  118.5 2.5 %collective-permute-start.8 = (bf16[8,128,256]{2,1,0:T(8,128)(2,1)S(1)}, bf16[8,128,256]{2,1,0:T(8,128)(2,1)S(1)}, u32[]{:S(2)}, u32[]{:S(2)}) collective-permute-start(bf16[8,128,256]{2,1,0:T(8,128)(2,1)S(1)} %all-to-all-done.3.g0), channel_id=1, source_target_pairs={{2,0},{3,1},{0,2},{1,3},{6,4},{7,5},{4,6},{5,7},{10,8},{11,9},{8,1... | collective-permute-start | bytes 1572872 | tf_op jit(solution)/shard_map/ppermute | solution.py:149
  121.0 2.5 %collective-permute-start.9 = (bf16[8,128,256]{2,1,0:T(8,128)(2,1)S(1)}, bf16[8,128,256]{2,1,0:T(8,128)(2,1)S(1)}, u32[]{:S(2)}, u32[]{:S(2)}) collective-permute-start(bf16[8,128,256]{2,1,0:T(8,128)(2,1)S(1)} %all-to-all-done.3.g0), channel_id=1, source_target_pairs={{3,0},{0,1},{1,2},{2,3},{7,4},{4,5},{5,6},{6,7},{11,8},{8,9},{9,10... | collective-permute-start | bytes 1572872 | tf_op jit(solution)/shard_map/ppermute | solution.py:149
  123.5 2.7 %all-to-all-done.5 = f32[32,8,384]{2,1,0:T(8,128)S(1)} async-done(((f32[32,8,384]{2,1,0:T(8,128)}), f32[32,8,384]{2,1,0:T(8,128)S(1)}, u32[]{:S(2)}, u32[]{:S(2)}) %all-to-all-start.5) | async-done | bytes 393248 | tf_op jit(solution)/shard_map/all_to_all | solution.py:159
  126.9 9.1 %all-to-all-start.6 = ((f32[16,8,384]{2,1,0:T(8,128)}), f32[16,8,384]{2,1,0:T(8,128)}, u32[]{:S(2)}, u32[]{:S(2)}) async-start(f32[16,8,384]{2,1,0:T(8,128)} %broadcast_in_dim.16), calls=%async_computation.6 | async-start | bytes 393216 | tf_op jit(solution)/shard_map/all_to_all | solution.py:160
  136.1 12.7 %collective-permute-done.9.g3 = bf16[8,128,256]{2,1,0:T(8,128)(2,1)S(1)} collective-permute-done((bf16[8,128,256]{2,1,0:T(8,128)(2,1)S(1)}, bf16[8,128,256]{2,1,0:T(8,128)(2,1)S(1)}, u32[]{:S(2)}, u32[]{:S(2)}) %collective-permute-start.9) | collective-permute-done | bytes 524320 | tf_op jit(solution)/shard_map/ppermute | solution.py:149
  152.7 3.1 %collective-permute-start.10 = (bf16[8,128,256]{2,1,0:T(8,128)(2,1)}, bf16[8,128,256]{2,1,0:T(8,128)(2,1)S(1)}, u32[]{:S(2)}, u32[]{:S(2)}) collective-permute-start(bf16[8,128,256]{2,1,0:T(8,128)(2,1)} %get-tuple-element.23), channel_id=1, source_target_pairs={{0,32},{32,0},{1,33},{33,1},{2,34},{34,2},{3,35},{35,3},{4,36},{36... | collective-permute-start | bytes 1572872 | tf_op jit(solution)/shard_map/ppermute | solution.py:178
  157.5 6.0 %all-to-all-start.7 = ((f32[32,8,384]{2,1,0:T(8,128)}), f32[32,8,384]{2,1,0:T(8,128)S(1)}, u32[]{:S(2)}, u32[]{:S(2)}) async-start(f32[32,8,384]{2,1,0:T(8,128)} %broadcast_in_dim.17), calls=%async_computation.7 | async-start | bytes 786432 | tf_op jit(solution)/shard_map/all_to_all | solution.py:161
  164.5 13.5 %all-to-all-done.7 = f32[32,8,384]{2,1,0:T(8,128)S(1)} async-done(((f32[32,8,384]{2,1,0:T(8,128)}), f32[32,8,384]{2,1,0:T(8,128)S(1)}, u32[]{:S(2)}, u32[]{:S(2)}) %all-to-all-start.7) | async-done | bytes 393248 | tf_op jit(solution)/shard_map/all_to_all | solution.py:161
  178.0 3.5 %all-to-all-start.4 = ((bf16[8,128,256]{2,1,0:T(8,128)(2,1)}), bf16[8,128,256]{2,1,0:T(8,128)(2,1)S(1)}, u32[]{:S(2)}, u32[]{:S(2)}) async-start(bf16[8,128,256]{2,1,0:T(8,128)(2,1)} %add_convert_fusion), calls=%async_computation.4 | async-start | bytes 1048576 | tf_op jit(solution)/shard_map/all_to_all | solution.py:179
  182.9 14.4 %all-to-all-done.4 = bf16[8,128,256]{2,1,0:T(8,128)(2,1)S(1)} async-done(((bf16[8,128,256]{2,1,0:T(8,128)(2,1)}), bf16[8,128,256]{2,1,0:T(8,128)(2,1)S(1)}, u32[]{:S(2)}, u32[]{:S(2)}) %all-to-all-start.4) | async-done | bytes 524320 | tf_op jit(solution)/shard_map/all_to_all | solution.py:179
  (61 shorter events, 25.7 us)
Async XLA Ops:
  0.6 89.5 %copy-start = (bf16[256,256]{1,0:T(8,128)(2,1)S(1)}, bf16[256,256]{1,0:T(8,128)(2,1)}, u32[]{:S(2)}) copy-start(bf16[256,256]{1,0:T(8,128)(2,1)} %param.11) | copy-start | bytes 393220
  23.9 7.2 %collective-permute-start = (bf16[8,128,256]{2,1,0:T(8,128)(2,1)S(1)}, bf16[8,128,256]{2,1,0:T(8,128)(2,1)S(1)}, u32[]{:S(2)}, u32[]{:S(2)}) collective-permute-start(bf16[8,128,256]{2,1,0:T(8,128)(2,1)S(1)} %all_to_all.40), channel_id=1, source_target_pairs={{0,32},{32,0},{1,33},{33,1},{2,34},{34,2},{3,35},{35,3},{4,36},{36... | collective-permute-start | bytes 1572872 | tf_op jit(solution)/shard_map/ppermute | solution.py:113
  31.0 1.1 copy-start.1
  33.3 18.5 %collective-permute-start.6 = (bf16[8,128,128]{2,1,0:T(8,128)(2,1)S(1)}, bf16[8,128,128]{2,1,0:T(8,128)(2,1)S(1)}, u32[]{:S(2)}, u32[]{:S(2)}) collective-permute-start(bf16[8,128,128]{2,1,0:T(8,128)(2,1)S(1)} %get-tuple-element.21), channel_id=1, source_target_pairs={{0,3},{1,0},{2,1},{3,2},{4,7},{5,4},{6,5},{7,6},{8,11},{9,8},{10,9... | collective-permute-start | bytes 786440 | tf_op jit(solution)/shard_map/ppermute | solution.py:130
  37.7 16.0 %collective-permute-start.5 = (bf16[8,128,128]{2,1,0:T(8,128)(2,1)S(1)}, bf16[8,128,128]{2,1,0:T(8,128)(2,1)S(1)}, u32[]{:S(2)}, u32[]{:S(2)}) collective-permute-start(bf16[8,128,128]{2,1,0:T(8,128)(2,1)S(1)} %get-tuple-element.20), channel_id=1, source_target_pairs={{0,2},{1,3},{2,0},{3,1},{4,6},{5,7},{6,4},{7,5},{8,10},{9,11},{10,... | collective-permute-start | bytes 786440 | tf_op jit(solution)/shard_map/ppermute | solution.py:130
  41.0 14.2 %collective-permute-start.4 = (bf16[8,128,128]{2,1,0:T(8,128)(2,1)S(1)}, bf16[8,128,128]{2,1,0:T(8,128)(2,1)S(1)}, u32[]{:S(2)}, u32[]{:S(2)}) collective-permute-start(bf16[8,128,128]{2,1,0:T(8,128)(2,1)S(1)} %get-tuple-element.19), channel_id=1, source_target_pairs={{0,1},{1,2},{2,3},{3,0},{4,5},{5,6},{6,7},{7,4},{8,9},{9,10},{10,1... | collective-permute-start | bytes 786440 | tf_op jit(solution)/shard_map/ppermute | solution.py:130
  44.1 22.7 %collective-permute-start.3 = (bf16[8,128,128]{2,1,0:T(8,128)(2,1)S(1)}, bf16[8,128,128]{2,1,0:T(8,128)(2,1)S(1)}, u32[]{:S(2)}, u32[]{:S(2)}) collective-permute-start(bf16[8,128,128]{2,1,0:T(8,128)(2,1)S(1)} %get-tuple-element.17), channel_id=1, source_target_pairs={{0,3},{1,0},{2,1},{3,2},{4,7},{5,4},{6,5},{7,6},{8,11},{9,8},{10,9... | collective-permute-start | bytes 786440 | tf_op jit(solution)/shard_map/ppermute | solution.py:130
  48.7 18.1 %collective-permute-start.2 = (bf16[8,128,128]{2,1,0:T(8,128)(2,1)S(1)}, bf16[8,128,128]{2,1,0:T(8,128)(2,1)S(1)}, u32[]{:S(2)}, u32[]{:S(2)}) collective-permute-start(bf16[8,128,128]{2,1,0:T(8,128)(2,1)S(1)} %get-tuple-element.16), channel_id=1, source_target_pairs={{0,2},{1,3},{2,0},{3,1},{4,6},{5,7},{6,4},{7,5},{8,10},{9,11},{10,... | collective-permute-start | bytes 786440 | tf_op jit(solution)/shard_map/ppermute | solution.py:130
  51.8 15.0 %collective-permute-start.1 = (bf16[8,128,128]{2,1,0:T(8,128)(2,1)S(1)}, bf16[8,128,128]{2,1,0:T(8,128)(2,1)S(1)}, u32[]{:S(2)}, u32[]{:S(2)}) collective-permute-start(bf16[8,128,128]{2,1,0:T(8,128)(2,1)S(1)} %get-tuple-element.15), channel_id=1, source_target_pairs={{0,1},{1,2},{2,3},{3,0},{4,5},{5,6},{6,7},{7,4},{8,9},{9,10},{10,1... | collective-permute-start | bytes 786440 | tf_op jit(solution)/shard_map/ppermute | solution.py:130
  56.0 21.4 %all-to-all-start.2 = ((bf16[8,128,128]{2,1,0:T(8,128)(2,1)}), bf16[8,128,128]{2,1,0:T(8,128)(2,1)S(1)}, u32[]{:S(2)}, u32[]{:S(2)}) async-start(bf16[8,128,128]{2,1,0:T(8,128)(2,1)} %add_convert_fusion.1), calls=%async_computation.2 | async-start | bytes 524288 | tf_op jit(solution)/shard_map/all_to_all | solution.py:131
  77.3 12.8 %all-to-all-start.1 = ((bf16[8,128,128]{2,1,0:T(8,128)(2,1)}), bf16[8,128,128]{2,1,0:T(8,128)(2,1)S(1)}, u32[]{:S(2)}, u32[]{:S(2)}) async-start(bf16[8,128,128]{2,1,0:T(8,128)(2,1)} %add_convert_fusion.2), calls=%async_computation.1 | async-start | bytes 524288 | tf_op jit(solution)/shard_map/all_to_all | solution.py:131
  90.2 0.8 copy-start.7
  90.2 0.8 copy-start.8
  92.8 17.6 %all-to-all-start.3 = ((bf16[8,128,256]{2,1,0:T(8,128)(2,1)}), bf16[8,128,256]{2,1,0:T(8,128)(2,1)S(1)}, u32[]{:S(2)}, u32[]{:S(2)}) async-start(bf16[8,128,256]{2,1,0:T(8,128)(2,1)} %broadcast_in_dim.13), calls=%async_computation.3 | async-start | bytes 1048576 | tf_op jit(solution)/shard_map/all_to_all | solution.py:146
  110.4 15.8 %all-to-all-start.5 = ((f32[32,8,384]{2,1,0:T(8,128)}), f32[32,8,384]{2,1,0:T(8,128)S(1)}, u32[]{:S(2)}, u32[]{:S(2)}) async-start(f32[32,8,384]{2,1,0:T(8,128)} %maximum_multiply_fusion), calls=%async_computation.5 | async-start | bytes 786432 | tf_op jit(solution)/shard_map/all_to_all | solution.py:159
  114.3 21.8 %collective-permute-start.7 = (bf16[8,128,256]{2,1,0:T(8,128)(2,1)S(1)}, bf16[8,128,256]{2,1,0:T(8,128)(2,1)S(1)}, u32[]{:S(2)}, u32[]{:S(2)}) collective-permute-start(bf16[8,128,256]{2,1,0:T(8,128)(2,1)S(1)} %all-to-all-done.3.g0), channel_id=1, source_target_pairs={{1,0},{2,1},{3,2},{0,3},{5,4},{6,5},{7,6},{4,7},{9,8},{10,9},{11,1... | collective-permute-start | bytes 1572872 | tf_op jit(solution)/shard_map/ppermute | solution.py:149
  118.5 17.5 %collective-permute-start.8 = (bf16[8,128,256]{2,1,0:T(8,128)(2,1)S(1)}, bf16[8,128,256]{2,1,0:T(8,128)(2,1)S(1)}, u32[]{:S(2)}, u32[]{:S(2)}) collective-permute-start(bf16[8,128,256]{2,1,0:T(8,128)(2,1)S(1)} %all-to-all-done.3.g0), channel_id=1, source_target_pairs={{2,0},{3,1},{0,2},{1,3},{6,4},{7,5},{4,6},{5,7},{10,8},{11,9},{8,1... | collective-permute-start | bytes 1572872 | tf_op jit(solution)/shard_map/ppermute | solution.py:149
  121.0 27.7 %collective-permute-start.9 = (bf16[8,128,256]{2,1,0:T(8,128)(2,1)S(1)}, bf16[8,128,256]{2,1,0:T(8,128)(2,1)S(1)}, u32[]{:S(2)}, u32[]{:S(2)}) collective-permute-start(bf16[8,128,256]{2,1,0:T(8,128)(2,1)S(1)} %all-to-all-done.3.g0), channel_id=1, source_target_pairs={{3,0},{0,1},{1,2},{2,3},{7,4},{4,5},{5,6},{6,7},{11,8},{8,9},{9,10... | collective-permute-start | bytes 1572872 | tf_op jit(solution)/shard_map/ppermute | solution.py:149
  126.9 28.9 %all-to-all-start.6 = ((f32[16,8,384]{2,1,0:T(8,128)}), f32[16,8,384]{2,1,0:T(8,128)}, u32[]{:S(2)}, u32[]{:S(2)}) async-start(f32[16,8,384]{2,1,0:T(8,128)} %broadcast_in_dim.16), calls=%async_computation.6 | async-start | bytes 393216 | tf_op jit(solution)/shard_map/all_to_all | solution.py:160
  149.6 1.0 copy-start.3
  152.7 10.9 %collective-permute-start.10 = (bf16[8,128,256]{2,1,0:T(8,128)(2,1)}, bf16[8,128,256]{2,1,0:T(8,128)(2,1)S(1)}, u32[]{:S(2)}, u32[]{:S(2)}) collective-permute-start(bf16[8,128,256]{2,1,0:T(8,128)(2,1)} %get-tuple-element.23), channel_id=1, source_target_pairs={{0,32},{32,0},{1,33},{33,1},{2,34},{34,2},{3,35},{35,3},{4,36},{36... | collective-permute-start | bytes 1572872 | tf_op jit(solution)/shard_map/ppermute | solution.py:178
  157.5 20.5 %all-to-all-start.7 = ((f32[32,8,384]{2,1,0:T(8,128)}), f32[32,8,384]{2,1,0:T(8,128)S(1)}, u32[]{:S(2)}, u32[]{:S(2)}) async-start(f32[32,8,384]{2,1,0:T(8,128)} %broadcast_in_dim.17), calls=%async_computation.7 | async-start | bytes 786432 | tf_op jit(solution)/shard_map/all_to_all | solution.py:161
  178.0 19.3 %all-to-all-start.4 = ((bf16[8,128,256]{2,1,0:T(8,128)(2,1)}), bf16[8,128,256]{2,1,0:T(8,128)(2,1)S(1)}, u32[]{:S(2)}, u32[]{:S(2)}) async-start(bf16[8,128,256]{2,1,0:T(8,128)(2,1)} %add_convert_fusion), calls=%async_computation.4 | async-start | bytes 1048576 | tf_op jit(solution)/shard_map/all_to_all | solution.py:179
  182.9 14.5 %copy-start.4 = (f32[128]{0:T(128)S(1)}, f32[128]{0:T(128)}, u32[]{:S(2)}) copy-start(f32[128]{0:T(128)} %param.10) | copy-start | bytes 1540
  (3 other events, 2.1 us)

commit v3 on v2

--- a/solution.py
+++ b/solution.py
@@ -112,25 +112,20 @@
     own = lax.all_to_all(repeat(share, n_y), "y", 0, 0, tiled=True)
     other = lax.ppermute(own, "core", swap)
 
-    part = hidden // 2
-    sums = []
-    for h in range(2):
-        cut = slice(h * part, (h + 1) * part)
-        blocks = pl.pallas_call(
-            forward_kernel,
-            out_shape=(jax.ShapeDtypeStruct((n_z, n, part), BF16),) * n_x,
-            in_specs=[SMEM, VMEM, VMEM, VMEM],
-            out_specs=(VMEM,) * n_x,
-            scratch_shapes=[pltpu.VMEM((tile_rows, n, part), F32)],
-            compiler_params=pltpu.CompilerParams(vmem_limit_bytes=40 * 2**20),
-            name="forward_tiles",
-        )(info, tiles, own[:, :, cut], other[:, :, cut])
-        over_x = blocks[0].astype(F32)
-        for d in range(1, n_x):
-            over_x += lax.ppermute(blocks[d], "x", ring(n_x, d)).astype(F32)
-        terms = lax.all_to_all(over_x.astype(BF16), "z", 0, 0, tiled=True)
-        sums.append(jnp.sum(terms.astype(F32), axis=0))
-    mixed = jnp.concatenate(sums, axis=1)
+    blocks = pl.pallas_call(
+        forward_kernel,
+        out_shape=(jax.ShapeDtypeStruct((n_z, n, hidden), BF16),) * n_x,
+        in_specs=[SMEM, VMEM, VMEM, VMEM],
+        out_specs=(VMEM,) * n_x,
+        scratch_shapes=[pltpu.VMEM((tile_rows, n, hidden), F32)],
+        compiler_params=pltpu.CompilerParams(vmem_limit_bytes=40 * 2**20),
+        name="forward_tiles",
+    )(info, tiles, own, other)
+    over_x = blocks[0].astype(F32)
+    for d in range(1, n_x):
+        over_x += lax.ppermute(blocks[d], "x", ring(n_x, d)).astype(F32)
+    terms = lax.all_to_all(over_x.astype(BF16), "z", 0, 0, tiled=True)
+    mixed = jnp.sum(terms.astype(F32), axis=0)
 
     high = mixed.astype(BF16)
     low = (mixed - high.astype(F32)).astype(BF16)
@@ -143,25 +138,37 @@
     grad_pre = cotangent.astype(F32) * (sigma * (1.0 + pre * (1.0 - sigma)))
     grad_here = (grad_pre * row_norm[:, None]).astype(BF16)
 
+    weight_part = lax.dot_general(
+        high, grad_here, (((0,), (0,)), ((), ())), preferred_element_type=F32
+    )
+    bias_part = jnp.sum(grad_pre, axis=0)
+    chunk = hidden // tile_cols
+    both = jnp.concatenate(
+        [
+            (weight_part * scale).reshape(tile_cols, chunk, hidden),
+            jnp.broadcast_to(bias_part * scale, (tile_cols, 8, hidden)),
+        ],
+        axis=1,
+    ).astype(BF16)
     g0 = lax.all_to_all(repeat(grad_here, n_z), "z", 0, 0, tiled=True)
+    g0, both = lax.optimization_barrier((g0, both))
     g = [g0]
     for d in range(1, n_x):
         g.append(lax.ppermute(g0, "x", [((i + d) % n_x, i) for i in range(n_x)]))
-
-    weight_part = lax.dot_general(
-        high, grad_here, (((0,), (0,)), ((), ())), preferred_element_type=F32
-    )
-    bias_part = jnp.sum(grad_pre, axis=0)
-    both = jnp.concatenate(
-        [weight_part, jnp.broadcast_to(bias_part[:, None], (hidden, 128))], axis=1
-    )
-    both = (both * scale).reshape(tile_rows, hidden // tile_rows, hidden + 128)
-    both = jnp.sum(lax.all_to_all(both, COL, 0, 0, tiled=True), axis=0)
-    both = jnp.sum(lax.all_to_all(repeat(both, tile_cols), ROW, 0, 0, tiled=True), axis=0)
-    both = lax.all_to_all(repeat(both, tile_rows), COL, 0, 0, tiled=True)
-    both = both.reshape(hidden, hidden + 128)
-    grad_weight = both[:, :hidden]
-    grad_bias = both[:, hidden]
+    both = jnp.sum(lax.all_to_all(both, ROW, 0, 0, tiled=True).astype(F32), axis=0)
+    both = lax.all_to_all(repeat(both.astype(BF16), tile_rows), COL, 0, 0, tiled=True)
+    both = jnp.sum(both.astype(F32), axis=0)
+    grad_bias = both[chunk]
+    chunk_here = both[:chunk].astype(BF16)
+    chunk_other = lax.ppermute(chunk_here, "core", swap)
+    first = lax.axis_index("core") == 0
+    chunks = jnp.concatenate(
+        [
+            jnp.where(first, chunk_here, chunk_other),
+            jnp.where(first, chunk_other, chunk_here),
+        ],
+        axis=0,
+    )
 
     keep, send = pl.pallas_call(
         backward_kernel,
@@ -176,7 +183,10 @@
         name="backward_tiles",
     )(info, tiles, *g)
     pair = (keep + lax.ppermute(send, "core", swap).astype(F32)).astype(BF16)
-    column_total = jnp.sum(lax.all_to_all(pair, "y", 0, 0, tiled=True).astype(F32), axis=0)
+    last = jnp.concatenate([pair, repeat(chunks, n_y)], axis=1)
+    last = lax.all_to_all(last, "y", 0, 0, tiled=True)
+    column_total = jnp.sum(last[:, :n].astype(F32), axis=0)
+    grad_weight = last[:, n:].reshape(hidden, hidden).astype(F32)
     grad_mixed = (col_norm[:, None] * column_total).astype(BF16)
     grad_features = lax.dot_general(
         grad_mixed, weight, (((1,), (1,)), ((), ())), preferred_element_type=F32

time: 200 us -> 195 us (0.975)
  blocking collectives: 22.2 us -> 48.7 us
  starting transfers between devices: 77.3 us -> 54.5 us
  local copies, waits for them, and re-layouts: 8.42 us -> 4.22 us
  waiting for transfers between devices: 76.6 us -> 73.3 us
    all_to_all x6 -> x3, waiting for transfers between devices: 49.6 us -> 20.2 us  [the longest x1 20.2 us: body(): last = lax.all_to_all(last, 'y', 0, 0, tiled=True)]
    all_to_all x0 -> x1, blocking collectives: none -> 26.5 us  [body(): terms = lax.all_to_all(over_x.astype(BF16), 'z', 0, 0, tiled=True)]
    all_to_all x6 -> x3, starting transfers between devices: 36.8 us -> 17.5 us  [the longest x1 7.23 us: body(): lax.all_to_all(both, ROW, 0, 0, tiled=True).astype(F32)]
    ppermute x6 -> x3, waiting for transfers between devices: 1.38 us -> 19.6 us  [body(): over_x += lax.ppermute(blocks[d], 'x', ring(n_x, d)).astype(F32)]
    ppermute x6 -> x3, starting transfers between devices: 19.2 us -> 10.5 us  [body(): over_x += lax.ppermute(blocks[d], 'x', ring(n_x, d)).astype(F32)]
    ppermute x3, waiting for transfers between devices: 12.7 us -> 18.2 us  [body(): g.append(lax.ppermute(g0, 'x', [((i + d) % n_x, i) for i in range(n_x)]))]
    unnamed x18, local copies, waits for them, and re-layouts: 4.18 us -> 1.88 us
    ppermute x3, starting transfers between devices: 9.21 us -> 11.3 us  [body(): g.append(lax.ppermute(g0, 'x', [((i + d) % n_x, i) for i in range(n_x)]))]
  transfers between devices with their start and end apart: 18 -> 13, of which waited for: 8 -> 10; matrix products, arithmetic and copies ran while one was open for 4% -> 2% of each run, Pallas kernels for 2% -> 1%
where the time goes in v3:
time: 195 us; the launch traced here: 193 us
  waiting for transfers between devices  73.3 us (38%)
  starting transfers between devices  54.5 us (28%)
  blocking collectives  48.7 us (25%)
  other arithmetic  5.07 us (3%)
  local copies, waits for them, and re-layouts  4.22 us (2%)
  Pallas kernels  3.58 us (2%)
  matrix products  2.07 us (1%)
    all_to_all x1, blocking collectives, body(): terms = lax.all_to_all(over_x.astype(BF16), 'z', 0, 0, tiled=True)  26.5 us
    all_to_all x1, blocking collectives, body(): own = lax.all_to_all(repeat(share, n_y), 'y', 0, 0, tiled=True)  22.2 us
    all_to_all x1, waiting for transfers between devices, body(): last = lax.all_to_all(last, 'y', 0, 0, tiled=True)  20.2 us
    ppermute x3, waiting for transfers between devices, body(): over_x += lax.ppermute(blocks[d], 'x', ring(n_x, d)).astype(F32)  19.6 us
    ppermute x3, waiting for transfers between devices, body(): g.append(lax.ppermute(g0, 'x', [((i + d) % n_x, i) for i in range(n_x)]))  18.2 us
    all_to_all x1, waiting for transfers between devices, body(): g0 = lax.all_to_all(repeat(grad_here, n_z), 'z', 0, 0, tiled=True)  13.5 us
    ppermute x3, starting transfers between devices, body(): g.append(lax.ppermute(g0, 'x', [((i + d) % n_x, i) for i in range(n_x)]))  11.3 us
    ppermute x3, starting transfers between devices, body(): over_x += lax.ppermute(blocks[d], 'x', ring(n_x, d)).astype(F32)  10.5 us
  transfers between devices with their start and end apart: 13, of which 10 were waited for; matrix products, arithmetic and copies ran while one was open for 2% of the time, Pallas kernels for 1%

profile of v3, /device:TPU:1, one launch (start us, length us, event | category | flops | bytes accessed | tf_op | source)
XLA Modules:
  0.0 193.0 jit_solution(8803407118210014850)
XLA Ops:
  1.7 22.2 %all_to_all.30.own = bf16[8,128,256]{2,1,0:T(8,128)(2,1)S(1)} all-to-all(bf16[8,128,256]{2,1,0:T(8,128)(2,1)S(1)} %broadcast_in_dim.10), channel_id=1, replica_groups=mesh['y'=8,'core'=2,'z'=8,'x'=4] {'y'}, dimensions={0} | all-to-all | bytes 1048576 | tf_op jit(solution)/shard_map/all_to_all | solution.py:112
  23.9 5.6 %collective-permute-start = (bf16[8,128,256]{2,1,0:T(8,128)(2,1)S(1)}, bf16[8,128,256]{2,1,0:T(8,128)(2,1)S(1)}, u32[]{:S(2)}, u32[]{:S(2)}) collective-permute-start(bf16[8,128,256]{2,1,0:T(8,128)(2,1)S(1)} %all_to_all.30.own), channel_id=1, source_target_pairs={{0,32},{32,0},{1,33},{33,1},{2,34},{34,2},{3,35},{35,3},{4,36},{36... | collective-permute-start | bytes 1572872 | tf_op jit(solution)/shard_map/ppermute | solution.py:113
  31.0 1.5 forward_tiles.1
  32.5 3.4 %collective-permute-start.1 = (bf16[8,128,256]{2,1,0:T(8,128)(2,1)S(1)}, bf16[8,128,256]{2,1,0:T(8,128)(2,1)S(1)}, u32[]{:S(2)}, u32[]{:S(2)}) collective-permute-start(bf16[8,128,256]{2,1,0:T(8,128)(2,1)S(1)} %get-tuple-element.13), channel_id=1, source_target_pairs={{0,1},{1,2},{2,3},{3,0},{4,5},{5,6},{6,7},{7,4},{8,9},{9,10},{10,1... | collective-permute-start | bytes 1572872 | tf_op jit(solution)/shard_map/ppermute | solution.py:126
  35.9 4.8 %collective-permute-start.2 = (bf16[8,128,256]{2,1,0:T(8,128)(2,1)S(1)}, bf16[8,128,256]{2,1,0:T(8,128)(2,1)S(1)}, u32[]{:S(2)}, u32[]{:S(2)}) collective-permute-start(bf16[8,128,256]{2,1,0:T(8,128)(2,1)S(1)} %get-tuple-element.14), channel_id=1, source_target_pairs={{0,2},{1,3},{2,0},{3,1},{4,6},{5,7},{6,4},{7,5},{8,10},{9,11},{10,... | collective-permute-start | bytes 1572872 | tf_op jit(solution)/shard_map/ppermute | solution.py:126
  40.8 2.3 %collective-permute-start.3 = (bf16[8,128,256]{2,1,0:T(8,128)(2,1)S(1)}, bf16[8,128,256]{2,1,0:T(8,128)(2,1)S(1)}, u32[]{:S(2)}, u32[]{:S(2)}) collective-permute-start(bf16[8,128,256]{2,1,0:T(8,128)(2,1)S(1)} %get-tuple-element.15), channel_id=1, source_target_pairs={{0,3},{1,0},{2,1},{3,2},{4,7},{5,4},{6,5},{7,6},{8,11},{9,8},{10,9... | collective-permute-start | bytes 1572872 | tf_op jit(solution)/shard_map/ppermute | solution.py:126
  43.1 5.7 %collective-permute-done.1 = bf16[8,128,256]{2,1,0:T(8,128)(2,1)S(1)} collective-permute-done((bf16[8,128,256]{2,1,0:T(8,128)(2,1)S(1)}, bf16[8,128,256]{2,1,0:T(8,128)(2,1)S(1)}, u32[]{:S(2)}, u32[]{:S(2)}) %collective-permute-start.1) | collective-permute-done | bytes 524320 | tf_op jit(solution)/shard_map/ppermute | solution.py:126
  48.8 12.9 %collective-permute-done.2 = bf16[8,128,256]{2,1,0:T(8,128)(2,1)S(1)} collective-permute-done((bf16[8,128,256]{2,1,0:T(8,128)(2,1)S(1)}, bf16[8,128,256]{2,1,0:T(8,128)(2,1)S(1)}, u32[]{:S(2)}, u32[]{:S(2)}) %collective-permute-start.2) | collective-permute-done | bytes 524320 | tf_op jit(solution)/shard_map/ppermute | solution.py:126
  63.1 26.5 %all_to_all.31 = bf16[8,128,256]{2,1,0:T(8,128)(2,1)S(1)} all-to-all(bf16[8,128,256]{2,1,0:T(8,128)(2,1)S(1)} %add_convert_fusion.1), channel_id=1, replica_groups=mesh['y'=8,'core'=2,'z'=8,'x'=4] {'z'}, dimensions={0} | all-to-all | bytes 1048576 | tf_op jit(solution)/shard_map/all_to_all | solution.py:127
  91.6 3.5 %all-to-all-start.2 = ((bf16[8,128,256]{2,1,0:T(8,128)(2,1)}), bf16[8,128,256]{2,1,0:T(8,128)(2,1)S(1)}, u32[]{:S(2)}, u32[]{:S(2)}) async-start(bf16[8,128,256]{2,1,0:T(8,128)(2,1)} %broadcast_in_dim.11), calls=%async_computation.2 | async-start | bytes 1048576 | tf_op jit(solution)/shard_map/all_to_all | solution.py:153
  96.1 13.5 %all-to-all-done.2.g0 = bf16[8,128,256]{2,1,0:T(8,128)(2,1)S(1)} async-done(((bf16[8,128,256]{2,1,0:T(8,128)(2,1)}), bf16[8,128,256]{2,1,0:T(8,128)(2,1)S(1)}, u32[]{:S(2)}, u32[]{:S(2)}) %all-to-all-start.2) | async-done | bytes 524320 | tf_op jit(solution)/shard_map/all_to_all | solution.py:153
  109.6 7.2 %all-to-all-start.3 = ((bf16[16,24,256]{2,1,0:T(8,128)(2,1)}), bf16[16,24,256]{2,1,0:T(8,128)(2,1)S(1)}, u32[]{:S(2)}, u32[]{:S(2)}) async-start(bf16[16,24,256]{2,1,0:T(8,128)(2,1)} %pad_maximum_fusion.1), calls=%async_computation.3 | async-start | bytes 393216 | tf_op jit(solution)/shard_map/all_to_all | solution.py:158
  116.8 5.0 %collective-permute-start.6 = (bf16[8,128,256]{2,1,0:T(8,128)(2,1)S(1)}, bf16[8,128,256]{2,1,0:T(8,128)(2,1)S(1)}, u32[]{:S(2)}, u32[]{:S(2)}) collective-permute-start(bf16[8,128,256]{2,1,0:T(8,128)(2,1)S(1)} %all-to-all-done.2.g0), channel_id=1, source_target_pairs={{3,0},{0,1},{1,2},{2,3},{7,4},{4,5},{5,6},{6,7},{11,8},{8,9},{9,10... | collective-permute-start | bytes 1572872 | tf_op jit(solution)/shard_map/ppermute | solution.py:157
  121.9 3.6 %collective-permute-start.5 = (bf16[8,128,256]{2,1,0:T(8,128)(2,1)S(1)}, bf16[8,128,256]{2,1,0:T(8,128)(2,1)S(1)}, u32[]{:S(2)}, u32[]{:S(2)}) collective-permute-start(bf16[8,128,256]{2,1,0:T(8,128)(2,1)S(1)} %all-to-all-done.2.g0), channel_id=1, source_target_pairs={{2,0},{3,1},{0,2},{1,3},{6,4},{7,5},{4,6},{5,7},{10,8},{11,9},{8,1... | collective-permute-start | bytes 1572872 | tf_op jit(solution)/shard_map/ppermute | solution.py:157
  125.4 2.7 %collective-permute-start.4 = (bf16[8,128,256]{2,1,0:T(8,128)(2,1)S(1)}, bf16[8,128,256]{2,1,0:T(8,128)(2,1)S(1)}, u32[]{:S(2)}, u32[]{:S(2)}) collective-permute-start(bf16[8,128,256]{2,1,0:T(8,128)(2,1)S(1)} %all-to-all-done.2.g0), channel_id=1, source_target_pairs={{1,0},{2,1},{3,2},{0,3},{5,4},{6,5},{7,6},{4,7},{9,8},{10,9},{11,1... | collective-permute-start | bytes 1572872 | tf_op jit(solution)/shard_map/ppermute | solution.py:157
  128.9 4.6 %all-to-all-start.4 = ((bf16[32,24,256]{2,1,0:T(8,128)(2,1)}), bf16[32,24,256]{2,1,0:T(8,128)(2,1)}, u32[]{:S(2)}, u32[]{:S(2)}) async-start(bf16[32,24,256]{2,1,0:T(8,128)(2,1)} %broadcast_in_dim.13), calls=%async_computation.4 | async-start | bytes 786432 | tf_op jit(solution)/shard_map/all_to_all | solution.py:159
  134.5 16.1 %collective-permute-done.5.g2 = bf16[8,128,256]{2,1,0:T(8,128)(2,1)S(1)} collective-permute-done((bf16[8,128,256]{2,1,0:T(8,128)(2,1)S(1)}, bf16[8,128,256]{2,1,0:T(8,128)(2,1)S(1)}, u32[]{:S(2)}, u32[]{:S(2)}) %collective-permute-start.5) | collective-permute-done | bytes 524320 | tf_op jit(solution)/shard_map/ppermute | solution.py:157
  150.5 1.2 collective-permute-done.4.g1
  153.5 2.1 %backward_tiles.1 = (f32[8,128,256]{2,1,0:T(8,128)S(1)}, bf16[8,128,256]{2,1,0:T(8,128)(2,1)}) custom-call(s32[51]{0:T(128)S(1)} %concatenate.13.info, bf16[24,128,128]{2,1,0:T(8,128)(2,1)S(1)} %bitcast.20, bf16[8,128,256]{2,1,0:T(8,128)(2,1)S(1)} %all-to-all-done.2.g0, bf16[8,128,256]{2,1,0:T(8,128)(2,1)S(1)} %copy-done.3, ...), custom_call_target="tpu_custom_call" | custom-call | tf_op jit(solution)/shard_map/backward_tiles/pallas_call | solution.py:173
  155.6 4.2 %collective-permute-start.7 = (bf16[8,128,256]{2,1,0:T(8,128)(2,1)}, bf16[8,128,256]{2,1,0:T(8,128)(2,1)S(1)}, u32[]{:S(2)}, u32[]{:S(2)}) collective-permute-start(bf16[8,128,256]{2,1,0:T(8,128)(2,1)} %get-tuple-element.18), channel_id=1, source_target_pairs={{0,32},{32,0},{1,33},{33,1},{2,34},{34,2},{3,35},{35,3},{4,36},{36... | collective-permute-start | bytes 1572872 | tf_op jit(solution)/shard_map/ppermute | solution.py:185
  159.9 1.1 convert_reduce_fusion.2
  160.9 1.9 collective-permute-start.8
  164.9 5.6 %all-to-all-start.5 = ((bf16[8,160,256]{2,1,0:T(8,128)(2,1)}), bf16[8,160,256]{2,1,0:T(8,128)(2,1)S(1)}, u32[]{:S(2)}, u32[]{:S(2)}) async-start(bf16[8,160,256]{2,1,0:T(8,128)(2,1)} %pad_maximum_fusion), calls=%async_computation.5 | async-start | bytes 1310720 | tf_op jit(solution)/shard_map/all_to_all | solution.py:187
  171.1 20.2 %all-to-all-done.5 = bf16[8,160,256]{2,1,0:T(8,128)(2,1)S(1)} async-done(((bf16[8,160,256]{2,1,0:T(8,128)(2,1)}), bf16[8,160,256]{2,1,0:T(8,128)(2,1)S(1)}, u32[]{:S(2)}, u32[]{:S(2)}) %all-to-all-start.5) | async-done | bytes 655392 | tf_op jit(solution)/shard_map/all_to_all | solution.py:187
  (52 shorter events, 14.0 us)
Async XLA Ops:
  0.6 89.0 %copy-start = (bf16[256,256]{1,0:T(8,128)(2,1)S(1)}, bf16[256,256]{1,0:T(8,128)(2,1)}, u32[]{:S(2)}) copy-start(bf16[256,256]{1,0:T(8,128)(2,1)} %param.11) | copy-start | bytes 393220
  0.6 29.5 %copy-start.5 = (s32[1,1,24,2]{2,3,1,0:T(2,128)S(1)}, s32[1,1,24,2]{2,3,1,0:T(2,128)}, u32[]{:S(2)}) copy-start(s32[1,1,24,2]{2,3,1,0:T(2,128)} %param.13) | copy-start | bytes 580
  0.7 30.4 %copy-start.1 = (bf16[1,1,24,128,128]{4,3,2,1,0:T(8,128)(2,1)S(1)}, bf16[1,1,24,128,128]{4,3,2,1,0:T(8,128)(2,1)}, u32[]{:S(2)}) copy-start(bf16[1,1,24,128,128]{4,3,2,1,0:T(8,128)(2,1)} %param.15) | copy-start | bytes 2359300
  23.9 7.1 %collective-permute-start = (bf16[8,128,256]{2,1,0:T(8,128)(2,1)S(1)}, bf16[8,128,256]{2,1,0:T(8,128)(2,1)S(1)}, u32[]{:S(2)}, u32[]{:S(2)}) collective-permute-start(bf16[8,128,256]{2,1,0:T(8,128)(2,1)S(1)} %all_to_all.30.own), channel_id=1, source_target_pairs={{0,32},{32,0},{1,33},{33,1},{2,34},{34,2},{3,35},{35,3},{4,36},{36... | collective-permute-start | bytes 1572872 | tf_op jit(solution)/shard_map/ppermute | solution.py:113
  32.5 16.3 %collective-permute-start.1 = (bf16[8,128,256]{2,1,0:T(8,128)(2,1)S(1)}, bf16[8,128,256]{2,1,0:T(8,128)(2,1)S(1)}, u32[]{:S(2)}, u32[]{:S(2)}) collective-permute-start(bf16[8,128,256]{2,1,0:T(8,128)(2,1)S(1)} %get-tuple-element.13), channel_id=1, source_target_pairs={{0,1},{1,2},{2,3},{3,0},{4,5},{5,6},{6,7},{7,4},{8,9},{9,10},{10,1... | collective-permute-start | bytes 1572872 | tf_op jit(solution)/shard_map/ppermute | solution.py:126
  35.9 25.8 %collective-permute-start.2 = (bf16[8,128,256]{2,1,0:T(8,128)(2,1)S(1)}, bf16[8,128,256]{2,1,0:T(8,128)(2,1)S(1)}, u32[]{:S(2)}, u32[]{:S(2)}) collective-permute-start(bf16[8,128,256]{2,1,0:T(8,128)(2,1)S(1)} %get-tuple-element.14), channel_id=1, source_target_pairs={{0,2},{1,3},{2,0},{3,1},{4,6},{5,7},{6,4},{7,5},{8,10},{9,11},{10,... | collective-permute-start | bytes 1572872 | tf_op jit(solution)/shard_map/ppermute | solution.py:126
  40.8 22.0 %collective-permute-start.3 = (bf16[8,128,256]{2,1,0:T(8,128)(2,1)S(1)}, bf16[8,128,256]{2,1,0:T(8,128)(2,1)S(1)}, u32[]{:S(2)}, u32[]{:S(2)}) collective-permute-start(bf16[8,128,256]{2,1,0:T(8,128)(2,1)S(1)} %get-tuple-element.15), channel_id=1, source_target_pairs={{0,3},{1,0},{2,1},{3,2},{4,7},{5,4},{6,5},{7,6},{8,11},{9,8},{10,9... | collective-permute-start | bytes 1572872 | tf_op jit(solution)/shard_map/ppermute | solution.py:126
  63.0 26.8 %copy-start.6 = (f32[128]{0:T(128)S(1)}, f32[128]{0:T(128)}, u32[]{:S(2)}) copy-start(f32[128]{0:T(128)} %param.16) | copy-start | bytes 1540
  63.0 26.8 %copy-start.7 = (bf16[128,256]{1,0:T(8,128)(2,1)S(1)}, bf16[128,256]{1,0:T(8,128)(2,1)}, u32[]{:S(2)}) copy-start(bf16[128,256]{1,0:T(8,128)(2,1)} %param.17) | copy-start | bytes 196612
  63.1 26.8 %copy-start.8 = (f32[256]{0:T(256)S(1)}, f32[256]{0:T(256)}, u32[]{:S(2)}) copy-start(f32[256]{0:T(256)} %param.12) | copy-start | bytes 3076
  91.6 17.9 %all-to-all-start.2 = ((bf16[8,128,256]{2,1,0:T(8,128)(2,1)}), bf16[8,128,256]{2,1,0:T(8,128)(2,1)S(1)}, u32[]{:S(2)}, u32[]{:S(2)}) async-start(bf16[8,128,256]{2,1,0:T(8,128)(2,1)} %broadcast_in_dim.11), calls=%async_computation.2 | async-start | bytes 1048576 | tf_op jit(solution)/shard_map/all_to_all | solution.py:153
  109.6 18.5 %all-to-all-start.3 = ((bf16[16,24,256]{2,1,0:T(8,128)(2,1)}), bf16[16,24,256]{2,1,0:T(8,128)(2,1)S(1)}, u32[]{:S(2)}, u32[]{:S(2)}) async-start(bf16[16,24,256]{2,1,0:T(8,128)(2,1)} %pad_maximum_fusion.1), calls=%async_computation.3 | async-start | bytes 393216 | tf_op jit(solution)/shard_map/all_to_all | solution.py:158
  116.8 17.6 %collective-permute-start.6 = (bf16[8,128,256]{2,1,0:T(8,128)(2,1)S(1)}, bf16[8,128,256]{2,1,0:T(8,128)(2,1)S(1)}, u32[]{:S(2)}, u32[]{:S(2)}) collective-permute-start(bf16[8,128,256]{2,1,0:T(8,128)(2,1)S(1)} %all-to-all-done.2.g0), channel_id=1, source_target_pairs={{3,0},{0,1},{1,2},{2,3},{7,4},{4,5},{5,6},{6,7},{11,8},{8,9},{9,10... | collective-permute-start | bytes 1572872 | tf_op jit(solution)/shard_map/ppermute | solution.py:157
  121.9 28.7 %collective-permute-start.5 = (bf16[8,128,256]{2,1,0:T(8,128)(2,1)S(1)}, bf16[8,128,256]{2,1,0:T(8,128)(2,1)S(1)}, u32[]{:S(2)}, u32[]{:S(2)}) collective-permute-start(bf16[8,128,256]{2,1,0:T(8,128)(2,1)S(1)} %all-to-all-done.2.g0), channel_id=1, source_target_pairs={{2,0},{3,1},{0,2},{1,3},{6,4},{7,5},{4,6},{5,7},{10,8},{11,9},{8,1... | collective-permute-start | bytes 1572872 | tf_op jit(solution)/shard_map/ppermute | solution.py:157
  125.4 26.3 %collective-permute-start.4 = (bf16[8,128,256]{2,1,0:T(8,128)(2,1)S(1)}, bf16[8,128,256]{2,1,0:T(8,128)(2,1)S(1)}, u32[]{:S(2)}, u32[]{:S(2)}) collective-permute-start(bf16[8,128,256]{2,1,0:T(8,128)(2,1)S(1)} %all-to-all-done.2.g0), channel_id=1, source_target_pairs={{1,0},{2,1},{3,2},{0,3},{5,4},{6,5},{7,6},{4,7},{9,8},{10,9},{11,1... | collective-permute-start | bytes 1572872 | tf_op jit(solution)/shard_map/ppermute | solution.py:157
  128.9 30.9 %all-to-all-start.4 = ((bf16[32,24,256]{2,1,0:T(8,128)(2,1)}), bf16[32,24,256]{2,1,0:T(8,128)(2,1)}, u32[]{:S(2)}, u32[]{:S(2)}) async-start(bf16[32,24,256]{2,1,0:T(8,128)(2,1)} %broadcast_in_dim.13), calls=%async_computation.4 | async-start | bytes 786432 | tf_op jit(solution)/shard_map/all_to_all | solution.py:159
  151.7 0.8 copy-start.2
  152.5 1.0 copy-start.3
  155.6 7.3 %collective-permute-start.7 = (bf16[8,128,256]{2,1,0:T(8,128)(2,1)}, bf16[8,128,256]{2,1,0:T(8,128)(2,1)S(1)}, u32[]{:S(2)}, u32[]{:S(2)}) collective-permute-start(bf16[8,128,256]{2,1,0:T(8,128)(2,1)} %get-tuple-element.18), channel_id=1, source_target_pairs={{0,32},{32,0},{1,33},{33,1},{2,34},{34,2},{3,35},{35,3},{4,36},{36... | collective-permute-start | bytes 1572872 | tf_op jit(solution)/shard_map/ppermute | solution.py:185
  160.9 3.1 %collective-permute-start.8 = (bf16[16,256]{1,0:T(8,128)(2,1)S(1)}, bf16[16,256]{1,0:T(8,128)(2,1)S(1)}, u32[]{:S(2)}, u32[]{:S(2)}) collective-permute-start(bf16[16,256]{1,0:T(8,128)(2,1)S(1)} %slice.33), channel_id=1, source_target_pairs={{0,32},{32,0},{1,33},{33,1},{2,34},{34,2},{3,35},{35,3},{4,36},{36... | collective-permute-start | bytes 24584 | tf_op jit(solution)/shard_map/ppermute | solution.py:163
  164.9 26.5 %copy-start.4 = (f32[128]{0:T(128)S(1)}, f32[128]{0:T(128)}, u32[]{:S(2)}) copy-start(f32[128]{0:T(128)} %param.10) | copy-start | bytes 1540
  164.9 26.4 %all-to-all-start.5 = ((bf16[8,160,256]{2,1,0:T(8,128)(2,1)}), bf16[8,160,256]{2,1,0:T(8,128)(2,1)S(1)}, u32[]{:S(2)}, u32[]{:S(2)}) async-start(bf16[8,160,256]{2,1,0:T(8,128)(2,1)} %pad_maximum_fusion), calls=%async_computation.5 | async-start | bytes 1310720 | tf_op jit(solution)/shard_map/all_to_all | solution.py:187

commit v4 on v3

--- a/solution.py
+++ b/solution.py
@@ -16,12 +16,11 @@
 UNROLL = 4
 
 
-def forward_kernel(info, tiles, own, other, o0, o1, o2, o3, total):
+def forward_kernel(info, tiles, own, other, out, total):
     slots = tiles.shape[0]
     count = info[2 * slots]
     core = info[2 * slots + 1]
-    here = info[2 * slots + 2]
-    n_x, n_z = 4, o0.shape[0]
+    n_x, n_z = out.shape[:2]
     total[...] = jnp.zeros_like(total)
 
     def step(b, _):
@@ -34,14 +33,13 @@
             picked = jnp.where((c % 2) == core, own[half], other[half])
             product = jnp.dot(tiles[k], picked, preferred_element_type=F32)
             products.append(jnp.where(k < count, product, 0.0))
-            places.append((r % n_x - here + n_x) % n_x * n_z + r // n_x)
+            places.append(r % n_x * n_z + r // n_x)
         for place, product in zip(places, products):
             total[place] += product
         return 0
 
     lax.fori_loop(0, (count + UNROLL - 1) // UNROLL, step, 0)
-    for d, out in enumerate((o0, o1, o2, o3)):
-        out[...] = total[d * n_z : (d + 1) * n_z].astype(out.dtype)
+    out[...] = total[...].reshape(out.shape).astype(out.dtype)
 
 
 def backward_kernel(info, tiles, g0, g1, g2, g3, keep, send, total):
@@ -114,16 +112,14 @@
 
     blocks = pl.pallas_call(
         forward_kernel,
-        out_shape=(jax.ShapeDtypeStruct((n_z, n, hidden), BF16),) * n_x,
+        out_shape=jax.ShapeDtypeStruct((n_x, n_z, n, hidden), BF16),
         in_specs=[SMEM, VMEM, VMEM, VMEM],
-        out_specs=(VMEM,) * n_x,
+        out_specs=VMEM,
         scratch_shapes=[pltpu.VMEM((tile_rows, n, hidden), F32)],
         compiler_params=pltpu.CompilerParams(vmem_limit_bytes=40 * 2**20),
         name="forward_tiles",
     )(info, tiles, own, other)
-    over_x = blocks[0].astype(F32)
-    for d in range(1, n_x):
-        over_x += lax.ppermute(blocks[d], "x", ring(n_x, d)).astype(F32)
+    over_x = jnp.sum(lax.all_to_all(blocks, "x", 0, 0, tiled=True).astype(F32), axis=0)
     terms = lax.all_to_all(over_x.astype(BF16), "z", 0, 0, tiled=True)
     mixed = jnp.sum(terms.astype(F32), axis=0)
 
@@ -152,9 +148,7 @@
     ).astype(BF16)
     g0 = lax.all_to_all(repeat(grad_here, n_z), "z", 0, 0, tiled=True)
     g0, both = lax.optimization_barrier((g0, both))
-    g = [g0]
-    for d in range(1, n_x):
-        g.append(lax.ppermute(g0, "x", [((i + d) % n_x, i) for i in range(n_x)]))
+    g = [g0] + [lax.ppermute(g0, "x", ring(n_x, n_x - d)) for d in range(1, n_x)]
     both = jnp.sum(lax.all_to_all(both, ROW, 0, 0, tiled=True).astype(F32), axis=0)
     both = lax.all_to_all(repeat(both.astype(BF16), tile_rows), COL, 0, 0, tiled=True)
     both = jnp.sum(both.astype(F32), axis=0)

time: 195 us -> 193 us (0.990)
  blocking collectives: 48.7 us -> 76.7 us
  waiting for transfers between devices: 73.3 us -> 55 us
  starting transfers between devices: 54.5 us -> 42.6 us
    all_to_all x0 -> x1, blocking collectives: none -> 30.3 us  [body(): lax.all_to_all(blocks, 'x', 0, 0, tiled=True).astype(F32)]
    ppermute x6 -> x3, waiting for transfers between devices: 37.8 us -> 18 us  [body(): lax.ppermute(g0, 'x', ring(n_x, n_x - d))]
    ppermute x6 -> x3, starting transfers between devices: 21.8 us -> 8.43 us  [body(): lax.ppermute(g0, 'x', ring(n_x, n_x - d))]
    all_to_all x1, blocking collectives: 26.5 us -> 24.2 us  [body(): terms = lax.all_to_all(over_x.astype(BF16), 'z', 0, 0, tiled=True)]
  transfers between devices with their start and end apart: 13 -> 10, of which waited for: 10 -> 8; matrix products, arithmetic and copies ran while one was open for 2% -> 2% of each run, Pallas kernels for 1% -> 1%
where the time goes in v4:
time: 193 us; the launch traced here: 192 us
  blocking collectives  76.7 us (40%)
  waiting for transfers between devices  55 us (28%)
  starting transfers between devices  42.6 us (22%)
  other arithmetic  5.14 us (3%)
  Pallas kernels  4.61 us (2%)
  local copies, waits for them, and re-layouts  4.22 us (2%)
  matrix products  2.07 us (1%)
    all_to_all x1, blocking collectives, body(): lax.all_to_all(blocks, 'x', 0, 0, tiled=True).astype(F32)  30.3 us
    all_to_all x1, blocking collectives, body(): terms = lax.all_to_all(over_x.astype(BF16), 'z', 0, 0, tiled=True)  24.2 us
    all_to_all x1, blocking collectives, body(): own = lax.all_to_all(repeat(share, n_y), 'y', 0, 0, tiled=True)  22.2 us
    all_to_all x1, waiting for transfers between devices, body(): last = lax.all_to_all(last, 'y', 0, 0, tiled=True)  20.2 us
    ppermute x3, waiting for transfers between devices, body(): lax.ppermute(g0, 'x', ring(n_x, n_x - d))  18 us
    all_to_all x1, waiting for transfers between devices, body(): g0 = lax.all_to_all(repeat(grad_here, n_z), 'z', 0, 0, tiled=True)  13.2 us
    all_to_all x1, starting transfers between devices, body(): lax.all_to_all(both, ROW, 0, 0, tiled=True).astype(F32)  8.82 us
    ppermute x3, starting transfers between devices, body(): lax.ppermute(g0, 'x', ring(n_x, n_x - d))  8.43 us
  transfers between devices with their start and end apart: 10, of which 8 were waited for; matrix products, arithmetic and copies ran while one was open for 2% of the time, Pallas kernels for 1%

profile of v4, /device:TPU:1, one launch (start us, length us, event | category | flops | bytes accessed | tf_op | source)
XLA Modules:
  0.0 191.9 jit_solution(14691334651547187683)
XLA Ops:
  0.7 1.0 multiply_convert_fusion.3
  1.7 22.2 %all_to_all.35.own = bf16[8,128,256]{2,1,0:T(8,128)(2,1)S(1)} all-to-all(bf16[8,128,256]{2,1,0:T(8,128)(2,1)S(1)} %broadcast_in_dim.10), channel_id=1, replica_groups=mesh['y'=8,'core'=2,'z'=8,'x'=4] {'y'}, dimensions={0} | all-to-all | bytes 1048576 | tf_op jit(solution)/shard_map/all_to_all | solution.py:110
  23.9 5.6 %collective-permute-start = (bf16[8,128,256]{2,1,0:T(8,128)(2,1)S(1)}, bf16[8,128,256]{2,1,0:T(8,128)(2,1)S(1)}, u32[]{:S(2)}, u32[]{:S(2)}) collective-permute-start(bf16[8,128,256]{2,1,0:T(8,128)(2,1)S(1)} %all_to_all.35.own), channel_id=1, source_target_pairs={{0,32},{32,0},{1,33},{33,1},{2,34},{34,2},{3,35},{35,3},{4,36},{36... | collective-permute-start | bytes 1572872 | tf_op jit(solution)/shard_map/ppermute | solution.py:111
  31.0 2.0 %forward_tiles.1 = bf16[4,8,128,256]{3,2,1,0:T(8,128)(2,1)S(1)} custom-call(s32[51]{0:T(128)S(1)} %concatenate.13.info, bf16[24,128,128]{2,1,0:T(8,128)(2,1)S(1)} %bitcast.19, bf16[8,128,256]{2,1,0:T(8,128)(2,1)S(1)} %all_to_all.35.own, bf16[8,128,256]{2,1,0:T(8,128)(2,1)S(1)} %collective-permute-done.other), custom_call_target="tpu_custom_call" | custom-call | tf_op jit(solution)/shard_map/forward_tiles/pallas_call | solution.py:113
  33.0 30.3 %all_to_all.36 = bf16[4,8,128,256]{3,2,1,0:T(8,128)(2,1)S(1)} all-to-all(bf16[4,8,128,256]{3,2,1,0:T(8,128)(2,1)S(1)} %forward_tiles.1), channel_id=1, replica_groups=mesh['y'=8,'core'=2,'z'=8,'x'=4] {'x'}, dimensions={0} | all-to-all | bytes 4194304 | tf_op jit(solution)/shard_map/all_to_all | solution.py:122
  63.7 24.2 %all_to_all.37 = bf16[8,128,256]{2,1,0:T(8,128)(2,1)S(1)} all-to-all(bf16[8,128,256]{2,1,0:T(8,128)(2,1)S(1)} %reduce_sum.60), channel_id=1, replica_groups=mesh['y'=8,'core'=2,'z'=8,'x'=4] {'z'}, dimensions={0} | all-to-all | bytes 1048576 | tf_op jit(solution)/shard_map/all_to_all | solution.py:123
  90.0 3.5 %all-to-all-start.3 = ((bf16[8,128,256]{2,1,0:T(8,128)(2,1)}), bf16[8,128,256]{2,1,0:T(8,128)(2,1)S(1)}, u32[]{:S(2)}, u32[]{:S(2)}) async-start(bf16[8,128,256]{2,1,0:T(8,128)(2,1)} %broadcast_in_dim.11), calls=%async_computation.3 | async-start | bytes 1048576 | tf_op jit(solution)/shard_map/all_to_all | solution.py:149
  94.4 13.2 %all-to-all-done.3.g0 = bf16[8,128,256]{2,1,0:T(8,128)(2,1)S(1)} async-done(((bf16[8,128,256]{2,1,0:T(8,128)(2,1)}), bf16[8,128,256]{2,1,0:T(8,128)(2,1)S(1)}, u32[]{:S(2)}, u32[]{:S(2)}) %all-to-all-start.3) | async-done | bytes 524320 | tf_op jit(solution)/shard_map/all_to_all | solution.py:149
  107.6 8.8 %all-to-all-start.4 = ((bf16[16,24,256]{2,1,0:T(8,128)(2,1)}), bf16[16,24,256]{2,1,0:T(8,128)(2,1)S(1)}, u32[]{:S(2)}, u32[]{:S(2)}) async-start(bf16[16,24,256]{2,1,0:T(8,128)(2,1)} %pad_maximum_fusion.1), calls=%async_computation.4 | async-start | bytes 393216 | tf_op jit(solution)/shard_map/all_to_all | solution.py:152
  116.4 2.2 %collective-permute-start.3 = (bf16[8,128,256]{2,1,0:T(8,128)(2,1)S(1)}, bf16[8,128,256]{2,1,0:T(8,128)(2,1)S(1)}, u32[]{:S(2)}, u32[]{:S(2)}) collective-permute-start(bf16[8,128,256]{2,1,0:T(8,128)(2,1)S(1)} %all-to-all-done.3.g0), channel_id=1, source_target_pairs={{0,1},{1,2},{2,3},{3,0},{4,5},{5,6},{6,7},{7,4},{8,9},{9,10},{10,1... | collective-permute-start | bytes 1572872 | tf_op jit(solution)/shard_map/ppermute | solution.py:151
  118.6 3.7 %collective-permute-start.2 = (bf16[8,128,256]{2,1,0:T(8,128)(2,1)S(1)}, bf16[8,128,256]{2,1,0:T(8,128)(2,1)S(1)}, u32[]{:S(2)}, u32[]{:S(2)}) collective-permute-start(bf16[8,128,256]{2,1,0:T(8,128)(2,1)S(1)} %all-to-all-done.3.g0), channel_id=1, source_target_pairs={{0,2},{1,3},{2,0},{3,1},{4,6},{5,7},{6,4},{7,5},{8,10},{9,11},{10,... | collective-permute-start | bytes 1572872 | tf_op jit(solution)/shard_map/ppermute | solution.py:151
  122.3 2.5 %collective-permute-start.1 = (bf16[8,128,256]{2,1,0:T(8,128)(2,1)S(1)}, bf16[8,128,256]{2,1,0:T(8,128)(2,1)S(1)}, u32[]{:S(2)}, u32[]{:S(2)}) collective-permute-start(bf16[8,128,256]{2,1,0:T(8,128)(2,1)S(1)} %all-to-all-done.3.g0), channel_id=1, source_target_pairs={{0,3},{1,0},{2,1},{3,2},{4,7},{5,4},{6,5},{7,6},{8,11},{9,8},{10,9... | collective-permute-start | bytes 1572872 | tf_op jit(solution)/shard_map/ppermute | solution.py:151
  124.9 1.9 all-to-all-done.4
  127.6 4.6 %all-to-all-start.5 = ((bf16[32,24,256]{2,1,0:T(8,128)(2,1)}), bf16[32,24,256]{2,1,0:T(8,128)(2,1)}, u32[]{:S(2)}, u32[]{:S(2)}) async-start(bf16[32,24,256]{2,1,0:T(8,128)(2,1)} %broadcast_in_dim.13), calls=%async_computation.5 | async-start | bytes 786432 | tf_op jit(solution)/shard_map/all_to_all | solution.py:153
  132.2 5.0 %collective-permute-done.3.g3 = bf16[8,128,256]{2,1,0:T(8,128)(2,1)S(1)} collective-permute-done((bf16[8,128,256]{2,1,0:T(8,128)(2,1)S(1)}, bf16[8,128,256]{2,1,0:T(8,128)(2,1)S(1)}, u32[]{:S(2)}, u32[]{:S(2)}) %collective-permute-start.3) | collective-permute-done | bytes 524320 | tf_op jit(solution)/shard_map/ppermute | solution.py:151
  137.1 10.7 %collective-permute-done.2.g2 = bf16[8,128,256]{2,1,0:T(8,128)(2,1)S(1)} collective-permute-done((bf16[8,128,256]{2,1,0:T(8,128)(2,1)S(1)}, bf16[8,128,256]{2,1,0:T(8,128)(2,1)S(1)}, u32[]{:S(2)}, u32[]{:S(2)}) %collective-permute-start.2) | collective-permute-done | bytes 524320 | tf_op jit(solution)/shard_map/ppermute | solution.py:151
  147.8 2.4 %collective-permute-done.1.g1 = bf16[8,128,256]{2,1,0:T(8,128)(2,1)S(1)} collective-permute-done((bf16[8,128,256]{2,1,0:T(8,128)(2,1)S(1)}, bf16[8,128,256]{2,1,0:T(8,128)(2,1)S(1)}, u32[]{:S(2)}, u32[]{:S(2)}) %collective-permute-start.1) | collective-permute-done | bytes 524320 | tf_op jit(solution)/shard_map/ppermute | solution.py:151
  151.0 1.0 copy-done.3
  152.0 2.6 %backward_tiles.1 = (f32[8,128,256]{2,1,0:T(8,128)S(1)}, bf16[8,128,256]{2,1,0:T(8,128)(2,1)}) custom-call(s32[51]{0:T(128)S(1)} %concatenate.13.info, bf16[24,128,128]{2,1,0:T(8,128)(2,1)S(1)} %bitcast.20, bf16[8,128,256]{2,1,0:T(8,128)(2,1)S(1)} %all-to-all-done.3.g0, bf16[8,128,256]{2,1,0:T(8,128)(2,1)S(1)} %copy-done.3, ...), custom_call_target="tpu_custom_call" | custom-call | tf_op jit(solution)/shard_map/backward_tiles/pallas_call | solution.py:167
  154.6 3.1 %collective-permute-start.4 = (bf16[8,128,256]{2,1,0:T(8,128)(2,1)}, bf16[8,128,256]{2,1,0:T(8,128)(2,1)S(1)}, u32[]{:S(2)}, u32[]{:S(2)}) collective-permute-start(bf16[8,128,256]{2,1,0:T(8,128)(2,1)} %get-tuple-element.10), channel_id=1, source_target_pairs={{0,32},{32,0},{1,33},{33,1},{2,34},{34,2},{3,35},{35,3},{4,36},{36... | collective-permute-start | bytes 1572872 | tf_op jit(solution)/shard_map/ppermute | solution.py:179
  157.7 1.1 convert_reduce_fusion.2
  158.8 1.9 %collective-permute-start.5 = (bf16[16,256]{1,0:T(8,128)(2,1)S(1)}, bf16[16,256]{1,0:T(8,128)(2,1)S(1)}, u32[]{:S(2)}, u32[]{:S(2)}) collective-permute-start(bf16[16,256]{1,0:T(8,128)(2,1)S(1)} %slice.33), channel_id=1, source_target_pairs={{0,32},{32,0},{1,33},{33,1},{2,34},{34,2},{3,35},{35,3},{4,36},{36... | collective-permute-start | bytes 24584 | tf_op jit(solution)/shard_map/ppermute | solution.py:157
  162.8 6.7 %all-to-all-start.6 = ((bf16[8,160,256]{2,1,0:T(8,128)(2,1)}), bf16[8,160,256]{2,1,0:T(8,128)(2,1)S(1)}, u32[]{:S(2)}, u32[]{:S(2)}) async-start(bf16[8,160,256]{2,1,0:T(8,128)(2,1)} %pad_maximum_fusion), calls=%async_computation.6 | async-start | bytes 1310720 | tf_op jit(solution)/shard_map/all_to_all | solution.py:181
  170.0 20.2 %all-to-all-done.6 = bf16[8,160,256]{2,1,0:T(8,128)(2,1)S(1)} async-done(((bf16[8,160,256]{2,1,0:T(8,128)(2,1)}), bf16[8,160,256]{2,1,0:T(8,128)(2,1)S(1)}, u32[]{:S(2)}, u32[]{:S(2)}) %all-to-all-start.6) | async-done | bytes 655392 | tf_op jit(solution)/shard_map/all_to_all | solution.py:181
  (47 shorter events, 10.1 us)
Async XLA Ops:
  0.6 87.4 %copy-start = (bf16[256,256]{1,0:T(8,128)(2,1)S(1)}, bf16[256,256]{1,0:T(8,128)(2,1)}, u32[]{:S(2)}) copy-start(bf16[256,256]{1,0:T(8,128)(2,1)} %param.11) | copy-start | bytes 393220
  0.6 29.5 %copy-start.5 = (s32[1,1,24,2]{2,3,1,0:T(2,128)S(1)}, s32[1,1,24,2]{2,3,1,0:T(2,128)}, u32[]{:S(2)}) copy-start(s32[1,1,24,2]{2,3,1,0:T(2,128)} %param.13) | copy-start | bytes 580
  0.7 30.4 %copy-start.1 = (bf16[1,1,24,128,128]{4,3,2,1,0:T(8,128)(2,1)S(1)}, bf16[1,1,24,128,128]{4,3,2,1,0:T(8,128)(2,1)}, u32[]{:S(2)}) copy-start(bf16[1,1,24,128,128]{4,3,2,1,0:T(8,128)(2,1)} %param.15) | copy-start | bytes 2359300
  23.9 7.1 %collective-permute-start = (bf16[8,128,256]{2,1,0:T(8,128)(2,1)S(1)}, bf16[8,128,256]{2,1,0:T(8,128)(2,1)S(1)}, u32[]{:S(2)}, u32[]{:S(2)}) collective-permute-start(bf16[8,128,256]{2,1,0:T(8,128)(2,1)S(1)} %all_to_all.35.own), channel_id=1, source_target_pairs={{0,32},{32,0},{1,33},{33,1},{2,34},{34,2},{3,35},{35,3},{4,36},{36... | collective-permute-start | bytes 1572872 | tf_op jit(solution)/shard_map/ppermute | solution.py:111
  63.7 24.5 %copy-start.6 = (f32[128]{0:T(128)S(1)}, f32[128]{0:T(128)}, u32[]{:S(2)}) copy-start(f32[128]{0:T(128)} %param.16) | copy-start | bytes 1540
  63.7 24.5 %copy-start.7 = (bf16[128,256]{1,0:T(8,128)(2,1)S(1)}, bf16[128,256]{1,0:T(8,128)(2,1)}, u32[]{:S(2)}) copy-start(bf16[128,256]{1,0:T(8,128)(2,1)} %param.17) | copy-start | bytes 196612
  63.7 24.5 %copy-start.8 = (f32[256]{0:T(256)S(1)}, f32[256]{0:T(256)}, u32[]{:S(2)}) copy-start(f32[256]{0:T(256)} %param.12) | copy-start | bytes 3076
  90.0 17.6 %all-to-all-start.3 = ((bf16[8,128,256]{2,1,0:T(8,128)(2,1)}), bf16[8,128,256]{2,1,0:T(8,128)(2,1)S(1)}, u32[]{:S(2)}, u32[]{:S(2)}) async-start(bf16[8,128,256]{2,1,0:T(8,128)(2,1)} %broadcast_in_dim.11), calls=%async_computation.3 | async-start | bytes 1048576 | tf_op jit(solution)/shard_map/all_to_all | solution.py:149
  107.6 19.1 %all-to-all-start.4 = ((bf16[16,24,256]{2,1,0:T(8,128)(2,1)}), bf16[16,24,256]{2,1,0:T(8,128)(2,1)S(1)}, u32[]{:S(2)}, u32[]{:S(2)}) async-start(bf16[16,24,256]{2,1,0:T(8,128)(2,1)} %pad_maximum_fusion.1), calls=%async_computation.4 | async-start | bytes 393216 | tf_op jit(solution)/shard_map/all_to_all | solution.py:152
  116.4 20.7 %collective-permute-start.3 = (bf16[8,128,256]{2,1,0:T(8,128)(2,1)S(1)}, bf16[8,128,256]{2,1,0:T(8,128)(2,1)S(1)}, u32[]{:S(2)}, u32[]{:S(2)}) collective-permute-start(bf16[8,128,256]{2,1,0:T(8,128)(2,1)S(1)} %all-to-all-done.3.g0), channel_id=1, source_target_pairs={{0,1},{1,2},{2,3},{3,0},{4,5},{5,6},{6,7},{7,4},{8,9},{9,10},{10,1... | collective-permute-start | bytes 1572872 | tf_op jit(solution)/shard_map/ppermute | solution.py:151
  118.6 29.2 %collective-permute-start.2 = (bf16[8,128,256]{2,1,0:T(8,128)(2,1)S(1)}, bf16[8,128,256]{2,1,0:T(8,128)(2,1)S(1)}, u32[]{:S(2)}, u32[]{:S(2)}) collective-permute-start(bf16[8,128,256]{2,1,0:T(8,128)(2,1)S(1)} %all-to-all-done.3.g0), channel_id=1, source_target_pairs={{0,2},{1,3},{2,0},{3,1},{4,6},{5,7},{6,4},{7,5},{8,10},{9,11},{10,... | collective-permute-start | bytes 1572872 | tf_op jit(solution)/shard_map/ppermute | solution.py:151
  122.3 27.8 %collective-permute-start.1 = (bf16[8,128,256]{2,1,0:T(8,128)(2,1)S(1)}, bf16[8,128,256]{2,1,0:T(8,128)(2,1)S(1)}, u32[]{:S(2)}, u32[]{:S(2)}) collective-permute-start(bf16[8,128,256]{2,1,0:T(8,128)(2,1)S(1)} %all-to-all-done.3.g0), channel_id=1, source_target_pairs={{0,3},{1,0},{2,1},{3,2},{4,7},{5,4},{6,5},{7,6},{8,11},{9,8},{10,9... | collective-permute-start | bytes 1572872 | tf_op jit(solution)/shard_map/ppermute | solution.py:151
  127.6 30.2 %all-to-all-start.5 = ((bf16[32,24,256]{2,1,0:T(8,128)(2,1)}), bf16[32,24,256]{2,1,0:T(8,128)(2,1)}, u32[]{:S(2)}, u32[]{:S(2)}) async-start(bf16[32,24,256]{2,1,0:T(8,128)(2,1)} %broadcast_in_dim.13), calls=%async_computation.5 | async-start | bytes 786432 | tf_op jit(solution)/shard_map/all_to_all | solution.py:153
  150.1 0.8 copy-start.2
  150.9 1.0 copy-start.3
  154.6 6.1 %collective-permute-start.4 = (bf16[8,128,256]{2,1,0:T(8,128)(2,1)}, bf16[8,128,256]{2,1,0:T(8,128)(2,1)S(1)}, u32[]{:S(2)}, u32[]{:S(2)}) collective-permute-start(bf16[8,128,256]{2,1,0:T(8,128)(2,1)} %get-tuple-element.10), channel_id=1, source_target_pairs={{0,32},{32,0},{1,33},{33,1},{2,34},{34,2},{3,35},{35,3},{4,36},{36... | collective-permute-start | bytes 1572872 | tf_op jit(solution)/shard_map/ppermute | solution.py:179
  158.8 3.1 %collective-permute-start.5 = (bf16[16,256]{1,0:T(8,128)(2,1)S(1)}, bf16[16,256]{1,0:T(8,128)(2,1)S(1)}, u32[]{:S(2)}, u32[]{:S(2)}) collective-permute-start(bf16[16,256]{1,0:T(8,128)(2,1)S(1)} %slice.33), channel_id=1, source_target_pairs={{0,32},{32,0},{1,33},{33,1},{2,34},{34,2},{3,35},{35,3},{4,36},{36... | collective-permute-start | bytes 24584 | tf_op jit(solution)/shard_map/ppermute | solution.py:157
  162.8 27.5 %copy-start.4 = (f32[128]{0:T(128)S(1)}, f32[128]{0:T(128)}, u32[]{:S(2)}) copy-start(f32[128]{0:T(128)} %param.10) | copy-start | bytes 1540
  162.8 27.4 %all-to-all-start.6 = ((bf16[8,160,256]{2,1,0:T(8,128)(2,1)}), bf16[8,160,256]{2,1,0:T(8,128)(2,1)S(1)}, u32[]{:S(2)}, u32[]{:S(2)}) async-start(bf16[8,160,256]{2,1,0:T(8,128)(2,1)} %pad_maximum_fusion), calls=%async_computation.6 | async-start | bytes 1310720 | tf_op jit(solution)/shard_map/all_to_all | solution.py:181

commit v5 on v4

--- a/solution.py
+++ b/solution.py
@@ -42,11 +42,11 @@
     out[...] = total[...].reshape(out.shape).astype(out.dtype)
 
 
-def backward_kernel(info, tiles, g0, g1, g2, g3, keep, send, total):
+def backward_kernel(info, tiles, g, keep, send, total):
     slots = tiles.shape[0]
     count = info[2 * slots]
     core = info[2 * slots + 1]
-    here = info[2 * slots + 2]
+    n_x, n_z = 4, g.shape[0] // 4
     n_half = keep.shape[0]
     total[...] = jnp.zeros_like(total)
 
@@ -56,13 +56,7 @@
             k = b * UNROLL + u
             r = info[k]
             c = info[slots + k]
-            z = r // 4
-            d = (r % 4 - here + 4) % 4
-            picked = jnp.where(
-                d < 2,
-                jnp.where(d == 0, g0[z], g1[z]),
-                jnp.where(d == 2, g2[z], g3[z]),
-            )
+            picked = g[r % n_x * n_z + r // n_x]
             product = lax.dot_general(
                 tiles[k], picked, (((0,), (0,)), ((), ())), preferred_element_type=F32
             )
@@ -75,10 +69,6 @@
     lax.fori_loop(0, (count + UNROLL - 1) // UNROLL, step, 0)
     keep[...] = total[:n_half]
     send[...] = total[n_half:].astype(send.dtype)
-
-
-def ring(n, d):
-    return [(i, (i + d) % n) for i in range(n)]
 
 
 def repeat(a, n):
@@ -102,7 +92,6 @@
             coords[:, 1],
             tile_count[0],
             lax.axis_index("core").reshape(1),
-            lax.axis_index("x").reshape(1),
         ]
     )
 
@@ -148,7 +137,7 @@
     ).astype(BF16)
     g0 = lax.all_to_all(repeat(grad_here, n_z), "z", 0, 0, tiled=True)
     g0, both = lax.optimization_barrier((g0, both))
-    g = [g0] + [lax.ppermute(g0, "x", ring(n_x, n_x - d)) for d in range(1, n_x)]
+    g = lax.all_gather(g0, "x", axis=0, tiled=True)
     both = jnp.sum(lax.all_to_all(both, ROW, 0, 0, tiled=True).astype(F32), axis=0)
     both = lax.all_to_all(repeat(both.astype(BF16), tile_rows), COL, 0, 0, tiled=True)
     both = jnp.sum(both.astype(F32), axis=0)
@@ -170,12 +159,12 @@
             jax.ShapeDtypeStruct((n_y, n, hidden), F32),
             jax.ShapeDtypeStruct((n_y, n, hidden), BF16),
         ),
-        in_specs=[SMEM, VMEM, VMEM, VMEM, VMEM, VMEM],
+        in_specs=[SMEM, VMEM, VMEM],
         out_specs=(VMEM, VMEM),
         scratch_shapes=[pltpu.VMEM((tile_cols, n, hidden), F32)],
         compiler_params=pltpu.CompilerParams(vmem_limit_bytes=40 * 2**20),
         name="backward_tiles",
-    )(info, tiles, *g)
+    )(info, tiles, g)
     pair = (keep + lax.ppermute(send, "core", swap).astype(F32)).astype(BF16)
     last = jnp.concatenate([pair, repeat(chunks, n_y)], axis=1)
     last = lax.all_to_all(last, "y", 0, 0, tiled=True)

time: 193 us -> 196 us (1.016)
  blocking collectives: 76.7 us -> 94.8 us
  starting transfers between devices: 42.6 us -> 25.7 us
  between operations: 1.57 us -> 14.9 us
  waiting for transfers between devices: 55 us -> 45.8 us
    ppermute x3 -> x0, waiting for transfers between devices: 18 us -> none  [body(): lax.ppermute(g0, 'x', ring(n_x, n_x - d))]
    all_to_all x0 -> x1, blocking collectives: none -> 17.2 us  [body(): lax.all_to_all(both, ROW, 0, 0, tiled=True).astype(F32)]
    all_gather x0 -> x1, waiting for transfers between devices: none -> 10.7 us  [body(): g = lax.all_gather(g0, 'x', axis=0, tiled=True)]
    all_to_all x1 -> x0, starting transfers between devices: 8.82 us -> none  [body(): lax.all_to_all(both, ROW, 0, 0, tiled=True).astype(F32)]
    ppermute x3 -> x0, starting transfers between devices: 8.43 us -> none  [body(): lax.ppermute(g0, 'x', ring(n_x, n_x - d))]
    all_to_all x1, blocking collectives: 24.2 us -> 26.2 us  [body(): terms = lax.all_to_all(over_x.astype(BF16), 'z', 0, 0, tiled=True)]
  transfers between devices with their start and end apart: 10 -> 7, of which waited for: 8 -> 4; matrix products, arithmetic and copies ran while one was open for 2% -> 1% of each run, Pallas kernels for 1% -> 1%
where the time goes in v5:
time: 196 us
  blocking collectives  94.8 us (48%)
  waiting for transfers between devices  45.8 us (23%)
  starting transfers between devices  25.7 us (13%)
  between operations  14.9 us (8%)
  local copies, waits for them, and re-layouts  5.43 us (3%)
  other arithmetic  3.57 us (2%)
  Pallas kernels  3.33 us (2%)
  matrix products  2.07 us (1%)
    all_to_all x1, blocking collectives, body(): lax.all_to_all(blocks, 'x', 0, 0, tiled=True).astype(F32)  29.3 us
    all_to_all x1, blocking collectives, body(): terms = lax.all_to_all(over_x.astype(BF16), 'z', 0, 0, tiled=True)  26.2 us
    all_to_all x1, blocking collectives, body(): own = lax.all_to_all(repeat(share, n_y), 'y', 0, 0, tiled=True)  22.2 us
    all_to_all x1, waiting for transfers between devices, body(): last = lax.all_to_all(last, 'y', 0, 0, tiled=True)  20.2 us
    all_to_all x1, blocking collectives, body(): lax.all_to_all(both, ROW, 0, 0, tiled=True).astype(F32)  17.2 us
    all_to_all x1, waiting for transfers between devices, body(): g0 = lax.all_to_all(repeat(grad_here, n_z), 'z', 0, 0, tiled=True)  13.8 us
    all_gather x1, waiting for transfers between devices, body(): g = lax.all_gather(g0, 'x', axis=0, tiled=True)  10.7 us
    all_to_all x1, starting transfers between devices, body(): last = lax.all_to_all(last, 'y', 0, 0, tiled=True)  8.34 us
  transfers between devices with their start and end apart: 7, of which 4 were waited for; matrix products, arithmetic and copies ran while one was open for 1% of the time, Pallas kernels for 1%

profile of v5, /device:TPU:1, one launch (start us, length us, event | category | flops | bytes accessed | tf_op | source)
XLA Modules:
  0.0 195.7 jit_solution(5106726349459044435)
XLA Ops:
  7.2 1.0 multiply_convert_fusion.3
  8.2 22.2 %all_to_all.35.own = bf16[8,128,256]{2,1,0:T(8,128)(2,1)S(1)} all-to-all(bf16[8,128,256]{2,1,0:T(8,128)(2,1)S(1)} %broadcast_in_dim.10), channel_id=1, replica_groups=mesh['y'=8,'core'=2,'z'=8,'x'=4] {'y'}, dimensions={0} | all-to-all | bytes 1048576 | tf_op jit(solution)/shard_map/all_to_all | solution.py:99
  30.4 5.6 %collective-permute-start = (bf16[8,128,256]{2,1,0:T(8,128)(2,1)S(1)}, bf16[8,128,256]{2,1,0:T(8,128)(2,1)S(1)}, u32[]{:S(2)}, u32[]{:S(2)}) collective-permute-start(bf16[8,128,256]{2,1,0:T(8,128)(2,1)S(1)} %all_to_all.35.own), channel_id=1, source_target_pairs={{0,32},{32,0},{1,33},{33,1},{2,34},{34,2},{3,35},{35,3},{4,36},{36... | collective-permute-start | bytes 1572872 | tf_op jit(solution)/shard_map/ppermute | solution.py:100
  37.6 1.7 forward_tiles.1
  39.3 29.3 %all_to_all.36 = bf16[4,8,128,256]{3,2,1,0:T(8,128)(2,1)S(1)} all-to-all(bf16[4,8,128,256]{3,2,1,0:T(8,128)(2,1)S(1)} %forward_tiles.1), channel_id=1, replica_groups=mesh['y'=8,'core'=2,'z'=8,'x'=4] {'x'}, dimensions={0} | all-to-all | bytes 4194304 | tf_op jit(solution)/shard_map/all_to_all | solution.py:111
  69.0 26.2 %all_to_all.37 = bf16[8,128,256]{2,1,0:T(8,128)(2,1)S(1)} all-to-all(bf16[8,128,256]{2,1,0:T(8,128)(2,1)S(1)} %reduce_sum.60), channel_id=1, replica_groups=mesh['y'=8,'core'=2,'z'=8,'x'=4] {'z'}, dimensions={0} | all-to-all | bytes 1048576 | tf_op jit(solution)/shard_map/all_to_all | solution.py:112
  95.5 0.9 fusion.8
  96.4 0.8 broadcast_in_dim.11
  97.2 3.5 %all-to-all-start.3 = ((bf16[8,128,256]{2,1,0:T(8,128)(2,1)}), bf16[8,128,256]{2,1,0:T(8,128)(2,1)S(1)}, u32[]{:S(2)}, u32[]{:S(2)}) async-start(bf16[8,128,256]{2,1,0:T(8,128)(2,1)} %broadcast_in_dim.11), calls=%async_computation.3 | async-start | bytes 1048576 | tf_op jit(solution)/shard_map/all_to_all | solution.py:138
  101.0 13.8 %all-to-all-done.3 = bf16[8,128,256]{2,1,0:T(8,128)(2,1)S(1)} async-done(((bf16[8,128,256]{2,1,0:T(8,128)(2,1)}), bf16[8,128,256]{2,1,0:T(8,128)(2,1)S(1)}, u32[]{:S(2)}, u32[]{:S(2)}) %all-to-all-start.3) | async-done | bytes 524320 | tf_op jit(solution)/shard_map/all_to_all | solution.py:138
  114.9 0.8 copy-done.3
  115.7 17.2 %all_to_all.38 = bf16[16,24,256]{2,1,0:T(8,128)(2,1)S(1)} all-to-all(bf16[16,24,256]{2,1,0:T(8,128)(2,1)S(1)} %pad_maximum_fusion.1), channel_id=1, replica_groups=mesh['y'=8,'core'=2,'z'=8,'x'=4] {'y','core'}, dimensions={0} | all-to-all | bytes 393216 | tf_op jit(solution)/shard_map/all_to_all | solution.py:141
  132.9 0.8 broadcast_in_dim.13
  133.7 3.9 %all-to-all-start.5 = ((bf16[32,24,256]{2,1,0:T(8,128)(2,1)}), bf16[32,24,256]{2,1,0:T(8,128)(2,1)S(1)}, u32[]{:S(2)}, u32[]{:S(2)}) async-start(bf16[32,24,256]{2,1,0:T(8,128)(2,1)} %broadcast_in_dim.13), calls=%async_computation.5 | async-start | bytes 786432 | tf_op jit(solution)/shard_map/all_to_all | solution.py:142
  137.6 10.7 %all-gather.2.cloned.1.call-done.g = bf16[32,128,256]{2,1,0:T(8,128)(2,1)} async-done(((bf16[8,128,256]{2,1,0:T(8,128)(2,1)}), bf16[32,128,256]{2,1,0:T(8,128)(2,1)}) %all-gather.2.cloned.1.call-update) | async-done | bytes 2097168 | tf_op jit(solution)/shard_map/all_gather | solution.py:140
  148.3 1.6 copy-done.2
  149.9 1.6 backward_tiles.1
  151.4 2.3 %collective-permute-start.1 = (bf16[8,128,256]{2,1,0:T(8,128)(2,1)S(1)}, bf16[8,128,256]{2,1,0:T(8,128)(2,1)S(1)}, u32[]{:S(2)}, u32[]{:S(2)}) collective-permute-start(bf16[8,128,256]{2,1,0:T(8,128)(2,1)S(1)} %get-tuple-element.10), channel_id=1, source_target_pairs={{0,32},{32,0},{1,33},{33,1},{2,34},{34,2},{3,35},{35,3},{4,36},{36... | collective-permute-start | bytes 1572872 | tf_op jit(solution)/shard_map/ppermute | solution.py:168
  153.9 2.0 %collective-permute-start.2 = (bf16[16,256]{1,0:T(8,128)(2,1)S(1)}, bf16[16,256]{1,0:T(8,128)(2,1)S(1)}, u32[]{:S(2)}, u32[]{:S(2)}) collective-permute-start(bf16[16,256]{1,0:T(8,128)(2,1)S(1)} %slice.33), channel_id=1, source_target_pairs={{0,32},{32,0},{1,33},{33,1},{2,34},{34,2},{3,35},{35,3},{4,36},{36... | collective-permute-start | bytes 24584 | tf_op jit(solution)/shard_map/ppermute | solution.py:146
  155.9 1.1 collective-permute-done.2
  157.1 0.9 pad_maximum_fusion
  158.0 8.3 %all-to-all-start.6 = ((bf16[8,160,256]{2,1,0:T(8,128)(2,1)}), bf16[8,160,256]{2,1,0:T(8,128)(2,1)S(1)}, u32[]{:S(2)}, u32[]{:S(2)}) async-start(bf16[8,160,256]{2,1,0:T(8,128)(2,1)} %pad_maximum_fusion), calls=%async_computation.6 | async-start | bytes 1310720 | tf_op jit(solution)/shard_map/all_to_all | solution.py:170
  166.9 20.2 %all-to-all-done.6 = bf16[8,160,256]{2,1,0:T(8,128)(2,1)S(1)} async-done(((bf16[8,160,256]{2,1,0:T(8,128)(2,1)}), bf16[8,160,256]{2,1,0:T(8,128)(2,1)S(1)}, u32[]{:S(2)}, u32[]{:S(2)}) %all-to-all-start.6) | async-done | bytes 655392 | tf_op jit(solution)/shard_map/all_to_all | solution.py:170
  187.2 0.8 convolution_convert_fusion
  (41 shorter events, 3.6 us)
Async XLA Ops:
  7.2 88.1 %copy-start = (bf16[256,256]{1,0:T(8,128)(2,1)S(1)}, bf16[256,256]{1,0:T(8,128)(2,1)}, u32[]{:S(2)}) copy-start(bf16[256,256]{1,0:T(8,128)(2,1)} %param.11) | copy-start | bytes 393220
  7.2 30.4 %copy-start.1 = (bf16[1,1,24,128,128]{4,3,2,1,0:T(8,128)(2,1)S(1)}, bf16[1,1,24,128,128]{4,3,2,1,0:T(8,128)(2,1)}, u32[]{:S(2)}) copy-start(bf16[1,1,24,128,128]{4,3,2,1,0:T(8,128)(2,1)} %param.15) | copy-start | bytes 2359300
  30.4 7.1 %collective-permute-start = (bf16[8,128,256]{2,1,0:T(8,128)(2,1)S(1)}, bf16[8,128,256]{2,1,0:T(8,128)(2,1)S(1)}, u32[]{:S(2)}, u32[]{:S(2)}) collective-permute-start(bf16[8,128,256]{2,1,0:T(8,128)(2,1)S(1)} %all_to_all.35.own), channel_id=1, source_target_pairs={{0,32},{32,0},{1,33},{33,1},{2,34},{34,2},{3,35},{35,3},{4,36},{36... | collective-permute-start | bytes 1572872 | tf_op jit(solution)/shard_map/ppermute | solution.py:100
  68.6 26.8 %copy-start.5 = (f32[128]{0:T(128)S(1)}, f32[128]{0:T(128)}, u32[]{:S(2)}) copy-start(f32[128]{0:T(128)} %param.16) | copy-start | bytes 1540
  68.6 26.8 %copy-start.7 = (f32[256]{0:T(256)S(1)}, f32[256]{0:T(256)}, u32[]{:S(2)}) copy-start(f32[256]{0:T(256)} %param.12) | copy-start | bytes 3076
  69.0 26.5 %copy-start.6 = (bf16[128,256]{1,0:T(8,128)(2,1)S(1)}, bf16[128,256]{1,0:T(8,128)(2,1)}, u32[]{:S(2)}) copy-start(bf16[128,256]{1,0:T(8,128)(2,1)} %param.17) | copy-start | bytes 196612
  97.2 17.7 %all-to-all-start.3 = ((bf16[8,128,256]{2,1,0:T(8,128)(2,1)}), bf16[8,128,256]{2,1,0:T(8,128)(2,1)S(1)}, u32[]{:S(2)}, u32[]{:S(2)}) async-start(bf16[8,128,256]{2,1,0:T(8,128)(2,1)} %broadcast_in_dim.11), calls=%async_computation.3 | async-start | bytes 1048576 | tf_op jit(solution)/shard_map/all_to_all | solution.py:138
  100.7 47.5 %all-gather.2.cloned.1.call-start = ((), (), s32[]{:S(2)}) async-start(), calls=%async_computation.7 | async-start | bytes 2621440 | tf_op jit(solution)/shard_map/all_gather | solution.py:140
  114.9 0.8 copy-start.3
  133.7 20.1 %all-to-all-start.5 = ((bf16[32,24,256]{2,1,0:T(8,128)(2,1)}), bf16[32,24,256]{2,1,0:T(8,128)(2,1)S(1)}, u32[]{:S(2)}, u32[]{:S(2)}) async-start(bf16[32,24,256]{2,1,0:T(8,128)(2,1)} %broadcast_in_dim.13), calls=%async_computation.5 | async-start | bytes 786432 | tf_op jit(solution)/shard_map/all_to_all | solution.py:142
  148.3 1.6 copy-start.2
  151.4 5.5 %collective-permute-start.1 = (bf16[8,128,256]{2,1,0:T(8,128)(2,1)S(1)}, bf16[8,128,256]{2,1,0:T(8,128)(2,1)S(1)}, u32[]{:S(2)}, u32[]{:S(2)}) collective-permute-start(bf16[8,128,256]{2,1,0:T(8,128)(2,1)S(1)} %get-tuple-element.10), channel_id=1, source_target_pairs={{0,32},{32,0},{1,33},{33,1},{2,34},{34,2},{3,35},{35,3},{4,36},{36... | collective-permute-start | bytes 1572872 | tf_op jit(solution)/shard_map/ppermute | solution.py:168
  153.9 3.1 %collective-permute-start.2 = (bf16[16,256]{1,0:T(8,128)(2,1)S(1)}, bf16[16,256]{1,0:T(8,128)(2,1)S(1)}, u32[]{:S(2)}, u32[]{:S(2)}) collective-permute-start(bf16[16,256]{1,0:T(8,128)(2,1)S(1)} %slice.33), channel_id=1, source_target_pairs={{0,32},{32,0},{1,33},{33,1},{2,34},{34,2},{3,35},{35,3},{4,36},{36... | collective-permute-start | bytes 24584 | tf_op jit(solution)/shard_map/ppermute | solution.py:146
  157.1 30.1 %copy-start.4 = (f32[128]{0:T(128)S(1)}, f32[128]{0:T(128)}, u32[]{:S(2)}) copy-start(f32[128]{0:T(128)} %param.10) | copy-start | bytes 1540
  158.0 29.1 %all-to-all-start.6 = ((bf16[8,160,256]{2,1,0:T(8,128)(2,1)}), bf16[8,160,256]{2,1,0:T(8,128)(2,1)S(1)}, u32[]{:S(2)}, u32[]{:S(2)}) async-start(bf16[8,160,256]{2,1,0:T(8,128)(2,1)} %pad_maximum_fusion), calls=%async_computation.6 | async-start | bytes 1310720 | tf_op jit(solution)/shard_map/all_to_all | solution.py:170
Sparse Core Ops, SparseCore 0:
  115.8 32.3 all-gather.1

commit v6 on v4

--- a/solution.py
+++ b/solution.py
@@ -42,12 +42,13 @@
     out[...] = total[...].reshape(out.shape).astype(out.dtype)
 
 
-def backward_kernel(info, tiles, g0, g1, g2, g3, keep, send, total):
+def backward_kernel(info, tiles, g0, g1, g2_low, g2_high, g3, keep, send, total):
     slots = tiles.shape[0]
     count = info[2 * slots]
     core = info[2 * slots + 1]
     here = info[2 * slots + 2]
     n_half = keep.shape[0]
+    half_z = g2_low.shape[0]
     total[...] = jnp.zeros_like(total)
 
     def step(b, _):
@@ -58,10 +59,11 @@
             c = info[slots + k]
             z = r // 4
             d = (r % 4 - here + 4) % 4
+            far = jnp.where(z < half_z, g2_low[z % half_z], g2_high[z % half_z])
             picked = jnp.where(
                 d < 2,
                 jnp.where(d == 0, g0[z], g1[z]),
-                jnp.where(d == 2, g2[z], g3[z]),
+                jnp.where(d == 2, far, g3[z]),
             )
             product = lax.dot_general(
                 tiles[k], picked, (((0,), (0,)), ((), ())), preferred_element_type=F32
@@ -148,7 +150,11 @@
     ).astype(BF16)
     g0 = lax.all_to_all(repeat(grad_here, n_z), "z", 0, 0, tiled=True)
     g0, both = lax.optimization_barrier((g0, both))
-    g = [g0] + [lax.ppermute(g0, "x", ring(n_x, n_x - d)) for d in range(1, n_x)]
+    g1 = lax.ppermute(g0, "x", ring(n_x, n_x - 1))
+    g3 = lax.ppermute(g0, "x", ring(n_x, 1))
+    g2_low = lax.ppermute(g1[: n_z // 2], "x", ring(n_x, n_x - 1))
+    g2_high = lax.ppermute(g3[n_z // 2 :], "x", ring(n_x, 1))
+    g = [g0, g1, g2_low, g2_high, g3]
     both = jnp.sum(lax.all_to_all(both, ROW, 0, 0, tiled=True).astype(F32), axis=0)
     both = lax.all_to_all(repeat(both.astype(BF16), tile_rows), COL, 0, 0, tiled=True)
     both = jnp.sum(both.astype(F32), axis=0)
@@ -170,7 +176,7 @@
             jax.ShapeDtypeStruct((n_y, n, hidden), F32),
             jax.ShapeDtypeStruct((n_y, n, hidden), BF16),
         ),
-        in_specs=[SMEM, VMEM, VMEM, VMEM, VMEM, VMEM],
+        in_specs=[SMEM] + [VMEM] * 6,
         out_specs=(VMEM, VMEM),
         scratch_shapes=[pltpu.VMEM((tile_cols, n, hidden), F32)],
         compiler_params=pltpu.CompilerParams(vmem_limit_bytes=40 * 2**20),

time: 193 us -> 190 us (0.984)
  waiting for transfers between devices: 55 us -> 48.7 us
  blocking collectives: 76.7 us -> 79.2 us
    ppermute x3 -> x4, waiting for transfers between devices: 18 us -> 8.31 us  [the longest x1 7.73 us: body(): g2_high = lax.ppermute(g3[n_z // 2:], 'x', ring(n_x, 1))]
    ppermute x3 -> x4, starting transfers between devices: 8.43 us -> 13 us  [the longest x1 4.3 us: body(): g1 = lax.ppermute(g0, 'x', ring(n_x, n_x - 1))]
    all_to_all x1, blocking collectives: 24.2 us -> 28.2 us  [body(): terms = lax.all_to_all(over_x.astype(BF16), 'z', 0, 0, tiled=True)]
    all_to_all x1, starting transfers between devices: 8.82 us -> 6.32 us  [body(): lax.all_to_all(both, ROW, 0, 0, tiled=True).astype(F32)]
    all_to_all x1, waiting for transfers between devices: 1.87 us -> 3.88 us  [body(): lax.all_to_all(both, ROW, 0, 0, tiled=True).astype(F32)]
  transfers between devices with their start and end apart: 10 -> 11, of which waited for: 8 -> 7; matrix products, arithmetic and copies ran while one was open for 2% -> 2% of each run, Pallas kernels for 1% -> 2%
where the time goes in v6:
time: 190 us; the launch traced here: 188 us
  blocking collectives  79.2 us (42%)
  waiting for transfers between devices  48.7 us (26%)
  starting transfers between devices  43.8 us (23%)
  other arithmetic  5.15 us (3%)
  Pallas kernels  5.15 us (3%)
  local copies, waits for them, and re-layouts  2.42 us (1%)
  matrix products  2.07 us (1%)
    all_to_all x1, blocking collectives, body(): lax.all_to_all(blocks, 'x', 0, 0, tiled=True).astype(F32)  28.8 us
    all_to_all x1, blocking collectives, body(): terms = lax.all_to_all(over_x.astype(BF16), 'z', 0, 0, tiled=True)  28.2 us
    all_to_all x1, blocking collectives, body(): own = lax.all_to_all(repeat(share, n_y), 'y', 0, 0, tiled=True)  22.2 us
    all_to_all x1, waiting for transfers between devices, body(): last = lax.all_to_all(last, 'y', 0, 0, tiled=True)  20.2 us
    all_to_all x1, waiting for transfers between devices, body(): g0 = lax.all_to_all(repeat(grad_here, n_z), 'z', 0, 0, tiled=True)  14.4 us
    ppermute x1, waiting for transfers between devices, body(): g2_high = lax.ppermute(g3[n_z // 2:], 'x', ring(n_x, 1))  7.73 us
    all_to_all x1, starting transfers between devices, body(): last = lax.all_to_all(last, 'y', 0, 0, tiled=True)  6.38 us
    all_to_all x1, starting transfers between devices, body(): lax.all_to_all(both, ROW, 0, 0, tiled=True).astype(F32)  6.32 us
  transfers between devices with their start and end apart: 11, of which 7 were waited for; matrix products, arithmetic and copies ran while one was open for 2% of the time, Pallas kernels for 2%

profile of v6, /device:TPU:1, one launch (start us, length us, event | category | flops | bytes accessed | tf_op | source)
XLA Modules:
  0.0 188.1 jit_solution(985476324268618101)
XLA Ops:
  0.7 1.0 multiply_convert_fusion.3
  1.7 22.2 %all_to_all.35.own = bf16[8,128,256]{2,1,0:T(8,128)(2,1)S(1)} all-to-all(bf16[8,128,256]{2,1,0:T(8,128)(2,1)S(1)} %broadcast_in_dim.10), channel_id=1, replica_groups=mesh['y'=8,'core'=2,'z'=8,'x'=4] {'y'}, dimensions={0} | all-to-all | bytes 1048576 | tf_op jit(solution)/shard_map/all_to_all | solution.py:112
  23.9 5.6 %collective-permute-start = (bf16[8,128,256]{2,1,0:T(8,128)(2,1)S(1)}, bf16[8,128,256]{2,1,0:T(8,128)(2,1)S(1)}, u32[]{:S(2)}, u32[]{:S(2)}) collective-permute-start(bf16[8,128,256]{2,1,0:T(8,128)(2,1)S(1)} %all_to_all.35.own), channel_id=1, source_target_pairs={{0,32},{32,0},{1,33},{33,1},{2,34},{34,2},{3,35},{35,3},{4,36},{36... | collective-permute-start | bytes 1572872 | tf_op jit(solution)/shard_map/ppermute | solution.py:113
  31.0 2.2 %forward_tiles.1 = bf16[4,8,128,256]{3,2,1,0:T(8,128)(2,1)S(1)} custom-call(s32[51]{0:T(128)S(1)} %concatenate.13.info, bf16[24,128,128]{2,1,0:T(8,128)(2,1)S(1)} %bitcast.19, bf16[8,128,256]{2,1,0:T(8,128)(2,1)S(1)} %all_to_all.35.own, bf16[8,128,256]{2,1,0:T(8,128)(2,1)S(1)} %collective-permute-done.other), custom_call_target="tpu_custom_call" | custom-call | tf_op jit(solution)/shard_map/forward_tiles/pallas_call | solution.py:115
  33.3 28.8 %all_to_all.36 = bf16[4,8,128,256]{3,2,1,0:T(8,128)(2,1)S(1)} all-to-all(bf16[4,8,128,256]{3,2,1,0:T(8,128)(2,1)S(1)} %forward_tiles.1), channel_id=1, replica_groups=mesh['y'=8,'core'=2,'z'=8,'x'=4] {'x'}, dimensions={0} | all-to-all | bytes 4194304 | tf_op jit(solution)/shard_map/all_to_all | solution.py:124
  62.5 28.2 %all_to_all.37 = bf16[8,128,256]{2,1,0:T(8,128)(2,1)S(1)} all-to-all(bf16[8,128,256]{2,1,0:T(8,128)(2,1)S(1)} %reduce_sum.60), channel_id=1, replica_groups=mesh['y'=8,'core'=2,'z'=8,'x'=4] {'z'}, dimensions={0} | all-to-all | bytes 1048576 | tf_op jit(solution)/shard_map/all_to_all | solution.py:125
  92.7 3.5 %all-to-all-start.3 = ((bf16[8,128,256]{2,1,0:T(8,128)(2,1)}), bf16[8,128,256]{2,1,0:T(8,128)(2,1)S(1)}, u32[]{:S(2)}, u32[]{:S(2)}) async-start(bf16[8,128,256]{2,1,0:T(8,128)(2,1)} %broadcast_in_dim.11), calls=%async_computation.3 | async-start | bytes 1048576 | tf_op jit(solution)/shard_map/all_to_all | solution.py:151
  97.2 14.4 %all-to-all-done.3.g0 = bf16[8,128,256]{2,1,0:T(8,128)(2,1)S(1)} async-done(((bf16[8,128,256]{2,1,0:T(8,128)(2,1)}), bf16[8,128,256]{2,1,0:T(8,128)(2,1)S(1)}, u32[]{:S(2)}, u32[]{:S(2)}) %all-to-all-start.3) | async-done | bytes 524320 | tf_op jit(solution)/shard_map/all_to_all | solution.py:151
  111.6 6.3 %all-to-all-start.4 = ((bf16[16,24,256]{2,1,0:T(8,128)(2,1)}), bf16[16,24,256]{2,1,0:T(8,128)(2,1)S(1)}, u32[]{:S(2)}, u32[]{:S(2)}) async-start(bf16[16,24,256]{2,1,0:T(8,128)(2,1)} %pad_maximum_fusion.1), calls=%async_computation.4 | async-start | bytes 393216 | tf_op jit(solution)/shard_map/all_to_all | solution.py:158
  117.9 2.2 %collective-permute-start.3 = (bf16[8,128,256]{2,1,0:T(8,128)(2,1)S(1)}, bf16[8,128,256]{2,1,0:T(8,128)(2,1)S(1)}, u32[]{:S(2)}, u32[]{:S(2)}) collective-permute-start(bf16[8,128,256]{2,1,0:T(8,128)(2,1)S(1)} %all-to-all-done.3.g0), channel_id=1, source_target_pairs={{0,1},{1,2},{2,3},{3,0},{4,5},{5,6},{6,7},{7,4},{8,9},{9,10},{10,1... | collective-permute-start | bytes 1572872 | tf_op jit(solution)/shard_map/ppermute | solution.py:154
  120.1 4.3 %collective-permute-start.1 = (bf16[8,128,256]{2,1,0:T(8,128)(2,1)S(1)}, bf16[8,128,256]{2,1,0:T(8,128)(2,1)S(1)}, u32[]{:S(2)}, u32[]{:S(2)}) collective-permute-start(bf16[8,128,256]{2,1,0:T(8,128)(2,1)S(1)} %all-to-all-done.3.g0), channel_id=1, source_target_pairs={{0,3},{1,0},{2,1},{3,2},{4,7},{5,4},{6,5},{7,6},{8,11},{9,8},{10,9... | collective-permute-start | bytes 1572872 | tf_op jit(solution)/shard_map/ppermute | solution.py:153
  124.4 3.9 %all-to-all-done.4 = bf16[16,24,256]{2,1,0:T(8,128)(2,1)S(1)} async-done(((bf16[16,24,256]{2,1,0:T(8,128)(2,1)}), bf16[16,24,256]{2,1,0:T(8,128)(2,1)S(1)}, u32[]{:S(2)}, u32[]{:S(2)}) %all-to-all-start.4) | async-done | bytes 196640 | tf_op jit(solution)/shard_map/all_to_all | solution.py:158
  129.1 4.6 %all-to-all-start.5 = ((bf16[32,24,256]{2,1,0:T(8,128)(2,1)}), bf16[32,24,256]{2,1,0:T(8,128)(2,1)}, u32[]{:S(2)}, u32[]{:S(2)}) async-start(bf16[32,24,256]{2,1,0:T(8,128)(2,1)} %broadcast_in_dim.13), calls=%async_computation.5 | async-start | bytes 786432 | tf_op jit(solution)/shard_map/all_to_all | solution.py:159
  134.3 2.4 %collective-permute-start.4 = (bf16[4,128,256]{2,1,0:T(8,128)(2,1)S(1)}, bf16[4,128,256]{2,1,0:T(8,128)(2,1)S(1)}, u32[]{:S(2)}, u32[]{:S(2)}) collective-permute-start(bf16[4,128,256]{2,1,0:T(8,128)(2,1)S(1)} %slice.34), channel_id=1, source_target_pairs={{0,1},{1,2},{2,3},{3,0},{4,5},{5,6},{6,7},{7,4},{8,9},{9,10},{10,1... | collective-permute-start | bytes 786440 | tf_op jit(solution)/shard_map/ppermute | solution.py:156
  136.7 4.1 %collective-permute-start.2 = (bf16[4,128,256]{2,1,0:T(8,128)(2,1)S(1)}, bf16[4,128,256]{2,1,0:T(8,128)(2,1)S(1)}, u32[]{:S(2)}, u32[]{:S(2)}) collective-permute-start(bf16[4,128,256]{2,1,0:T(8,128)(2,1)S(1)} %slice.33), channel_id=1, source_target_pairs={{0,3},{1,0},{2,1},{3,2},{4,7},{5,4},{6,5},{7,6},{8,11},{9,8},{10,9... | collective-permute-start | bytes 786440 | tf_op jit(solution)/shard_map/ppermute | solution.py:155
  140.9 7.7 %collective-permute-done.4.g2_high = bf16[4,128,256]{2,1,0:T(8,128)(2,1)S(1)} collective-permute-done((bf16[4,128,256]{2,1,0:T(8,128)(2,1)S(1)}, bf16[4,128,256]{2,1,0:T(8,128)(2,1)S(1)}, u32[]{:S(2)}, u32[]{:S(2)}) %collective-permute-start.4) | collective-permute-done | bytes 262176 | tf_op jit(solution)/shard_map/ppermute | solution.py:156
  148.6 2.9 %backward_tiles.1 = (f32[8,128,256]{2,1,0:T(8,128)S(1)}, bf16[8,128,256]{2,1,0:T(8,128)(2,1)}) custom-call(s32[51]{0:T(128)S(1)} %concatenate.13.info, bf16[24,128,128]{2,1,0:T(8,128)(2,1)S(1)} %bitcast.20, bf16[8,128,256]{2,1,0:T(8,128)(2,1)S(1)} %all-to-all-done.3.g0, bf16[8,128,256]{2,1,0:T(8,128)(2,1)S(1)} %collective-permute-done.1.g1, ...), custom_call_target="tpu_custom_call" | custom-call | tf_op jit(solution)/shard_map/backward_tiles/pallas_call | solution.py:173
  151.5 2.5 %collective-permute-start.5 = (bf16[8,128,256]{2,1,0:T(8,128)(2,1)}, bf16[8,128,256]{2,1,0:T(8,128)(2,1)S(1)}, u32[]{:S(2)}, u32[]{:S(2)}) collective-permute-start(bf16[8,128,256]{2,1,0:T(8,128)(2,1)} %get-tuple-element.10), channel_id=1, source_target_pairs={{0,32},{32,0},{1,33},{33,1},{2,34},{34,2},{3,35},{35,3},{4,36},{36... | collective-permute-start | bytes 1572872 | tf_op jit(solution)/shard_map/ppermute | solution.py:185
  154.0 1.1 convert_reduce_fusion.2
  155.1 1.9 %collective-permute-start.6 = (bf16[16,256]{1,0:T(8,128)(2,1)S(1)}, bf16[16,256]{1,0:T(8,128)(2,1)S(1)}, u32[]{:S(2)}, u32[]{:S(2)}) collective-permute-start(bf16[16,256]{1,0:T(8,128)(2,1)S(1)} %slice.43), channel_id=1, source_target_pairs={{0,32},{32,0},{1,33},{33,1},{2,34},{34,2},{3,35},{35,3},{4,36},{36... | collective-permute-start | bytes 24584 | tf_op jit(solution)/shard_map/ppermute | solution.py:163
  157.0 1.1 collective-permute-done.6
  158.3 0.9 pad_maximum_fusion
  159.2 6.4 %all-to-all-start.6 = ((bf16[8,160,256]{2,1,0:T(8,128)(2,1)}), bf16[8,160,256]{2,1,0:T(8,128)(2,1)S(1)}, u32[]{:S(2)}, u32[]{:S(2)}) async-start(bf16[8,160,256]{2,1,0:T(8,128)(2,1)} %pad_maximum_fusion), calls=%async_computation.6 | async-start | bytes 1310720 | tf_op jit(solution)/shard_map/all_to_all | solution.py:187
  166.2 20.2 %all-to-all-done.6 = bf16[8,160,256]{2,1,0:T(8,128)(2,1)S(1)} async-done(((bf16[8,160,256]{2,1,0:T(8,128)(2,1)}), bf16[8,160,256]{2,1,0:T(8,128)(2,1)S(1)}, u32[]{:S(2)}, u32[]{:S(2)}) %all-to-all-start.6) | async-done | bytes 655392 | tf_op jit(solution)/shard_map/all_to_all | solution.py:187
  (47 shorter events, 8.0 us)
Async XLA Ops:
  0.6 90.1 %copy-start = (bf16[256,256]{1,0:T(8,128)(2,1)S(1)}, bf16[256,256]{1,0:T(8,128)(2,1)}, u32[]{:S(2)}) copy-start(bf16[256,256]{1,0:T(8,128)(2,1)} %param.11) | copy-start | bytes 393220
  0.6 29.5 %copy-start.3 = (s32[1,1,24,2]{2,3,1,0:T(2,128)S(1)}, s32[1,1,24,2]{2,3,1,0:T(2,128)}, u32[]{:S(2)}) copy-start(s32[1,1,24,2]{2,3,1,0:T(2,128)} %param.13) | copy-start | bytes 580
  0.7 30.4 %copy-start.1 = (bf16[1,1,24,128,128]{4,3,2,1,0:T(8,128)(2,1)S(1)}, bf16[1,1,24,128,128]{4,3,2,1,0:T(8,128)(2,1)}, u32[]{:S(2)}) copy-start(bf16[1,1,24,128,128]{4,3,2,1,0:T(8,128)(2,1)} %param.15) | copy-start | bytes 2359300
  23.9 7.1 %collective-permute-start = (bf16[8,128,256]{2,1,0:T(8,128)(2,1)S(1)}, bf16[8,128,256]{2,1,0:T(8,128)(2,1)S(1)}, u32[]{:S(2)}, u32[]{:S(2)}) collective-permute-start(bf16[8,128,256]{2,1,0:T(8,128)(2,1)S(1)} %all_to_all.35.own), channel_id=1, source_target_pairs={{0,32},{32,0},{1,33},{33,1},{2,34},{34,2},{3,35},{35,3},{4,36},{36... | collective-permute-start | bytes 1572872 | tf_op jit(solution)/shard_map/ppermute | solution.py:113
  62.4 28.5 %copy-start.4 = (f32[128]{0:T(128)S(1)}, f32[128]{0:T(128)}, u32[]{:S(2)}) copy-start(f32[128]{0:T(128)} %param.16) | copy-start | bytes 1540
  62.5 28.5 %copy-start.5 = (bf16[128,256]{1,0:T(8,128)(2,1)S(1)}, bf16[128,256]{1,0:T(8,128)(2,1)}, u32[]{:S(2)}) copy-start(bf16[128,256]{1,0:T(8,128)(2,1)} %param.17) | copy-start | bytes 196612
  62.5 28.5 %copy-start.6 = (f32[256]{0:T(256)S(1)}, f32[256]{0:T(256)}, u32[]{:S(2)}) copy-start(f32[256]{0:T(256)} %param.12) | copy-start | bytes 3076
  92.7 18.9 %all-to-all-start.3 = ((bf16[8,128,256]{2,1,0:T(8,128)(2,1)}), bf16[8,128,256]{2,1,0:T(8,128)(2,1)S(1)}, u32[]{:S(2)}, u32[]{:S(2)}) async-start(bf16[8,128,256]{2,1,0:T(8,128)(2,1)} %broadcast_in_dim.11), calls=%async_computation.3 | async-start | bytes 1048576 | tf_op jit(solution)/shard_map/all_to_all | solution.py:151
  111.6 16.7 %all-to-all-start.4 = ((bf16[16,24,256]{2,1,0:T(8,128)(2,1)}), bf16[16,24,256]{2,1,0:T(8,128)(2,1)S(1)}, u32[]{:S(2)}, u32[]{:S(2)}) async-start(bf16[16,24,256]{2,1,0:T(8,128)(2,1)} %pad_maximum_fusion.1), calls=%async_computation.4 | async-start | bytes 393216 | tf_op jit(solution)/shard_map/all_to_all | solution.py:158
  117.9 16.4 %collective-permute-start.3 = (bf16[8,128,256]{2,1,0:T(8,128)(2,1)S(1)}, bf16[8,128,256]{2,1,0:T(8,128)(2,1)S(1)}, u32[]{:S(2)}, u32[]{:S(2)}) collective-permute-start(bf16[8,128,256]{2,1,0:T(8,128)(2,1)S(1)} %all-to-all-done.3.g0), channel_id=1, source_target_pairs={{0,1},{1,2},{2,3},{3,0},{4,5},{5,6},{6,7},{7,4},{8,9},{9,10},{10,1... | collective-permute-start | bytes 1572872 | tf_op jit(solution)/shard_map/ppermute | solution.py:154
  120.1 16.6 %collective-permute-start.1 = (bf16[8,128,256]{2,1,0:T(8,128)(2,1)S(1)}, bf16[8,128,256]{2,1,0:T(8,128)(2,1)S(1)}, u32[]{:S(2)}, u32[]{:S(2)}) collective-permute-start(bf16[8,128,256]{2,1,0:T(8,128)(2,1)S(1)} %all-to-all-done.3.g0), channel_id=1, source_target_pairs={{0,3},{1,0},{2,1},{3,2},{4,7},{5,4},{6,5},{7,6},{8,11},{9,8},{10,9... | collective-permute-start | bytes 1572872 | tf_op jit(solution)/shard_map/ppermute | solution.py:153
  129.1 24.9 %all-to-all-start.5 = ((bf16[32,24,256]{2,1,0:T(8,128)(2,1)}), bf16[32,24,256]{2,1,0:T(8,128)(2,1)}, u32[]{:S(2)}, u32[]{:S(2)}) async-start(bf16[32,24,256]{2,1,0:T(8,128)(2,1)} %broadcast_in_dim.13), calls=%async_computation.5 | async-start | bytes 786432 | tf_op jit(solution)/shard_map/all_to_all | solution.py:159
  134.3 14.3 %collective-permute-start.4 = (bf16[4,128,256]{2,1,0:T(8,128)(2,1)S(1)}, bf16[4,128,256]{2,1,0:T(8,128)(2,1)S(1)}, u32[]{:S(2)}, u32[]{:S(2)}) collective-permute-start(bf16[4,128,256]{2,1,0:T(8,128)(2,1)S(1)} %slice.34), channel_id=1, source_target_pairs={{0,1},{1,2},{2,3},{3,0},{4,5},{5,6},{6,7},{7,4},{8,9},{9,10},{10,1... | collective-permute-start | bytes 786440 | tf_op jit(solution)/shard_map/ppermute | solution.py:156
  136.7 11.8 %collective-permute-start.2 = (bf16[4,128,256]{2,1,0:T(8,128)(2,1)S(1)}, bf16[4,128,256]{2,1,0:T(8,128)(2,1)S(1)}, u32[]{:S(2)}, u32[]{:S(2)}) collective-permute-start(bf16[4,128,256]{2,1,0:T(8,128)(2,1)S(1)} %slice.33), channel_id=1, source_target_pairs={{0,3},{1,0},{2,1},{3,2},{4,7},{5,4},{6,5},{7,6},{8,11},{9,8},{10,9... | collective-permute-start | bytes 786440 | tf_op jit(solution)/shard_map/ppermute | solution.py:155
  151.5 6.7 %collective-permute-start.5 = (bf16[8,128,256]{2,1,0:T(8,128)(2,1)}, bf16[8,128,256]{2,1,0:T(8,128)(2,1)S(1)}, u32[]{:S(2)}, u32[]{:S(2)}) collective-permute-start(bf16[8,128,256]{2,1,0:T(8,128)(2,1)} %get-tuple-element.10), channel_id=1, source_target_pairs={{0,32},{32,0},{1,33},{33,1},{2,34},{34,2},{3,35},{35,3},{4,36},{36... | collective-permute-start | bytes 1572872 | tf_op jit(solution)/shard_map/ppermute | solution.py:185
  155.1 3.1 %collective-permute-start.6 = (bf16[16,256]{1,0:T(8,128)(2,1)S(1)}, bf16[16,256]{1,0:T(8,128)(2,1)S(1)}, u32[]{:S(2)}, u32[]{:S(2)}) collective-permute-start(bf16[16,256]{1,0:T(8,128)(2,1)S(1)} %slice.43), channel_id=1, source_target_pairs={{0,32},{32,0},{1,33},{33,1},{2,34},{34,2},{3,35},{35,3},{4,36},{36... | collective-permute-start | bytes 24584 | tf_op jit(solution)/shard_map/ppermute | solution.py:163
  159.2 27.2 %copy-start.2 = (f32[128]{0:T(128)S(1)}, f32[128]{0:T(128)}, u32[]{:S(2)}) copy-start(f32[128]{0:T(128)} %param.10) | copy-start | bytes 1540
  159.2 27.2 %all-to-all-start.6 = ((bf16[8,160,256]{2,1,0:T(8,128)(2,1)}), bf16[8,160,256]{2,1,0:T(8,128)(2,1)S(1)}, u32[]{:S(2)}, u32[]{:S(2)}) async-start(bf16[8,160,256]{2,1,0:T(8,128)(2,1)} %pad_maximum_fusion), calls=%async_computation.6 | async-start | bytes 1310720 | tf_op jit(solution)/shard_map/all_to_all | solution.py:187

commit v7 on v6

--- a/solution.py
+++ b/solution.py
@@ -160,15 +160,6 @@
     both = jnp.sum(both.astype(F32), axis=0)
     grad_bias = both[chunk]
     chunk_here = both[:chunk].astype(BF16)
-    chunk_other = lax.ppermute(chunk_here, "core", swap)
-    first = lax.axis_index("core") == 0
-    chunks = jnp.concatenate(
-        [
-            jnp.where(first, chunk_here, chunk_other),
-            jnp.where(first, chunk_other, chunk_here),
-        ],
-        axis=0,
-    )
 
     keep, send = pl.pallas_call(
         backward_kernel,
@@ -183,10 +174,16 @@
         name="backward_tiles",
     )(info, tiles, *g)
     pair = (keep + lax.ppermute(send, "core", swap).astype(F32)).astype(BF16)
-    last = jnp.concatenate([pair, repeat(chunks, n_y)], axis=1)
+    last = jnp.concatenate([pair, repeat(chunk_here, n_y)], axis=1)
     last = lax.all_to_all(last, "y", 0, 0, tiled=True)
     column_total = jnp.sum(last[:, :n].astype(F32), axis=0)
-    grad_weight = last[:, n:].reshape(hidden, hidden).astype(F32)
+    chunks = last[:, n:]
+    chunks_other = lax.ppermute(chunks, "core", swap)
+    first = lax.axis_index("core") == 0
+    grad_weight = jnp.concatenate(
+        [jnp.where(first, chunks, chunks_other), jnp.where(first, chunks_other, chunks)], axis=1
+    )
+    grad_weight = grad_weight.reshape(hidden, hidden).astype(F32)
     grad_mixed = (col_norm[:, None] * column_total).astype(BF16)
     grad_features = lax.dot_general(
         grad_mixed, weight, (((1,), (1,)), ((), ())), preferred_element_type=F32

time: 190 us -> 189 us (level)
  blocking collectives: 79.2 us -> 95.8 us
  starting transfers between devices: 43.8 us -> 35 us
  waiting for transfers between devices: 48.7 us -> 42.3 us
    all_to_all x0 -> x1, blocking collectives: none -> 18.6 us  [body(): lax.all_to_all(both, ROW, 0, 0, tiled=True).astype(F32)]
    all_to_all x1 -> x0, starting transfers between devices: 6.32 us -> none  [body(): lax.all_to_all(both, ROW, 0, 0, tiled=True).astype(F32)]
    all_to_all x1 -> x0, waiting for transfers between devices: 3.88 us -> none  [body(): lax.all_to_all(both, ROW, 0, 0, tiled=True).astype(F32)]
    all_to_all x1, blocking collectives: 28.2 us -> 25.1 us  [body(): terms = lax.all_to_all(over_x.astype(BF16), 'z', 0, 0, tiled=True)]
    all_to_all x1, starting transfers between devices: 6.38 us -> 3.67 us  [body(): last = lax.all_to_all(last, 'y', 0, 0, tiled=True)]
  transfers between devices with their start and end apart: 11 -> 10, of which waited for: 7 -> 5; matrix products, arithmetic and copies ran while one was open for 2% -> 2% of each run, Pallas kernels for 2% -> 1%
where the time goes in v7:
time: 189 us; the launch traced here: 188 us
  blocking collectives  95.8 us (51%)
  waiting for transfers between devices  42.3 us (22%)
  starting transfers between devices  35 us (19%)
  Pallas kernels  4.62 us (2%)
  other arithmetic  4.46 us (2%)
  local copies, waits for them, and re-layouts  2.4 us (1%)
  matrix products  2.07 us (1%)
    all_to_all x1, blocking collectives, body(): lax.all_to_all(blocks, 'x', 0, 0, tiled=True).astype(F32)  29.9 us
    all_to_all x1, blocking collectives, body(): terms = lax.all_to_all(over_x.astype(BF16), 'z', 0, 0, tiled=True)  25.1 us
    all_to_all x1, blocking collectives, body(): own = lax.all_to_all(repeat(share, n_y), 'y', 0, 0, tiled=True)  22.2 us
    all_to_all x1, waiting for transfers between devices, body(): last = lax.all_to_all(last, 'y', 0, 0, tiled=True)  18.8 us
    all_to_all x1, blocking collectives, body(): lax.all_to_all(both, ROW, 0, 0, tiled=True).astype(F32)  18.6 us
    all_to_all x1, waiting for transfers between devices, body(): g0 = lax.all_to_all(repeat(grad_here, n_z), 'z', 0, 0, tiled=True)  13.9 us
    ppermute x1, waiting for transfers between devices, body(): g2_high = lax.ppermute(g3[n_z // 2:], 'x', ring(n_x, 1))  8.24 us
    ppermute x1, starting transfers between devices, body(): other = lax.ppermute(own, 'core', swap)  5.6 us
  transfers between devices with their start and end apart: 10, of which 5 were waited for; matrix products, arithmetic and copies ran while one was open for 2% of the time, Pallas kernels for 1%

profile of v7, /device:TPU:1, one launch (start us, length us, event | category | flops | bytes accessed | tf_op | source)
XLA Modules:
  0.0 188.3 jit_solution(10019035061465138277)
XLA Ops:
  0.7 1.0 multiply_convert_fusion.3
  1.7 22.2 %all_to_all.35.own = bf16[8,128,256]{2,1,0:T(8,128)(2,1)S(1)} all-to-all(bf16[8,128,256]{2,1,0:T(8,128)(2,1)S(1)} %broadcast_in_dim.10), channel_id=1, replica_groups=mesh['y'=8,'core'=2,'z'=8,'x'=4] {'y'}, dimensions={0} | all-to-all | bytes 1048576 | tf_op jit(solution)/shard_map/all_to_all | solution.py:112
  23.9 5.6 %collective-permute-start = (bf16[8,128,256]{2,1,0:T(8,128)(2,1)S(1)}, bf16[8,128,256]{2,1,0:T(8,128)(2,1)S(1)}, u32[]{:S(2)}, u32[]{:S(2)}) collective-permute-start(bf16[8,128,256]{2,1,0:T(8,128)(2,1)S(1)} %all_to_all.35.own), channel_id=1, source_target_pairs={{0,32},{32,0},{1,33},{33,1},{2,34},{34,2},{3,35},{35,3},{4,36},{36... | collective-permute-start | bytes 1572872 | tf_op jit(solution)/shard_map/ppermute | solution.py:113
  31.0 2.0 %forward_tiles.1 = bf16[4,8,128,256]{3,2,1,0:T(8,128)(2,1)S(1)} custom-call(s32[51]{0:T(128)S(1)} %concatenate.13.info, bf16[24,128,128]{2,1,0:T(8,128)(2,1)S(1)} %bitcast.19, bf16[8,128,256]{2,1,0:T(8,128)(2,1)S(1)} %all_to_all.35.own, bf16[8,128,256]{2,1,0:T(8,128)(2,1)S(1)} %collective-permute-done.other), custom_call_target="tpu_custom_call" | custom-call | tf_op jit(solution)/shard_map/forward_tiles/pallas_call | solution.py:115
  33.0 29.9 %all_to_all.36 = bf16[4,8,128,256]{3,2,1,0:T(8,128)(2,1)S(1)} all-to-all(bf16[4,8,128,256]{3,2,1,0:T(8,128)(2,1)S(1)} %forward_tiles.1), channel_id=1, replica_groups=mesh['y'=8,'core'=2,'z'=8,'x'=4] {'x'}, dimensions={0} | all-to-all | bytes 4194304 | tf_op jit(solution)/shard_map/all_to_all | solution.py:124
  63.3 25.1 %all_to_all.37 = bf16[8,128,256]{2,1,0:T(8,128)(2,1)S(1)} all-to-all(bf16[8,128,256]{2,1,0:T(8,128)(2,1)S(1)} %reduce_sum.60), channel_id=1, replica_groups=mesh['y'=8,'core'=2,'z'=8,'x'=4] {'z'}, dimensions={0} | all-to-all | bytes 1048576 | tf_op jit(solution)/shard_map/all_to_all | solution.py:125
  88.8 0.9 fusion.8
  90.5 3.5 %all-to-all-start.3 = ((bf16[8,128,256]{2,1,0:T(8,128)(2,1)}), bf16[8,128,256]{2,1,0:T(8,128)(2,1)S(1)}, u32[]{:S(2)}, u32[]{:S(2)}) async-start(bf16[8,128,256]{2,1,0:T(8,128)(2,1)} %broadcast_in_dim.11), calls=%async_computation.3 | async-start | bytes 1048576 | tf_op jit(solution)/shard_map/all_to_all | solution.py:151
  94.3 13.9 %all-to-all-done.3.g0 = bf16[8,128,256]{2,1,0:T(8,128)(2,1)S(1)} async-done(((bf16[8,128,256]{2,1,0:T(8,128)(2,1)}), bf16[8,128,256]{2,1,0:T(8,128)(2,1)S(1)}, u32[]{:S(2)}, u32[]{:S(2)}) %all-to-all-start.3) | async-done | bytes 524320 | tf_op jit(solution)/shard_map/all_to_all | solution.py:151
  108.2 2.2 %collective-permute-start.3 = (bf16[8,128,256]{2,1,0:T(8,128)(2,1)S(1)}, bf16[8,128,256]{2,1,0:T(8,128)(2,1)S(1)}, u32[]{:S(2)}, u32[]{:S(2)}) collective-permute-start(bf16[8,128,256]{2,1,0:T(8,128)(2,1)S(1)} %all-to-all-done.3.g0), channel_id=1, source_target_pairs={{0,1},{1,2},{2,3},{3,0},{4,5},{5,6},{6,7},{7,4},{8,9},{9,10},{10,1... | collective-permute-start | bytes 1572872 | tf_op jit(solution)/shard_map/ppermute | solution.py:154
  110.4 4.3 %collective-permute-start.1 = (bf16[8,128,256]{2,1,0:T(8,128)(2,1)S(1)}, bf16[8,128,256]{2,1,0:T(8,128)(2,1)S(1)}, u32[]{:S(2)}, u32[]{:S(2)}) collective-permute-start(bf16[8,128,256]{2,1,0:T(8,128)(2,1)S(1)} %all-to-all-done.3.g0), channel_id=1, source_target_pairs={{0,3},{1,0},{2,1},{3,2},{4,7},{5,4},{6,5},{7,6},{8,11},{9,8},{10,9... | collective-permute-start | bytes 1572872 | tf_op jit(solution)/shard_map/ppermute | solution.py:153
  114.7 18.6 %all_to_all.38 = bf16[16,24,256]{2,1,0:T(8,128)(2,1)S(1)} all-to-all(bf16[16,24,256]{2,1,0:T(8,128)(2,1)S(1)} %pad_maximum_fusion.1), channel_id=1, replica_groups=mesh['y'=8,'core'=2,'z'=8,'x'=4] {'y','core'}, dimensions={0} | all-to-all | bytes 393216 | tf_op jit(solution)/shard_map/all_to_all | solution.py:158
  134.1 4.6 %all-to-all-start.5 = ((bf16[32,24,256]{2,1,0:T(8,128)(2,1)}), bf16[32,24,256]{2,1,0:T(8,128)(2,1)}, u32[]{:S(2)}, u32[]{:S(2)}) async-start(bf16[32,24,256]{2,1,0:T(8,128)(2,1)} %broadcast_in_dim.13), calls=%async_computation.5 | async-start | bytes 786432 | tf_op jit(solution)/shard_map/all_to_all | solution.py:159
  138.7 3.0 %collective-permute-start.4 = (bf16[4,128,256]{2,1,0:T(8,128)(2,1)S(1)}, bf16[4,128,256]{2,1,0:T(8,128)(2,1)S(1)}, u32[]{:S(2)}, u32[]{:S(2)}) collective-permute-start(bf16[4,128,256]{2,1,0:T(8,128)(2,1)S(1)} %slice.34), channel_id=1, source_target_pairs={{0,1},{1,2},{2,3},{3,0},{4,5},{5,6},{6,7},{7,4},{8,9},{9,10},{10,1... | collective-permute-start | bytes 786440 | tf_op jit(solution)/shard_map/ppermute | solution.py:156
  141.7 3.5 %collective-permute-start.2 = (bf16[4,128,256]{2,1,0:T(8,128)(2,1)S(1)}, bf16[4,128,256]{2,1,0:T(8,128)(2,1)S(1)}, u32[]{:S(2)}, u32[]{:S(2)}) collective-permute-start(bf16[4,128,256]{2,1,0:T(8,128)(2,1)S(1)} %slice.33), channel_id=1, source_target_pairs={{0,3},{1,0},{2,1},{3,2},{4,7},{5,4},{6,5},{7,6},{8,11},{9,8},{10,9... | collective-permute-start | bytes 786440 | tf_op jit(solution)/shard_map/ppermute | solution.py:155
  145.2 8.2 %collective-permute-done.4.g2_high = bf16[4,128,256]{2,1,0:T(8,128)(2,1)S(1)} collective-permute-done((bf16[4,128,256]{2,1,0:T(8,128)(2,1)S(1)}, bf16[4,128,256]{2,1,0:T(8,128)(2,1)S(1)}, u32[]{:S(2)}, u32[]{:S(2)}) %collective-permute-start.4) | collective-permute-done | bytes 262176 | tf_op jit(solution)/shard_map/ppermute | solution.py:156
  153.5 2.6 %backward_tiles.1 = (f32[8,128,256]{2,1,0:T(8,128)S(1)}, bf16[8,128,256]{2,1,0:T(8,128)(2,1)}) custom-call(s32[51]{0:T(128)S(1)} %concatenate.13.info, bf16[24,128,128]{2,1,0:T(8,128)(2,1)S(1)} %bitcast.20, bf16[8,128,256]{2,1,0:T(8,128)(2,1)S(1)} %all-to-all-done.3.g0, bf16[8,128,256]{2,1,0:T(8,128)(2,1)S(1)} %collective-permute-done.1.g1, ...), custom_call_target="tpu_custom_call" | custom-call | tf_op jit(solution)/shard_map/backward_tiles/pallas_call | solution.py:164
  156.1 2.3 %collective-permute-start.5 = (bf16[8,128,256]{2,1,0:T(8,128)(2,1)}, bf16[8,128,256]{2,1,0:T(8,128)(2,1)S(1)}, u32[]{:S(2)}, u32[]{:S(2)}) collective-permute-start(bf16[8,128,256]{2,1,0:T(8,128)(2,1)} %get-tuple-element.10), channel_id=1, source_target_pairs={{0,32},{32,0},{1,33},{33,1},{2,34},{34,2},{3,35},{35,3},{4,36},{36... | collective-permute-start | bytes 1572872 | tf_op jit(solution)/shard_map/ppermute | solution.py:176
  158.5 1.1 convert_reduce_fusion.2
  160.3 0.9 pad_maximum_fusion
  161.2 3.7 %all-to-all-start.6 = ((bf16[8,144,256]{2,1,0:T(8,128)(2,1)}), bf16[8,144,256]{2,1,0:T(8,128)(2,1)S(1)}, u32[]{:S(2)}, u32[]{:S(2)}) async-start(bf16[8,144,256]{2,1,0:T(8,128)(2,1)} %pad_maximum_fusion), calls=%async_computation.6 | async-start | bytes 1179648 | tf_op jit(solution)/shard_map/all_to_all | solution.py:178
  165.5 18.8 %all-to-all-done.6 = bf16[8,144,256]{2,1,0:T(8,128)(2,1)S(1)} async-done(((bf16[8,144,256]{2,1,0:T(8,128)(2,1)}), bf16[8,144,256]{2,1,0:T(8,128)(2,1)S(1)}, u32[]{:S(2)}, u32[]{:S(2)}) %all-to-all-start.6) | async-done | bytes 589856 | tf_op jit(solution)/shard_map/all_to_all | solution.py:178
  184.2 2.4 %collective-permute-start.6 = (bf16[8,16,256]{2,1,0:T(8,128)(2,1)S(1)}, bf16[8,16,256]{2,1,0:T(8,128)(2,1)S(1)}, u32[]{:S(2)}, u32[]{:S(2)}) collective-permute-start(bf16[8,16,256]{2,1,0:T(8,128)(2,1)S(1)} %slice.37), channel_id=1, source_target_pairs={{0,32},{32,0},{1,33},{33,1},{2,34},{34,2},{3,35},{35,3},{4,36},{36... | collective-permute-start | bytes 196616 | tf_op jit(solution)/shard_map/ppermute | solution.py:181
  186.7 0.8 convolution_convert_fusion
  (46 shorter events, 5.7 us)
Async XLA Ops:
  0.6 87.9 %copy-start = (bf16[256,256]{1,0:T(8,128)(2,1)S(1)}, bf16[256,256]{1,0:T(8,128)(2,1)}, u32[]{:S(2)}) copy-start(bf16[256,256]{1,0:T(8,128)(2,1)} %param.11) | copy-start | bytes 393220
  0.6 29.5 %copy-start.3 = (s32[1,1,24,2]{2,3,1,0:T(2,128)S(1)}, s32[1,1,24,2]{2,3,1,0:T(2,128)}, u32[]{:S(2)}) copy-start(s32[1,1,24,2]{2,3,1,0:T(2,128)} %param.13) | copy-start | bytes 580
  0.7 30.4 %copy-start.1 = (bf16[1,1,24,128,128]{4,3,2,1,0:T(8,128)(2,1)S(1)}, bf16[1,1,24,128,128]{4,3,2,1,0:T(8,128)(2,1)}, u32[]{:S(2)}) copy-start(bf16[1,1,24,128,128]{4,3,2,1,0:T(8,128)(2,1)} %param.15) | copy-start | bytes 2359300
  23.9 7.1 %collective-permute-start = (bf16[8,128,256]{2,1,0:T(8,128)(2,1)S(1)}, bf16[8,128,256]{2,1,0:T(8,128)(2,1)S(1)}, u32[]{:S(2)}, u32[]{:S(2)}) collective-permute-start(bf16[8,128,256]{2,1,0:T(8,128)(2,1)S(1)} %all_to_all.35.own), channel_id=1, source_target_pairs={{0,32},{32,0},{1,33},{33,1},{2,34},{34,2},{3,35},{35,3},{4,36},{36... | collective-permute-start | bytes 1572872 | tf_op jit(solution)/shard_map/ppermute | solution.py:113
  63.3 25.4 %copy-start.4 = (f32[128]{0:T(128)S(1)}, f32[128]{0:T(128)}, u32[]{:S(2)}) copy-start(f32[128]{0:T(128)} %param.16) | copy-start | bytes 1540
  63.3 25.4 %copy-start.5 = (bf16[128,256]{1,0:T(8,128)(2,1)S(1)}, bf16[128,256]{1,0:T(8,128)(2,1)}, u32[]{:S(2)}) copy-start(bf16[128,256]{1,0:T(8,128)(2,1)} %param.17) | copy-start | bytes 196612
  63.3 25.4 %copy-start.6 = (f32[256]{0:T(256)S(1)}, f32[256]{0:T(256)}, u32[]{:S(2)}) copy-start(f32[256]{0:T(256)} %param.12) | copy-start | bytes 3076
  90.5 17.7 %all-to-all-start.3 = ((bf16[8,128,256]{2,1,0:T(8,128)(2,1)}), bf16[8,128,256]{2,1,0:T(8,128)(2,1)S(1)}, u32[]{:S(2)}, u32[]{:S(2)}) async-start(bf16[8,128,256]{2,1,0:T(8,128)(2,1)} %broadcast_in_dim.11), calls=%async_computation.3 | async-start | bytes 1048576 | tf_op jit(solution)/shard_map/all_to_all | solution.py:151
  108.2 30.5 %collective-permute-start.3 = (bf16[8,128,256]{2,1,0:T(8,128)(2,1)S(1)}, bf16[8,128,256]{2,1,0:T(8,128)(2,1)S(1)}, u32[]{:S(2)}, u32[]{:S(2)}) collective-permute-start(bf16[8,128,256]{2,1,0:T(8,128)(2,1)S(1)} %all-to-all-done.3.g0), channel_id=1, source_target_pairs={{0,1},{1,2},{2,3},{3,0},{4,5},{5,6},{6,7},{7,4},{8,9},{9,10},{10,1... | collective-permute-start | bytes 1572872 | tf_op jit(solution)/shard_map/ppermute | solution.py:154
  110.4 31.3 %collective-permute-start.1 = (bf16[8,128,256]{2,1,0:T(8,128)(2,1)S(1)}, bf16[8,128,256]{2,1,0:T(8,128)(2,1)S(1)}, u32[]{:S(2)}, u32[]{:S(2)}) collective-permute-start(bf16[8,128,256]{2,1,0:T(8,128)(2,1)S(1)} %all-to-all-done.3.g0), channel_id=1, source_target_pairs={{0,3},{1,0},{2,1},{3,2},{4,7},{5,4},{6,5},{7,6},{8,11},{9,8},{10,9... | collective-permute-start | bytes 1572872 | tf_op jit(solution)/shard_map/ppermute | solution.py:153
  134.1 24.4 %all-to-all-start.5 = ((bf16[32,24,256]{2,1,0:T(8,128)(2,1)}), bf16[32,24,256]{2,1,0:T(8,128)(2,1)}, u32[]{:S(2)}, u32[]{:S(2)}) async-start(bf16[32,24,256]{2,1,0:T(8,128)(2,1)} %broadcast_in_dim.13), calls=%async_computation.5 | async-start | bytes 786432 | tf_op jit(solution)/shard_map/all_to_all | solution.py:159
  138.7 14.8 %collective-permute-start.4 = (bf16[4,128,256]{2,1,0:T(8,128)(2,1)S(1)}, bf16[4,128,256]{2,1,0:T(8,128)(2,1)S(1)}, u32[]{:S(2)}, u32[]{:S(2)}) collective-permute-start(bf16[4,128,256]{2,1,0:T(8,128)(2,1)S(1)} %slice.34), channel_id=1, source_target_pairs={{0,1},{1,2},{2,3},{3,0},{4,5},{5,6},{6,7},{7,4},{8,9},{9,10},{10,1... | collective-permute-start | bytes 786440 | tf_op jit(solution)/shard_map/ppermute | solution.py:156
  141.7 11.8 %collective-permute-start.2 = (bf16[4,128,256]{2,1,0:T(8,128)(2,1)S(1)}, bf16[4,128,256]{2,1,0:T(8,128)(2,1)S(1)}, u32[]{:S(2)}, u32[]{:S(2)}) collective-permute-start(bf16[4,128,256]{2,1,0:T(8,128)(2,1)S(1)} %slice.33), channel_id=1, source_target_pairs={{0,3},{1,0},{2,1},{3,2},{4,7},{5,4},{6,5},{7,6},{8,11},{9,8},{10,9... | collective-permute-start | bytes 786440 | tf_op jit(solution)/shard_map/ppermute | solution.py:155
  156.1 4.1 %collective-permute-start.5 = (bf16[8,128,256]{2,1,0:T(8,128)(2,1)}, bf16[8,128,256]{2,1,0:T(8,128)(2,1)S(1)}, u32[]{:S(2)}, u32[]{:S(2)}) collective-permute-start(bf16[8,128,256]{2,1,0:T(8,128)(2,1)} %get-tuple-element.10), channel_id=1, source_target_pairs={{0,32},{32,0},{1,33},{33,1},{2,34},{34,2},{3,35},{35,3},{4,36},{36... | collective-permute-start | bytes 1572872 | tf_op jit(solution)/shard_map/ppermute | solution.py:176
  161.2 25.5 %copy-start.2 = (f32[128]{0:T(128)S(1)}, f32[128]{0:T(128)}, u32[]{:S(2)}) copy-start(f32[128]{0:T(128)} %param.10) | copy-start | bytes 1540
  161.2 23.0 %all-to-all-start.6 = ((bf16[8,144,256]{2,1,0:T(8,128)(2,1)}), bf16[8,144,256]{2,1,0:T(8,128)(2,1)S(1)}, u32[]{:S(2)}, u32[]{:S(2)}) async-start(bf16[8,144,256]{2,1,0:T(8,128)(2,1)} %pad_maximum_fusion), calls=%async_computation.6 | async-start | bytes 1179648 | tf_op jit(solution)/shard_map/all_to_all | solution.py:178
  184.2 3.3 %collective-permute-start.6 = (bf16[8,16,256]{2,1,0:T(8,128)(2,1)S(1)}, bf16[8,16,256]{2,1,0:T(8,128)(2,1)S(1)}, u32[]{:S(2)}, u32[]{:S(2)}) collective-permute-start(bf16[8,16,256]{2,1,0:T(8,128)(2,1)S(1)} %slice.37), channel_id=1, source_target_pairs={{0,32},{32,0},{1,33},{33,1},{2,34},{34,2},{3,35},{35,3},{4,36},{36... | collective-permute-start | bytes 196616 | tf_op jit(solution)/shard_map/ppermute | solution.py:181

commit v8 on v7

--- a/solution.py
+++ b/solution.py
@@ -139,12 +139,22 @@
     weight_part = lax.dot_general(
         high, grad_here, (((0,), (0,)), ((), ())), preferred_element_type=F32
     )
-    bias_part = jnp.sum(grad_pre, axis=0)
+    bias_part = jnp.sum(grad_pre, axis=0) * scale
     chunk = hidden // tile_cols
+    first = lax.axis_index("core") == 0
+    pairs = (weight_part * scale).reshape(n_y, n_core, chunk, hidden)
+    away = jnp.concatenate(
+        [
+            jnp.where(first, pairs[:, 1], pairs[:, 0]),
+            jnp.broadcast_to(bias_part, (1, chunk, hidden)),
+        ],
+        axis=0,
+    ).astype(BF16)
+    away = lax.ppermute(away, "core", swap).astype(F32)
     both = jnp.concatenate(
         [
-            (weight_part * scale).reshape(tile_cols, chunk, hidden),
-            jnp.broadcast_to(bias_part * scale, (tile_cols, 8, hidden)),
+            jnp.where(first, pairs[:, 0], pairs[:, 1]) + away[:n_y],
+            jnp.broadcast_to(bias_part + away[n_y, 0], (n_y, 8, hidden)),
         ],
         axis=1,
     ).astype(BF16)
@@ -155,7 +165,7 @@
     g2_low = lax.ppermute(g1[: n_z // 2], "x", ring(n_x, n_x - 1))
     g2_high = lax.ppermute(g3[n_z // 2 :], "x", ring(n_x, 1))
     g = [g0, g1, g2_low, g2_high, g3]
-    both = jnp.sum(lax.all_to_all(both, ROW, 0, 0, tiled=True).astype(F32), axis=0)
+    both = jnp.sum(lax.all_to_all(both, "y", 0, 0, tiled=True).astype(F32), axis=0)
     both = lax.all_to_all(repeat(both.astype(BF16), tile_rows), COL, 0, 0, tiled=True)
     both = jnp.sum(both.astype(F32), axis=0)
     grad_bias = both[chunk]
@@ -179,7 +189,6 @@
     column_total = jnp.sum(last[:, :n].astype(F32), axis=0)
     chunks = last[:, n:]
     chunks_other = lax.ppermute(chunks, "core", swap)
-    first = lax.axis_index("core") == 0
     grad_weight = jnp.concatenate(
         [jnp.where(first, chunks, chunks_other), jnp.where(first, chunks_other, chunks)], axis=1
     )

time: 189 us -> 190 us (level)
  blocking collectives: 95.8 us -> 62 us
  waiting for transfers between devices: 42.3 us -> 60.8 us
  starting transfers between devices: 35 us -> 50.8 us
    all_to_all x2 -> x1, blocking collectives: 43.7 us -> 10.1 us  [body(): lax.all_to_all(both, 'y', 0, 0, tiled=True).astype(F32)]
    all_to_all x0 -> x1, waiting for transfers between devices: none -> 18 us  [body(): terms = lax.all_to_all(over_x.astype(BF16), 'z', 0, 0, tiled=True)]
    all_to_all x0 -> x1, starting transfers between devices: none -> 11.8 us  [body(): terms = lax.all_to_all(over_x.astype(BF16), 'z', 0, 0, tiled=True)]
    ppermute x0 -> x1, starting transfers between devices: none -> 2.4 us  [body(): away = lax.ppermute(away, 'core', swap).astype(F32)]
  transfers between devices with their start and end apart: 10 -> 12, of which waited for: 5 -> 8; matrix products, arithmetic and copies ran while one was open for 2% -> 2% of each run, Pallas kernels for 1% -> 1%
where the time goes in v8:
time: 190 us; the launch traced here: 189 us
  blocking collectives  62 us (33%)
  waiting for transfers between devices  60.8 us (32%)
  starting transfers between devices  50.8 us (27%)
  other arithmetic  5.4 us (3%)
  Pallas kernels  3.58 us (2%)
  local copies, waits for them, and re-layouts  2.41 us (1%)
  matrix products  2.07 us (1%)
    all_to_all x1, blocking collectives, body(): lax.all_to_all(blocks, 'x', 0, 0, tiled=True).astype(F32)  29.7 us
    all_to_all x1, blocking collectives, body(): own = lax.all_to_all(repeat(share, n_y), 'y', 0, 0, tiled=True)  22.2 us
    all_to_all x1, waiting for transfers between devices, body(): last = lax.all_to_all(last, 'y', 0, 0, tiled=True)  18.8 us
    all_to_all x1, waiting for transfers between devices, body(): terms = lax.all_to_all(over_x.astype(BF16), 'z', 0, 0, tiled=True)  18 us
    all_to_all x1, waiting for transfers between devices, body(): g0 = lax.all_to_all(repeat(grad_here, n_z), 'z', 0, 0, tiled=True)  14.4 us
    all_to_all x1, starting transfers between devices, body(): terms = lax.all_to_all(over_x.astype(BF16), 'z', 0, 0, tiled=True)  11.8 us
    all_to_all x1, blocking collectives, body(): lax.all_to_all(both, 'y', 0, 0, tiled=True).astype(F32)  10.1 us
    ppermute x1, waiting for transfers between devices, body(): g2_high = lax.ppermute(g3[n_z // 2:], 'x', ring(n_x, 1))  6.98 us
  transfers between devices with their start and end apart: 12, of which 8 were waited for; matrix products, arithmetic and copies ran while one was open for 2% of the time, Pallas kernels for 1%

profile of v8, /device:TPU:1, one launch (start us, length us, event | category | flops | bytes accessed | tf_op | source)
XLA Modules:
  0.0 188.7 jit_solution(4360308693506373117)
XLA Ops:
  0.7 1.0 multiply_convert_fusion.3
  1.7 22.2 %all_to_all.35.own = bf16[8,128,256]{2,1,0:T(8,128)(2,1)S(1)} all-to-all(bf16[8,128,256]{2,1,0:T(8,128)(2,1)S(1)} %broadcast_in_dim.12), channel_id=1, replica_groups=mesh['y'=8,'core'=2,'z'=8,'x'=4] {'y'}, dimensions={0} | all-to-all | bytes 1048576 | tf_op jit(solution)/shard_map/all_to_all | solution.py:112
  23.9 5.6 %collective-permute-start = (bf16[8,128,256]{2,1,0:T(8,128)(2,1)S(1)}, bf16[8,128,256]{2,1,0:T(8,128)(2,1)S(1)}, u32[]{:S(2)}, u32[]{:S(2)}) collective-permute-start(bf16[8,128,256]{2,1,0:T(8,128)(2,1)S(1)} %all_to_all.35.own), channel_id=1, source_target_pairs={{0,32},{32,0},{1,33},{33,1},{2,34},{34,2},{3,35},{35,3},{4,36},{36... | collective-permute-start | bytes 1572872 | tf_op jit(solution)/shard_map/ppermute | solution.py:113
  31.0 1.5 forward_tiles.1
  32.5 29.7 %all_to_all.36 = bf16[4,8,128,256]{3,2,1,0:T(8,128)(2,1)S(1)} all-to-all(bf16[4,8,128,256]{3,2,1,0:T(8,128)(2,1)S(1)} %forward_tiles.1), channel_id=1, replica_groups=mesh['y'=8,'core'=2,'z'=8,'x'=4] {'x'}, dimensions={0} | all-to-all | bytes 4194304 | tf_op jit(solution)/shard_map/all_to_all | solution.py:124
  62.3 1.3 reduce_sum.60
  63.6 11.8 %all-to-all-start.2 = ((bf16[8,128,256]{2,1,0:T(8,128)(2,1)}), bf16[8,128,256]{2,1,0:T(8,128)(2,1)S(1)}, u32[]{:S(2)}, u32[]{:S(2)}) async-start(bf16[8,128,256]{2,1,0:T(8,128)(2,1)} %reduce_sum.60), calls=%async_computation.2 | async-start | bytes 1048576 | tf_op jit(solution)/shard_map/all_to_all | solution.py:125
  75.4 18.0 %all-to-all-done.2 = bf16[8,128,256]{2,1,0:T(8,128)(2,1)S(1)} async-done(((bf16[8,128,256]{2,1,0:T(8,128)(2,1)}), bf16[8,128,256]{2,1,0:T(8,128)(2,1)S(1)}, u32[]{:S(2)}, u32[]{:S(2)}) %all-to-all-start.2) | async-done | bytes 524320 | tf_op jit(solution)/shard_map/all_to_all | solution.py:125
  95.6 3.5 %all-to-all-start.3 = ((bf16[8,128,256]{2,1,0:T(8,128)(2,1)}), bf16[8,128,256]{2,1,0:T(8,128)(2,1)S(1)}, u32[]{:S(2)}, u32[]{:S(2)}) async-start(bf16[8,128,256]{2,1,0:T(8,128)(2,1)} %broadcast_in_dim.13), calls=%async_computation.3 | async-start | bytes 1048576 | tf_op jit(solution)/shard_map/all_to_all | solution.py:161
  99.2 2.4 %collective-permute-start.1 = (bf16[9,16,256]{2,1,0:T(8,128)(2,1)S(1)}, bf16[9,16,256]{2,1,0:T(8,128)(2,1)S(1)}, u32[]{:S(2)}, u32[]{:S(2)}) collective-permute-start(bf16[9,16,256]{2,1,0:T(8,128)(2,1)S(1)} %pad_maximum_fusion.3), channel_id=1, source_target_pairs={{0,32},{32,0},{1,33},{33,1},{2,34},{34,2},{3,35},{35,3},{4,36},{36... | collective-permute-start | bytes 221192 | tf_op jit(solution)/shard_map/ppermute | solution.py:153
  102.6 14.4 %all-to-all-done.3.g0 = bf16[8,128,256]{2,1,0:T(8,128)(2,1)S(1)} async-done(((bf16[8,128,256]{2,1,0:T(8,128)(2,1)}), bf16[8,128,256]{2,1,0:T(8,128)(2,1)S(1)}, u32[]{:S(2)}, u32[]{:S(2)}) %all-to-all-start.3) | async-done | bytes 524320 | tf_op jit(solution)/shard_map/all_to_all | solution.py:161
  117.0 2.2 %collective-permute-start.4 = (bf16[8,128,256]{2,1,0:T(8,128)(2,1)S(1)}, bf16[8,128,256]{2,1,0:T(8,128)(2,1)S(1)}, u32[]{:S(2)}, u32[]{:S(2)}) collective-permute-start(bf16[8,128,256]{2,1,0:T(8,128)(2,1)S(1)} %all-to-all-done.3.g0), channel_id=1, source_target_pairs={{0,1},{1,2},{2,3},{3,0},{4,5},{5,6},{6,7},{7,4},{8,9},{9,10},{10,1... | collective-permute-start | bytes 1572872 | tf_op jit(solution)/shard_map/ppermute | solution.py:164
  119.2 4.3 %collective-permute-start.2 = (bf16[8,128,256]{2,1,0:T(8,128)(2,1)S(1)}, bf16[8,128,256]{2,1,0:T(8,128)(2,1)S(1)}, u32[]{:S(2)}, u32[]{:S(2)}) collective-permute-start(bf16[8,128,256]{2,1,0:T(8,128)(2,1)S(1)} %all-to-all-done.3.g0), channel_id=1, source_target_pairs={{0,3},{1,0},{2,1},{3,2},{4,7},{5,4},{6,5},{7,6},{8,11},{9,8},{10,9... | collective-permute-start | bytes 1572872 | tf_op jit(solution)/shard_map/ppermute | solution.py:163
  123.5 10.1 %all_to_all.37 = bf16[8,24,256]{2,1,0:T(8,128)(2,1)S(1)} all-to-all(bf16[8,24,256]{2,1,0:T(8,128)(2,1)S(1)} %pad_maximum_fusion.2), channel_id=1, replica_groups=mesh['y'=8,'core'=2,'z'=8,'x'=4] {'y'}, dimensions={0} | all-to-all | bytes 196608 | tf_op jit(solution)/shard_map/all_to_all | solution.py:168
  134.3 4.6 %all-to-all-start.5 = ((bf16[32,24,256]{2,1,0:T(8,128)(2,1)}), bf16[32,24,256]{2,1,0:T(8,128)(2,1)}, u32[]{:S(2)}, u32[]{:S(2)}) async-start(bf16[32,24,256]{2,1,0:T(8,128)(2,1)} %broadcast_in_dim.16), calls=%async_computation.5 | async-start | bytes 786432 | tf_op jit(solution)/shard_map/all_to_all | solution.py:169
  139.0 3.0 %collective-permute-start.5 = (bf16[4,128,256]{2,1,0:T(8,128)(2,1)S(1)}, bf16[4,128,256]{2,1,0:T(8,128)(2,1)S(1)}, u32[]{:S(2)}, u32[]{:S(2)}) collective-permute-start(bf16[4,128,256]{2,1,0:T(8,128)(2,1)S(1)} %slice.56), channel_id=1, source_target_pairs={{0,1},{1,2},{2,3},{3,0},{4,5},{5,6},{6,7},{7,4},{8,9},{9,10},{10,1... | collective-permute-start | bytes 786440 | tf_op jit(solution)/shard_map/ppermute | solution.py:166
  142.0 3.5 %collective-permute-start.3 = (bf16[4,128,256]{2,1,0:T(8,128)(2,1)S(1)}, bf16[4,128,256]{2,1,0:T(8,128)(2,1)S(1)}, u32[]{:S(2)}, u32[]{:S(2)}) collective-permute-start(bf16[4,128,256]{2,1,0:T(8,128)(2,1)S(1)} %slice.55), channel_id=1, source_target_pairs={{0,3},{1,0},{2,1},{3,2},{4,7},{5,4},{6,5},{7,6},{8,11},{9,8},{10,9... | collective-permute-start | bytes 786440 | tf_op jit(solution)/shard_map/ppermute | solution.py:165
  145.5 7.0 %collective-permute-done.5.g2_high = bf16[4,128,256]{2,1,0:T(8,128)(2,1)S(1)} collective-permute-done((bf16[4,128,256]{2,1,0:T(8,128)(2,1)S(1)}, bf16[4,128,256]{2,1,0:T(8,128)(2,1)S(1)}, u32[]{:S(2)}, u32[]{:S(2)}) %collective-permute-start.5) | collective-permute-done | bytes 262176 | tf_op jit(solution)/shard_map/ppermute | solution.py:166
  152.8 2.1 %backward_tiles.1 = (f32[8,128,256]{2,1,0:T(8,128)S(1)}, bf16[8,128,256]{2,1,0:T(8,128)(2,1)}) custom-call(s32[51]{0:T(128)S(1)} %concatenate.17.info, bf16[24,128,128]{2,1,0:T(8,128)(2,1)S(1)} %bitcast.41, bf16[8,128,256]{2,1,0:T(8,128)(2,1)S(1)} %all-to-all-done.3.g0, bf16[8,128,256]{2,1,0:T(8,128)(2,1)S(1)} %collective-permute-done.2.g1, ...), custom_call_target="tpu_custom_call" | custom-call | tf_op jit(solution)/shard_map/backward_tiles/pallas_call | solution.py:174
  154.9 3.9 %collective-permute-start.6 = (bf16[8,128,256]{2,1,0:T(8,128)(2,1)}, bf16[8,128,256]{2,1,0:T(8,128)(2,1)S(1)}, u32[]{:S(2)}, u32[]{:S(2)}) collective-permute-start(bf16[8,128,256]{2,1,0:T(8,128)(2,1)} %get-tuple-element.10), channel_id=1, source_target_pairs={{0,32},{32,0},{1,33},{33,1},{2,34},{34,2},{3,35},{35,3},{4,36},{36... | collective-permute-start | bytes 1572872 | tf_op jit(solution)/shard_map/ppermute | solution.py:186
  158.9 1.1 convert_reduce_fusion.2
  161.6 3.7 %all-to-all-start.6 = ((bf16[8,144,256]{2,1,0:T(8,128)(2,1)}), bf16[8,144,256]{2,1,0:T(8,128)(2,1)S(1)}, u32[]{:S(2)}, u32[]{:S(2)}) async-start(bf16[8,144,256]{2,1,0:T(8,128)(2,1)} %pad_maximum_fusion), calls=%async_computation.6 | async-start | bytes 1179648 | tf_op jit(solution)/shard_map/all_to_all | solution.py:188
  165.8 18.8 %all-to-all-done.6 = bf16[8,144,256]{2,1,0:T(8,128)(2,1)S(1)} async-done(((bf16[8,144,256]{2,1,0:T(8,128)(2,1)}), bf16[8,144,256]{2,1,0:T(8,128)(2,1)S(1)}, u32[]{:S(2)}, u32[]{:S(2)}) %all-to-all-start.6) | async-done | bytes 589856 | tf_op jit(solution)/shard_map/all_to_all | solution.py:188
  184.6 2.4 %collective-permute-start.7 = (bf16[8,16,256]{2,1,0:T(8,128)(2,1)S(1)}, bf16[8,16,256]{2,1,0:T(8,128)(2,1)S(1)}, u32[]{:S(2)}, u32[]{:S(2)}) collective-permute-start(bf16[8,16,256]{2,1,0:T(8,128)(2,1)S(1)} %slice.59), channel_id=1, source_target_pairs={{0,32},{32,0},{1,33},{33,1},{2,34},{34,2},{3,35},{35,3},{4,36},{36... | collective-permute-start | bytes 196616 | tf_op jit(solution)/shard_map/ppermute | solution.py:191
  (56 shorter events, 9.2 us)
Async XLA Ops:
  0.6 92.8 %copy-start = (bf16[256,256]{1,0:T(8,128)(2,1)S(1)}, bf16[256,256]{1,0:T(8,128)(2,1)}, u32[]{:S(2)}) copy-start(bf16[256,256]{1,0:T(8,128)(2,1)} %param.11) | copy-start | bytes 393220
  0.6 29.5 %copy-start.3 = (s32[1,1,24,2]{2,3,1,0:T(2,128)S(1)}, s32[1,1,24,2]{2,3,1,0:T(2,128)}, u32[]{:S(2)}) copy-start(s32[1,1,24,2]{2,3,1,0:T(2,128)} %param.13) | copy-start | bytes 580
  0.7 30.4 %copy-start.1 = (bf16[1,1,24,128,128]{4,3,2,1,0:T(8,128)(2,1)S(1)}, bf16[1,1,24,128,128]{4,3,2,1,0:T(8,128)(2,1)}, u32[]{:S(2)}) copy-start(bf16[1,1,24,128,128]{4,3,2,1,0:T(8,128)(2,1)} %param.15) | copy-start | bytes 2359300
  23.9 7.1 %collective-permute-start = (bf16[8,128,256]{2,1,0:T(8,128)(2,1)S(1)}, bf16[8,128,256]{2,1,0:T(8,128)(2,1)S(1)}, u32[]{:S(2)}, u32[]{:S(2)}) collective-permute-start(bf16[8,128,256]{2,1,0:T(8,128)(2,1)S(1)} %all_to_all.35.own), channel_id=1, source_target_pairs={{0,32},{32,0},{1,33},{33,1},{2,34},{34,2},{3,35},{35,3},{4,36},{36... | collective-permute-start | bytes 1572872 | tf_op jit(solution)/shard_map/ppermute | solution.py:113
  63.6 30.0 %copy-start.4 = (f32[128]{0:T(128)S(1)}, f32[128]{0:T(128)}, u32[]{:S(2)}) copy-start(f32[128]{0:T(128)} %param.16) | copy-start | bytes 1540
  63.6 30.0 %copy-start.5 = (bf16[128,256]{1,0:T(8,128)(2,1)S(1)}, bf16[128,256]{1,0:T(8,128)(2,1)}, u32[]{:S(2)}) copy-start(bf16[128,256]{1,0:T(8,128)(2,1)} %param.17) | copy-start | bytes 196612
  63.6 30.0 %copy-start.6 = (f32[256]{0:T(256)S(1)}, f32[256]{0:T(256)}, u32[]{:S(2)}) copy-start(f32[256]{0:T(256)} %param.12) | copy-start | bytes 3076
  63.6 29.8 %all-to-all-start.2 = ((bf16[8,128,256]{2,1,0:T(8,128)(2,1)}), bf16[8,128,256]{2,1,0:T(8,128)(2,1)S(1)}, u32[]{:S(2)}, u32[]{:S(2)}) async-start(bf16[8,128,256]{2,1,0:T(8,128)(2,1)} %reduce_sum.60), calls=%async_computation.2 | async-start | bytes 1048576 | tf_op jit(solution)/shard_map/all_to_all | solution.py:125
  95.6 21.4 %all-to-all-start.3 = ((bf16[8,128,256]{2,1,0:T(8,128)(2,1)}), bf16[8,128,256]{2,1,0:T(8,128)(2,1)S(1)}, u32[]{:S(2)}, u32[]{:S(2)}) async-start(bf16[8,128,256]{2,1,0:T(8,128)(2,1)} %broadcast_in_dim.13), calls=%async_computation.3 | async-start | bytes 1048576 | tf_op jit(solution)/shard_map/all_to_all | solution.py:161
  99.2 3.3 %collective-permute-start.1 = (bf16[9,16,256]{2,1,0:T(8,128)(2,1)S(1)}, bf16[9,16,256]{2,1,0:T(8,128)(2,1)S(1)}, u32[]{:S(2)}, u32[]{:S(2)}) collective-permute-start(bf16[9,16,256]{2,1,0:T(8,128)(2,1)S(1)} %pad_maximum_fusion.3), channel_id=1, source_target_pairs={{0,32},{32,0},{1,33},{33,1},{2,34},{34,2},{3,35},{35,3},{4,36},{36... | collective-permute-start | bytes 221192 | tf_op jit(solution)/shard_map/ppermute | solution.py:153
  117.0 22.0 %collective-permute-start.4 = (bf16[8,128,256]{2,1,0:T(8,128)(2,1)S(1)}, bf16[8,128,256]{2,1,0:T(8,128)(2,1)S(1)}, u32[]{:S(2)}, u32[]{:S(2)}) collective-permute-start(bf16[8,128,256]{2,1,0:T(8,128)(2,1)S(1)} %all-to-all-done.3.g0), channel_id=1, source_target_pairs={{0,1},{1,2},{2,3},{3,0},{4,5},{5,6},{6,7},{7,4},{8,9},{9,10},{10,1... | collective-permute-start | bytes 1572872 | tf_op jit(solution)/shard_map/ppermute | solution.py:164
  119.2 22.8 %collective-permute-start.2 = (bf16[8,128,256]{2,1,0:T(8,128)(2,1)S(1)}, bf16[8,128,256]{2,1,0:T(8,128)(2,1)S(1)}, u32[]{:S(2)}, u32[]{:S(2)}) collective-permute-start(bf16[8,128,256]{2,1,0:T(8,128)(2,1)S(1)} %all-to-all-done.3.g0), channel_id=1, source_target_pairs={{0,3},{1,0},{2,1},{3,2},{4,7},{5,4},{6,5},{7,6},{8,11},{9,8},{10,9... | collective-permute-start | bytes 1572872 | tf_op jit(solution)/shard_map/ppermute | solution.py:163
  134.3 24.5 %all-to-all-start.5 = ((bf16[32,24,256]{2,1,0:T(8,128)(2,1)}), bf16[32,24,256]{2,1,0:T(8,128)(2,1)}, u32[]{:S(2)}, u32[]{:S(2)}) async-start(bf16[32,24,256]{2,1,0:T(8,128)(2,1)} %broadcast_in_dim.16), calls=%async_computation.5 | async-start | bytes 786432 | tf_op jit(solution)/shard_map/all_to_all | solution.py:169
  139.0 13.5 %collective-permute-start.5 = (bf16[4,128,256]{2,1,0:T(8,128)(2,1)S(1)}, bf16[4,128,256]{2,1,0:T(8,128)(2,1)S(1)}, u32[]{:S(2)}, u32[]{:S(2)}) collective-permute-start(bf16[4,128,256]{2,1,0:T(8,128)(2,1)S(1)} %slice.56), channel_id=1, source_target_pairs={{0,1},{1,2},{2,3},{3,0},{4,5},{5,6},{6,7},{7,4},{8,9},{9,10},{10,1... | collective-permute-start | bytes 786440 | tf_op jit(solution)/shard_map/ppermute | solution.py:166
  142.0 10.9 %collective-permute-start.3 = (bf16[4,128,256]{2,1,0:T(8,128)(2,1)S(1)}, bf16[4,128,256]{2,1,0:T(8,128)(2,1)S(1)}, u32[]{:S(2)}, u32[]{:S(2)}) collective-permute-start(bf16[4,128,256]{2,1,0:T(8,128)(2,1)S(1)} %slice.55), channel_id=1, source_target_pairs={{0,3},{1,0},{2,1},{3,2},{4,7},{5,4},{6,5},{7,6},{8,11},{9,8},{10,9... | collective-permute-start | bytes 786440 | tf_op jit(solution)/shard_map/ppermute | solution.py:165
  154.9 5.6 %collective-permute-start.6 = (bf16[8,128,256]{2,1,0:T(8,128)(2,1)}, bf16[8,128,256]{2,1,0:T(8,128)(2,1)S(1)}, u32[]{:S(2)}, u32[]{:S(2)}) collective-permute-start(bf16[8,128,256]{2,1,0:T(8,128)(2,1)} %get-tuple-element.10), channel_id=1, source_target_pairs={{0,32},{32,0},{1,33},{33,1},{2,34},{34,2},{3,35},{35,3},{4,36},{36... | collective-permute-start | bytes 1572872 | tf_op jit(solution)/shard_map/ppermute | solution.py:186
  161.6 25.5 %copy-start.2 = (f32[128]{0:T(128)S(1)}, f32[128]{0:T(128)}, u32[]{:S(2)}) copy-start(f32[128]{0:T(128)} %param.10) | copy-start | bytes 1540
  161.6 23.0 %all-to-all-start.6 = ((bf16[8,144,256]{2,1,0:T(8,128)(2,1)}), bf16[8,144,256]{2,1,0:T(8,128)(2,1)S(1)}, u32[]{:S(2)}, u32[]{:S(2)}) async-start(bf16[8,144,256]{2,1,0:T(8,128)(2,1)} %pad_maximum_fusion), calls=%async_computation.6 | async-start | bytes 1179648 | tf_op jit(solution)/shard_map/all_to_all | solution.py:188
  184.6 3.3 %collective-permute-start.7 = (bf16[8,16,256]{2,1,0:T(8,128)(2,1)S(1)}, bf16[8,16,256]{2,1,0:T(8,128)(2,1)S(1)}, u32[]{:S(2)}, u32[]{:S(2)}) collective-permute-start(bf16[8,16,256]{2,1,0:T(8,128)(2,1)S(1)} %slice.59), channel_id=1, source_target_pairs={{0,32},{32,0},{1,33},{33,1},{2,34},{34,2},{3,35},{35,3},{4,36},{36... | collective-permute-start | bytes 196616 | tf_op jit(solution)/shard_map/ppermute | solution.py:191

commit v9 on v7

--- a/solution.py
+++ b/solution.py
@@ -143,8 +143,8 @@
     chunk = hidden // tile_cols
     both = jnp.concatenate(
         [
-            (weight_part * scale).reshape(tile_cols, chunk, hidden),
-            jnp.broadcast_to(bias_part * scale, (tile_cols, 8, hidden)),
+            (weight_part * scale).reshape(n_y, n_core * chunk, hidden),
+            jnp.broadcast_to(bias_part * scale, (n_y, 8, hidden)),
         ],
         axis=1,
     ).astype(BF16)
@@ -155,7 +155,12 @@
     g2_low = lax.ppermute(g1[: n_z // 2], "x", ring(n_x, n_x - 1))
     g2_high = lax.ppermute(g3[n_z // 2 :], "x", ring(n_x, 1))
     g = [g0, g1, g2_low, g2_high, g3]
-    both = jnp.sum(lax.all_to_all(both, ROW, 0, 0, tiled=True).astype(F32), axis=0)
+    both = jnp.sum(lax.all_to_all(both, "y", 0, 0, tiled=True).astype(F32), axis=0)
+    first = lax.axis_index("core") == 0
+    one, two, bias_sum = both[:chunk], both[chunk : 2 * chunk], both[2 * chunk :]
+    mine = jnp.concatenate([jnp.where(first, one, two), bias_sum], axis=0)
+    away = jnp.concatenate([jnp.where(first, two, one), bias_sum], axis=0).astype(BF16)
+    both = mine + lax.ppermute(away, "core", swap).astype(F32)
     both = lax.all_to_all(repeat(both.astype(BF16), tile_rows), COL, 0, 0, tiled=True)
     both = jnp.sum(both.astype(F32), axis=0)
     grad_bias = both[chunk]
@@ -179,7 +184,6 @@
     column_total = jnp.sum(last[:, :n].astype(F32), axis=0)
     chunks = last[:, n:]
     chunks_other = lax.ppermute(chunks, "core", swap)
-    first = lax.axis_index("core") == 0
     grad_weight = jnp.concatenate(
         [jnp.where(first, chunks, chunks_other), jnp.where(first, chunks_other, chunks)], axis=1
     )

time: 189 us -> 186 us (0.984)
  blocking collectives: 95.8 us -> 78.1 us
  starting transfers between devices: 35 us -> 47.5 us
    all_to_all x1 -> x0, blocking collectives: 18.6 us -> none  [body(): lax.all_to_all(both, ROW, 0, 0, tiled=True).astype(F32)]
    ppermute x0 -> x1, starting transfers between devices: none -> 7.26 us  [body(): both = mine + lax.ppermute(away, 'core', swap).astype(F32)]
    all_to_all x0 -> x1, starting transfers between devices: none -> 3.38 us  [body(): lax.all_to_all(both, 'y', 0, 0, tiled=True).astype(F32)]
  transfers between devices with their start and end apart: 10 -> 12, of which waited for: 5 -> 7; matrix products, arithmetic and copies ran while one was open for 2% -> 2% of each run, Pallas kernels for 1% -> 1%
where the time goes in v9:
time: 186 us; the launch traced here: 184 us
  blocking collectives  78.1 us (42%)
  starting transfers between devices  47.5 us (26%)
  waiting for transfers between devices  43.8 us (24%)
  other arithmetic  5.13 us (3%)
  Pallas kernels  3.58 us (2%)
  local copies, waits for them, and re-layouts  2.41 us (1%)
  matrix products  2.06 us (1%)
    all_to_all x1, blocking collectives, body(): lax.all_to_all(blocks, 'x', 0, 0, tiled=True).astype(F32)  30.3 us
    all_to_all x1, blocking collectives, body(): terms = lax.all_to_all(over_x.astype(BF16), 'z', 0, 0, tiled=True)  25.6 us
    all_to_all x1, blocking collectives, body(): own = lax.all_to_all(repeat(share, n_y), 'y', 0, 0, tiled=True)  22.2 us
    all_to_all x1, waiting for transfers between devices, body(): last = lax.all_to_all(last, 'y', 0, 0, tiled=True)  18.8 us
    all_to_all x1, waiting for transfers between devices, body(): g0 = lax.all_to_all(repeat(grad_here, n_z), 'z', 0, 0, tiled=True)  13.2 us
    ppermute x1, waiting for transfers between devices, body(): g2_high = lax.ppermute(g3[n_z // 2:], 'x', ring(n_x, 1))  7.88 us
    ppermute x1, starting transfers between devices, body(): both = mine + lax.ppermute(away, 'core', swap).astype(F32)  7.26 us
    ppermute x1, starting transfers between devices, body(): other = lax.ppermute(own, 'core', swap)  5.6 us
  transfers between devices with their start and end apart: 12, of which 7 were waited for; matrix products, arithmetic and copies ran while one was open for 2% of the time, Pallas kernels for 1%

profile of v9, /device:TPU:1, one launch (start us, length us, event | category | flops | bytes accessed | tf_op | source)
XLA Modules:
  0.0 184.3 jit_solution(17785706885410208046)
XLA Ops:
  0.7 1.0 multiply_convert_fusion.3
  1.7 22.2 %all_to_all.35.own = bf16[8,128,256]{2,1,0:T(8,128)(2,1)S(1)} all-to-all(bf16[8,128,256]{2,1,0:T(8,128)(2,1)S(1)} %broadcast_in_dim.10), channel_id=1, replica_groups=mesh['y'=8,'core'=2,'z'=8,'x'=4] {'y'}, dimensions={0} | all-to-all | bytes 1048576 | tf_op jit(solution)/shard_map/all_to_all | solution.py:112
  23.9 5.6 %collective-permute-start = (bf16[8,128,256]{2,1,0:T(8,128)(2,1)S(1)}, bf16[8,128,256]{2,1,0:T(8,128)(2,1)S(1)}, u32[]{:S(2)}, u32[]{:S(2)}) collective-permute-start(bf16[8,128,256]{2,1,0:T(8,128)(2,1)S(1)} %all_to_all.35.own), channel_id=1, source_target_pairs={{0,32},{32,0},{1,33},{33,1},{2,34},{34,2},{3,35},{35,3},{4,36},{36... | collective-permute-start | bytes 1572872 | tf_op jit(solution)/shard_map/ppermute | solution.py:113
  31.0 1.5 forward_tiles.1
  32.5 30.3 %all_to_all.36 = bf16[4,8,128,256]{3,2,1,0:T(8,128)(2,1)S(1)} all-to-all(bf16[4,8,128,256]{3,2,1,0:T(8,128)(2,1)S(1)} %forward_tiles.1), channel_id=1, replica_groups=mesh['y'=8,'core'=2,'z'=8,'x'=4] {'x'}, dimensions={0} | all-to-all | bytes 4194304 | tf_op jit(solution)/shard_map/all_to_all | solution.py:124
  63.3 25.6 %all_to_all.37 = bf16[8,128,256]{2,1,0:T(8,128)(2,1)S(1)} all-to-all(bf16[8,128,256]{2,1,0:T(8,128)(2,1)S(1)} %reduce_sum.57), channel_id=1, replica_groups=mesh['y'=8,'core'=2,'z'=8,'x'=4] {'z'}, dimensions={0} | all-to-all | bytes 1048576 | tf_op jit(solution)/shard_map/all_to_all | solution.py:125
  90.9 3.5 %all-to-all-start.3 = ((bf16[8,128,256]{2,1,0:T(8,128)(2,1)}), bf16[8,128,256]{2,1,0:T(8,128)(2,1)S(1)}, u32[]{:S(2)}, u32[]{:S(2)}) async-start(bf16[8,128,256]{2,1,0:T(8,128)(2,1)} %broadcast_in_dim.11), calls=%async_computation.3 | async-start | bytes 1048576 | tf_op jit(solution)/shard_map/all_to_all | solution.py:151
  95.3 13.2 %all-to-all-done.3.g0 = bf16[8,128,256]{2,1,0:T(8,128)(2,1)S(1)} async-done(((bf16[8,128,256]{2,1,0:T(8,128)(2,1)}), bf16[8,128,256]{2,1,0:T(8,128)(2,1)S(1)}, u32[]{:S(2)}, u32[]{:S(2)}) %all-to-all-start.3) | async-done | bytes 524320 | tf_op jit(solution)/shard_map/all_to_all | solution.py:151
  108.5 3.4 %all-to-all-start.4 = ((bf16[8,40,256]{2,1,0:T(8,128)(2,1)}), bf16[8,40,256]{2,1,0:T(8,128)(2,1)S(1)}, u32[]{:S(2)}, u32[]{:S(2)}) async-start(bf16[8,40,256]{2,1,0:T(8,128)(2,1)} %pad_maximum_fusion.1), calls=%async_computation.4 | async-start | bytes 327680 | tf_op jit(solution)/shard_map/all_to_all | solution.py:158
  111.9 2.2 %collective-permute-start.3 = (bf16[8,128,256]{2,1,0:T(8,128)(2,1)S(1)}, bf16[8,128,256]{2,1,0:T(8,128)(2,1)S(1)}, u32[]{:S(2)}, u32[]{:S(2)}) collective-permute-start(bf16[8,128,256]{2,1,0:T(8,128)(2,1)S(1)} %all-to-all-done.3.g0), channel_id=1, source_target_pairs={{0,1},{1,2},{2,3},{3,0},{4,5},{5,6},{6,7},{7,4},{8,9},{9,10},{10,1... | collective-permute-start | bytes 1572872 | tf_op jit(solution)/shard_map/ppermute | solution.py:154
  114.2 4.3 %collective-permute-start.1 = (bf16[8,128,256]{2,1,0:T(8,128)(2,1)S(1)}, bf16[8,128,256]{2,1,0:T(8,128)(2,1)S(1)}, u32[]{:S(2)}, u32[]{:S(2)}) collective-permute-start(bf16[8,128,256]{2,1,0:T(8,128)(2,1)S(1)} %all-to-all-done.3.g0), channel_id=1, source_target_pairs={{0,3},{1,0},{2,1},{3,2},{4,7},{5,4},{6,5},{7,6},{8,11},{9,8},{10,9... | collective-permute-start | bytes 1572872 | tf_op jit(solution)/shard_map/ppermute | solution.py:153
  118.4 1.7 all-to-all-done.4
  120.2 7.3 %collective-permute-start.6 = (bf16[24,256]{1,0:T(8,128)(2,1)S(1)}, bf16[24,256]{1,0:T(8,128)(2,1)S(1)}, u32[]{:S(2)}, u32[]{:S(2)}) collective-permute-start(bf16[24,256]{1,0:T(8,128)(2,1)S(1)} %pad_maximum_fusion.3), channel_id=1, source_target_pairs={{0,32},{32,0},{1,33},{33,1},{2,34},{34,2},{3,35},{35,3},{4,36},{36... | collective-permute-start | bytes 36872 | tf_op jit(solution)/shard_map/ppermute | solution.py:163
  129.1 4.6 %all-to-all-start.5 = ((bf16[32,24,256]{2,1,0:T(8,128)(2,1)}), bf16[32,24,256]{2,1,0:T(8,128)(2,1)}, u32[]{:S(2)}, u32[]{:S(2)}) async-start(bf16[32,24,256]{2,1,0:T(8,128)(2,1)} %broadcast_in_dim.13), calls=%async_computation.5 | async-start | bytes 786432 | tf_op jit(solution)/shard_map/all_to_all | solution.py:164
  133.7 3.0 %collective-permute-start.4 = (bf16[4,128,256]{2,1,0:T(8,128)(2,1)S(1)}, bf16[4,128,256]{2,1,0:T(8,128)(2,1)S(1)}, u32[]{:S(2)}, u32[]{:S(2)}) collective-permute-start(bf16[4,128,256]{2,1,0:T(8,128)(2,1)S(1)} %slice.46), channel_id=1, source_target_pairs={{0,1},{1,2},{2,3},{3,0},{4,5},{5,6},{6,7},{7,4},{8,9},{9,10},{10,1... | collective-permute-start | bytes 786440 | tf_op jit(solution)/shard_map/ppermute | solution.py:156
  136.7 3.5 %collective-permute-start.2 = (bf16[4,128,256]{2,1,0:T(8,128)(2,1)S(1)}, bf16[4,128,256]{2,1,0:T(8,128)(2,1)S(1)}, u32[]{:S(2)}, u32[]{:S(2)}) collective-permute-start(bf16[4,128,256]{2,1,0:T(8,128)(2,1)S(1)} %slice.45), channel_id=1, source_target_pairs={{0,3},{1,0},{2,1},{3,2},{4,7},{5,4},{6,5},{7,6},{8,11},{9,8},{10,9... | collective-permute-start | bytes 786440 | tf_op jit(solution)/shard_map/ppermute | solution.py:155
  140.2 7.9 %collective-permute-done.4.g2_high = bf16[4,128,256]{2,1,0:T(8,128)(2,1)S(1)} collective-permute-done((bf16[4,128,256]{2,1,0:T(8,128)(2,1)S(1)}, bf16[4,128,256]{2,1,0:T(8,128)(2,1)S(1)}, u32[]{:S(2)}, u32[]{:S(2)}) %collective-permute-start.4) | collective-permute-done | bytes 262176 | tf_op jit(solution)/shard_map/ppermute | solution.py:156
  148.1 2.1 %backward_tiles.1 = (f32[8,128,256]{2,1,0:T(8,128)S(1)}, bf16[8,128,256]{2,1,0:T(8,128)(2,1)}) custom-call(s32[51]{0:T(128)S(1)} %concatenate.20.info, bf16[24,128,128]{2,1,0:T(8,128)(2,1)S(1)} %bitcast.20, bf16[8,128,256]{2,1,0:T(8,128)(2,1)S(1)} %all-to-all-done.3.g0, bf16[8,128,256]{2,1,0:T(8,128)(2,1)S(1)} %collective-permute-done.1.g1, ...), custom_call_target="tpu_custom_call" | custom-call | tf_op jit(solution)/shard_map/backward_tiles/pallas_call | solution.py:169
  150.2 3.0 %collective-permute-start.5 = (bf16[8,128,256]{2,1,0:T(8,128)(2,1)}, bf16[8,128,256]{2,1,0:T(8,128)(2,1)S(1)}, u32[]{:S(2)}, u32[]{:S(2)}) collective-permute-start(bf16[8,128,256]{2,1,0:T(8,128)(2,1)} %get-tuple-element.10), channel_id=1, source_target_pairs={{0,32},{32,0},{1,33},{33,1},{2,34},{34,2},{3,35},{35,3},{4,36},{36... | collective-permute-start | bytes 1572872 | tf_op jit(solution)/shard_map/ppermute | solution.py:181
  153.2 1.1 convert_reduce_fusion.2
  155.1 0.9 pad_maximum_fusion
  155.9 4.8 %all-to-all-start.6 = ((bf16[8,144,256]{2,1,0:T(8,128)(2,1)}), bf16[8,144,256]{2,1,0:T(8,128)(2,1)S(1)}, u32[]{:S(2)}, u32[]{:S(2)}) async-start(bf16[8,144,256]{2,1,0:T(8,128)(2,1)} %pad_maximum_fusion), calls=%async_computation.6 | async-start | bytes 1179648 | tf_op jit(solution)/shard_map/all_to_all | solution.py:183
  161.3 18.8 %all-to-all-done.6 = bf16[8,144,256]{2,1,0:T(8,128)(2,1)S(1)} async-done(((bf16[8,144,256]{2,1,0:T(8,128)(2,1)}), bf16[8,144,256]{2,1,0:T(8,128)(2,1)S(1)}, u32[]{:S(2)}, u32[]{:S(2)}) %all-to-all-start.6) | async-done | bytes 589856 | tf_op jit(solution)/shard_map/all_to_all | solution.py:183
  180.2 2.4 %collective-permute-start.7 = (bf16[8,16,256]{2,1,0:T(8,128)(2,1)S(1)}, bf16[8,16,256]{2,1,0:T(8,128)(2,1)S(1)}, u32[]{:S(2)}, u32[]{:S(2)}) collective-permute-start(bf16[8,16,256]{2,1,0:T(8,128)(2,1)S(1)} %slice.52), channel_id=1, source_target_pairs={{0,32},{32,0},{1,33},{33,1},{2,34},{34,2},{3,35},{35,3},{4,36},{36... | collective-permute-start | bytes 196616 | tf_op jit(solution)/shard_map/ppermute | solution.py:186
  (55 shorter events, 8.9 us)
Async XLA Ops:
  0.6 88.3 %copy-start = (bf16[256,256]{1,0:T(8,128)(2,1)S(1)}, bf16[256,256]{1,0:T(8,128)(2,1)}, u32[]{:S(2)}) copy-start(bf16[256,256]{1,0:T(8,128)(2,1)} %param.11) | copy-start | bytes 393220
  0.6 29.5 %copy-start.3 = (s32[1,1,24,2]{2,3,1,0:T(2,128)S(1)}, s32[1,1,24,2]{2,3,1,0:T(2,128)}, u32[]{:S(2)}) copy-start(s32[1,1,24,2]{2,3,1,0:T(2,128)} %param.13) | copy-start | bytes 580
  0.7 30.4 %copy-start.1 = (bf16[1,1,24,128,128]{4,3,2,1,0:T(8,128)(2,1)S(1)}, bf16[1,1,24,128,128]{4,3,2,1,0:T(8,128)(2,1)}, u32[]{:S(2)}) copy-start(bf16[1,1,24,128,128]{4,3,2,1,0:T(8,128)(2,1)} %param.15) | copy-start | bytes 2359300
  23.9 7.1 %collective-permute-start = (bf16[8,128,256]{2,1,0:T(8,128)(2,1)S(1)}, bf16[8,128,256]{2,1,0:T(8,128)(2,1)S(1)}, u32[]{:S(2)}, u32[]{:S(2)}) collective-permute-start(bf16[8,128,256]{2,1,0:T(8,128)(2,1)S(1)} %all_to_all.35.own), channel_id=1, source_target_pairs={{0,32},{32,0},{1,33},{33,1},{2,34},{34,2},{3,35},{35,3},{4,36},{36... | collective-permute-start | bytes 1572872 | tf_op jit(solution)/shard_map/ppermute | solution.py:113
  63.2 25.8 %copy-start.4 = (f32[128]{0:T(128)S(1)}, f32[128]{0:T(128)}, u32[]{:S(2)}) copy-start(f32[128]{0:T(128)} %param.16) | copy-start | bytes 1540
  63.2 25.8 %copy-start.5 = (bf16[128,256]{1,0:T(8,128)(2,1)S(1)}, bf16[128,256]{1,0:T(8,128)(2,1)}, u32[]{:S(2)}) copy-start(bf16[128,256]{1,0:T(8,128)(2,1)} %param.17) | copy-start | bytes 196612
  63.3 25.8 %copy-start.6 = (f32[256]{0:T(256)S(1)}, f32[256]{0:T(256)}, u32[]{:S(2)}) copy-start(f32[256]{0:T(256)} %param.12) | copy-start | bytes 3076
  90.9 17.7 %all-to-all-start.3 = ((bf16[8,128,256]{2,1,0:T(8,128)(2,1)}), bf16[8,128,256]{2,1,0:T(8,128)(2,1)S(1)}, u32[]{:S(2)}, u32[]{:S(2)}) async-start(bf16[8,128,256]{2,1,0:T(8,128)(2,1)} %broadcast_in_dim.11), calls=%async_computation.3 | async-start | bytes 1048576 | tf_op jit(solution)/shard_map/all_to_all | solution.py:151
  108.5 11.6 %all-to-all-start.4 = ((bf16[8,40,256]{2,1,0:T(8,128)(2,1)}), bf16[8,40,256]{2,1,0:T(8,128)(2,1)S(1)}, u32[]{:S(2)}, u32[]{:S(2)}) async-start(bf16[8,40,256]{2,1,0:T(8,128)(2,1)} %pad_maximum_fusion.1), calls=%async_computation.4 | async-start | bytes 327680 | tf_op jit(solution)/shard_map/all_to_all | solution.py:158
  111.9 21.7 %collective-permute-start.3 = (bf16[8,128,256]{2,1,0:T(8,128)(2,1)S(1)}, bf16[8,128,256]{2,1,0:T(8,128)(2,1)S(1)}, u32[]{:S(2)}, u32[]{:S(2)}) collective-permute-start(bf16[8,128,256]{2,1,0:T(8,128)(2,1)S(1)} %all-to-all-done.3.g0), channel_id=1, source_target_pairs={{0,1},{1,2},{2,3},{3,0},{4,5},{5,6},{6,7},{7,4},{8,9},{9,10},{10,1... | collective-permute-start | bytes 1572872 | tf_op jit(solution)/shard_map/ppermute | solution.py:154
  114.2 22.5 %collective-permute-start.1 = (bf16[8,128,256]{2,1,0:T(8,128)(2,1)S(1)}, bf16[8,128,256]{2,1,0:T(8,128)(2,1)S(1)}, u32[]{:S(2)}, u32[]{:S(2)}) collective-permute-start(bf16[8,128,256]{2,1,0:T(8,128)(2,1)S(1)} %all-to-all-done.3.g0), channel_id=1, source_target_pairs={{0,3},{1,0},{2,1},{3,2},{4,7},{5,4},{6,5},{7,6},{8,11},{9,8},{10,9... | collective-permute-start | bytes 1572872 | tf_op jit(solution)/shard_map/ppermute | solution.py:153
  120.2 8.1 %collective-permute-start.6 = (bf16[24,256]{1,0:T(8,128)(2,1)S(1)}, bf16[24,256]{1,0:T(8,128)(2,1)S(1)}, u32[]{:S(2)}, u32[]{:S(2)}) collective-permute-start(bf16[24,256]{1,0:T(8,128)(2,1)S(1)} %pad_maximum_fusion.3), channel_id=1, source_target_pairs={{0,32},{32,0},{1,33},{33,1},{2,34},{34,2},{3,35},{35,3},{4,36},{36... | collective-permute-start | bytes 36872 | tf_op jit(solution)/shard_map/ppermute | solution.py:163
  129.1 24.1 %all-to-all-start.5 = ((bf16[32,24,256]{2,1,0:T(8,128)(2,1)}), bf16[32,24,256]{2,1,0:T(8,128)(2,1)}, u32[]{:S(2)}, u32[]{:S(2)}) async-start(bf16[32,24,256]{2,1,0:T(8,128)(2,1)} %broadcast_in_dim.13), calls=%async_computation.5 | async-start | bytes 786432 | tf_op jit(solution)/shard_map/all_to_all | solution.py:164
  133.7 14.4 %collective-permute-start.4 = (bf16[4,128,256]{2,1,0:T(8,128)(2,1)S(1)}, bf16[4,128,256]{2,1,0:T(8,128)(2,1)S(1)}, u32[]{:S(2)}, u32[]{:S(2)}) collective-permute-start(bf16[4,128,256]{2,1,0:T(8,128)(2,1)S(1)} %slice.46), channel_id=1, source_target_pairs={{0,1},{1,2},{2,3},{3,0},{4,5},{5,6},{6,7},{7,4},{8,9},{9,10},{10,1... | collective-permute-start | bytes 786440 | tf_op jit(solution)/shard_map/ppermute | solution.py:156
  136.7 11.4 %collective-permute-start.2 = (bf16[4,128,256]{2,1,0:T(8,128)(2,1)S(1)}, bf16[4,128,256]{2,1,0:T(8,128)(2,1)S(1)}, u32[]{:S(2)}, u32[]{:S(2)}) collective-permute-start(bf16[4,128,256]{2,1,0:T(8,128)(2,1)S(1)} %slice.45), channel_id=1, source_target_pairs={{0,3},{1,0},{2,1},{3,2},{4,7},{5,4},{6,5},{7,6},{8,11},{9,8},{10,9... | collective-permute-start | bytes 786440 | tf_op jit(solution)/shard_map/ppermute | solution.py:155
  150.2 4.7 %collective-permute-start.5 = (bf16[8,128,256]{2,1,0:T(8,128)(2,1)}, bf16[8,128,256]{2,1,0:T(8,128)(2,1)S(1)}, u32[]{:S(2)}, u32[]{:S(2)}) collective-permute-start(bf16[8,128,256]{2,1,0:T(8,128)(2,1)} %get-tuple-element.10), channel_id=1, source_target_pairs={{0,32},{32,0},{1,33},{33,1},{2,34},{34,2},{3,35},{35,3},{4,36},{36... | collective-permute-start | bytes 1572872 | tf_op jit(solution)/shard_map/ppermute | solution.py:181
  155.9 26.7 %copy-start.2 = (f32[128]{0:T(128)S(1)}, f32[128]{0:T(128)}, u32[]{:S(2)}) copy-start(f32[128]{0:T(128)} %param.10) | copy-start | bytes 1540
  155.9 24.2 %all-to-all-start.6 = ((bf16[8,144,256]{2,1,0:T(8,128)(2,1)}), bf16[8,144,256]{2,1,0:T(8,128)(2,1)S(1)}, u32[]{:S(2)}, u32[]{:S(2)}) async-start(bf16[8,144,256]{2,1,0:T(8,128)(2,1)} %pad_maximum_fusion), calls=%async_computation.6 | async-start | bytes 1179648 | tf_op jit(solution)/shard_map/all_to_all | solution.py:183
  180.2 3.3 %collective-permute-start.7 = (bf16[8,16,256]{2,1,0:T(8,128)(2,1)S(1)}, bf16[8,16,256]{2,1,0:T(8,128)(2,1)S(1)}, u32[]{:S(2)}, u32[]{:S(2)}) collective-permute-start(bf16[8,16,256]{2,1,0:T(8,128)(2,1)S(1)} %slice.52), channel_id=1, source_target_pairs={{0,32},{32,0},{1,33},{33,1},{2,34},{34,2},{3,35},{35,3},{4,36},{36... | collective-permute-start | bytes 196616 | tf_op jit(solution)/shard_map/ppermute | solution.py:186
